TPU v7x, 32 devices: a whole 2x2x4 slice. The times are simulated.
32 devices in a mesh: dp: 2 (over core), seq: 16 (over z, y, x).
Axes of the slice: x: 2, y: 2, z: 4, core: 2. Of those that a mesh axis runs over, the one named last changes fastest.
Arguments:
- block_input: bfloat16 [16, 2048, 1536], P('dp', 'seq'), may hold values from -6 to 6
- skip_input: bfloat16 [16, 4096, 1536], P('dp', 'seq'), may hold values from -6 to 6
- species: int32 [16], P('dp'), may hold values from 0 to 1
- cotangent: bfloat16 [16, 4096, 1536], P('dp', 'seq'), may hold values from -6 to 6
- params: float32 [18110976], P(('dp', 'seq')), may hold values from -2 to 2, as said below
- first_moment: float32 [18110976], P(('dp', 'seq')), may hold values from -768 to 768
- second_moment: float32 [18110976], P(('dp', 'seq')), may hold values from 65536 to 262144
Outputs:
- block_out: bfloat16 [16, 4096, 1536], P('dp', 'seq')
- input_grad: float32 [16, 2048, 1536], P('dp', 'seq')
- skip_grad: float32 [16, 4096, 1536], P('dp', 'seq')
- new_params: float32 [18110976], P(('dp', 'seq'))
- new_first: float32 [18110976], P(('dp', 'seq'))
- new_second: float32 [18110976], P(('dp', 'seq'))
- params_copy: bfloat16 [18110976], P(('dp', 'seq'))
Inputs may be any that keep to these rules, and one draw needn't show every extreme that they name: `params`: entries of the weight matrices have spreads about the inverse root of their fan-in; gains lie near 1. `species`: 0 marks a human window, 1 a mouse window.
All inputs are finite; a program needn't handle non-finite values.
Results may differ from a plain program's by a relative error of at most 0.0096.
Values may be sent and summed in bfloat16 or wider, within the bound.
No kernel may reach another device: no remote copies, remote signals or barrier semaphores. Data moves between devices by JAX's collectives and lax.ppermute only.
A program may use at most 640 MiB of HBM per device.

v0:
```python
import functools
import math

import jax
import jax.numpy as jnp
from jax import lax
from jax.experimental import pallas as pl
from jax.experimental.pallas import tpu as pltpu
from jax.sharding import PartitionSpec as P

D = 1536
H = 8
KD = 64
VD = 192
FF = 3072
F = 192
STEP = 10
BLOCK = 256
ROWS = 11776
QKV_ROWS = 2560
TAIL = 24576
MARGIN = 320


eps_norm = 1e-05
beta_one = 0.5
beta_two = 0.5
adam_eps = 1e-08
decay_rate = 0.01
highest = lax.Precision.HIGHEST


def padded_2(array, sides, width):
    for axis, dim in sides:
        devices, length = (lax.axis_size(axis), array.shape[dim])
        up = [(i, (i + 1) % devices) for i in range(devices - 1)]
        down = [(j, i) for i, j in up]
        last = lax.slice_in_dim(array, length - width, length, axis=dim)
        initial = lax.slice_in_dim(array, 0, width, axis=dim)
        before = lax.ppermute(last, axis, up)
        after = lax.ppermute(initial, axis, down)
        array = jnp.concatenate([before, array, after], axis=dim)
    return array


def segment_ends():
    counts = [
        D * H * KD,
        D * H * KD,
        D * H * VD,
        H * VD * D,
        D * FF,
        FF * D,
        D * D,
        F * H,
        FF,
        12 * D,
    ]
    limits = []
    running = 0
    for amount in counts:
        running = running + amount
        limits.append(running)
    return limits


def rate_at(position):
    limits = segment_ends()
    step_rates = [
        2.0 / math.sqrt(D),
        2.0 / math.sqrt(D),
        2.0 / math.sqrt(D),
        8.0 / math.sqrt(H * VD),
        2.0 / math.sqrt(D),
        2.0 / math.sqrt(FF),
        2.0 / math.sqrt(D),
        3.0 / math.sqrt(F),
        0.4,
        0.4,
    ]
    result = jnp.full(position.shape, step_rates[-1], jnp.float32)
    for segment in range(len(limits) - 2, -1, -1):
        result = jnp.where(position < limits[segment], step_rates[segment], result)
    return result


def adam_update(param_old, first_old, second_old, gradient, position):
    step_rate = rate_at(position)
    first_new = beta_one * first_old + (1.0 - beta_one) * gradient
    second_new = beta_two * second_old + (1.0 - beta_two) * gradient * gradient
    first_hat = first_new / (1.0 - beta_one**STEP)
    second_hat = second_new / (1.0 - beta_two**STEP)
    param_new = param_old - step_rate * (
        first_hat / (jnp.sqrt(second_hat) + adam_eps) + decay_rate * param_old
    )
    return (param_new, first_new, second_new)


def position_basis(length):
    offsets = jnp.arange(2 * length - 1).astype(jnp.float32) - (length - 1)
    halves = F // 2
    ladder = jnp.arange(halves).astype(jnp.float32) / max(halves - 1, 1)
    lifetimes = jnp.exp(ladder * math.log(length))
    decays = jnp.exp(-jnp.abs(offsets)[:, None] * (math.log(2.0) / lifetimes)[None, :])
    return jnp.concatenate([decays, jnp.sign(offsets)[:, None] * decays], axis=1)


def layer_stats(inputs, norm_gain, norm_bias):
    centered = inputs - jnp.mean(inputs, axis=-1, keepdims=True)
    inverse = lax.rsqrt(jnp.mean(centered * centered, axis=-1, keepdims=True) + eps_norm)
    normed = centered * inverse
    return (normed * norm_gain + norm_bias, normed, inverse)


def norm_back(upstream, normed, inverse, norm_gain):
    scaled = upstream * norm_gain
    return inverse * (
        scaled
        - jnp.mean(scaled, axis=-1, keepdims=True)
        - normed * jnp.mean(scaled * normed, axis=-1, keepdims=True)
    )


def gelu_slope(before):
    return 0.5 * (1.0 + lax.erf(before * (1.0 / math.sqrt(2.0)))) + before * jnp.exp(
        -0.5 * before * before
    ) * (1.0 / math.sqrt(2.0 * math.pi))


def spread_rows(first_row, bands):
    start = pltpu.roll(first_row, 0, 1, stride=1, stride_axis=0)
    bands[0:8, :] = start
    height = 8
    while height < BLOCK:
        bands[height : 2 * height, :] = pltpu.roll(bands[0:height, :], height, 1)
        height *= 2


def collect_rows(bands, width):
    height = BLOCK // 2
    while height >= 8:
        bands[0:height, :] = bands[0:height, :] + pltpu.roll(
            bands[height : 2 * height, :], width - height, 1
        )
        height //= 2
    total = bands[0:1, :]
    for row in range(1, 8):
        total = total + pltpu.roll(bands[row : row + 1, :], width - row, 1)
    return total


def forward_kernel(table_ref, q_ref, k_ref, v_ref, out_ref, lse_ref, bands, scores, *, blocks):
    block = pl.program_id(0)

    @pl.when(block == 0)
    def _():
        spread_rows(table_ref[...], bands)

    queries = q_ref[...]
    top = jnp.full((1, BLOCK), -jnp.inf, jnp.float32)
    for j in range(blocks):
        at = pl.multiple_of((block - j + blocks - 1) * BLOCK, BLOCK)
        part = (
            jnp.dot(
                k_ref[j * BLOCK : (j + 1) * BLOCK, :], queries, preferred_element_type=jnp.float32
            )
            + bands[:, pl.ds(at, BLOCK)]
        )
        scores[j * BLOCK : (j + 1) * BLOCK, :] = part
        top = jnp.maximum(top, jnp.max(part, axis=0, keepdims=True))
    total = jnp.zeros((1, BLOCK), jnp.float32)
    result = jnp.zeros((VD, BLOCK), jnp.float32)
    for j in range(blocks):
        grown = jnp.exp(scores[j * BLOCK : (j + 1) * BLOCK, :] - top)
        total = total + jnp.sum(grown, axis=0, keepdims=True)
        result = result + jnp.dot(
            v_ref[:, j * BLOCK : (j + 1) * BLOCK],
            grown.astype(jnp.bfloat16),
            preferred_element_type=jnp.float32,
        )
    result = (result * (1.0 / total)).astype(jnp.bfloat16)
    for part in range(BLOCK // 128):
        out_ref[part] = result[:, part * 128 : (part + 1) * 128]
    lse_ref[...] = top + jnp.log(total)


def attention_forward(table, queries, key_rows, values):
    length = key_rows.shape[0]
    blocks = length // BLOCK
    parts = BLOCK // 128
    return pl.pallas_call(
        functools.partial(forward_kernel, blocks=blocks),
        grid=(blocks,),
        in_specs=[
            pl.BlockSpec((8, 2 * length), lambda i: (0, 0)),
            pl.BlockSpec((KD, BLOCK), lambda i: (0, i)),
            pl.BlockSpec((length, KD), lambda i: (0, 0)),
            pl.BlockSpec((VD, length), lambda i: (0, 0)),
        ],
        out_specs=[
            pl.BlockSpec((parts, VD, 128), lambda i: (i, 0, 0)),
            pl.BlockSpec((1, BLOCK), lambda i: (0, i)),
        ],
        out_shape=[
            jax.ShapeDtypeStruct((length // 128, VD, 128), jnp.bfloat16),
            jax.ShapeDtypeStruct((1, length), jnp.float32),
        ],
        scratch_shapes=[
            pltpu.VMEM((BLOCK, 2 * length), jnp.float32),
            pltpu.VMEM((length, BLOCK), jnp.float32),
        ],
        compiler_params=pltpu.CompilerParams(vmem_limit_bytes=40 * 2**20),
        cost_estimate=pl.CostEstimate(
            flops=4 * length * length * 256,
            bytes_accessed=8 * length * (KD + VD),
            transcendentals=length * length,
        ),
    )(table, queries, key_rows, values)


def backward_kernel(
    table_ref,
    q_ref,
    k_ref,
    kt_ref,
    v_ref,
    out_ref,
    grad_ref,
    lse_ref,
    dq_ref,
    dk_ref,
    dv_ref,
    dt_ref,
    bands,
    grad_bands,
    dk_sum,
    dv_sum,
    *,
    blocks,
):
    block = pl.program_id(0)

    @pl.when(block == 0)
    def _():
        spread_rows(table_ref[...], bands)
        grad_bands[...] = jnp.zeros_like(grad_bands)
        dk_sum[...] = jnp.zeros_like(dk_sum)
        dv_sum[...] = jnp.zeros_like(dv_sum)

    parts = BLOCK // 128
    grad_t = jnp.concatenate([grad_ref[part] for part in range(parts)], axis=1)
    out_t = jnp.concatenate([out_ref[part] for part in range(parts)], axis=1)
    delta = jnp.sum(
        grad_t.astype(jnp.float32) * out_t.astype(jnp.float32), axis=0, keepdims=True
    )
    grad_rows = grad_t.T
    queries = q_ref[...]
    query_rows = queries.T
    lse = lse_ref[...]
    dq = jnp.zeros((KD, BLOCK), jnp.float32)
    for j in range(blocks):
        span = slice(j * BLOCK, (j + 1) * BLOCK)
        at = pl.multiple_of((block - j + blocks - 1) * BLOCK, BLOCK)
        part = (
            jnp.dot(k_ref[span, :], queries, preferred_element_type=jnp.float32)
            + bands[:, pl.ds(at, BLOCK)]
        )
        soft = jnp.exp(part - lse)
        grad_soft = jnp.dot(v_ref[span, :], grad_t, preferred_element_type=jnp.float32)
        grad_scores = soft * (grad_soft - delta)
        grad_bands[:, pl.ds(at, BLOCK)] = grad_bands[:, pl.ds(at, BLOCK)] + grad_scores
        low = grad_scores.astype(jnp.bfloat16)
        dv_sum[span, :] = dv_sum[span, :] + jnp.dot(
            soft.astype(jnp.bfloat16), grad_rows, preferred_element_type=jnp.float32
        )
        dk_sum[span, :] = dk_sum[span, :] + jnp.dot(
            low, query_rows, preferred_element_type=jnp.float32
        )
        dq = dq + jnp.dot(kt_ref[:, span], low, preferred_element_type=jnp.float32)
    dq_ref[...] = (dq * (1.0 / math.sqrt(KD))).astype(jnp.bfloat16)

    @pl.when(block == blocks - 1)
    def _():
        dk_ref[...] = dk_sum[...].astype(jnp.bfloat16)
        dv_ref[...] = dv_sum[...].astype(jnp.bfloat16)
        dt_ref[...] = collect_rows(grad_bands, grad_bands.shape[1])


def attention_backward(table, queries, key_rows, keys, value_rows, heads, grad_heads, lse):
    length = key_rows.shape[0]
    blocks = length // BLOCK
    parts = BLOCK // 128
    return pl.pallas_call(
        functools.partial(backward_kernel, blocks=blocks),
        grid=(blocks,),
        in_specs=[
            pl.BlockSpec((8, 2 * length), lambda i: (0, 0)),
            pl.BlockSpec((KD, BLOCK), lambda i: (0, i)),
            pl.BlockSpec((length, KD), lambda i: (0, 0)),
            pl.BlockSpec((KD, length), lambda i: (0, 0)),
            pl.BlockSpec((length, VD), lambda i: (0, 0)),
            pl.BlockSpec((parts, VD, 128), lambda i: (i, 0, 0)),
            pl.BlockSpec((parts, VD, 128), lambda i: (i, 0, 0)),
            pl.BlockSpec((1, BLOCK), lambda i: (0, i)),
        ],
        out_specs=[
            pl.BlockSpec((KD, BLOCK), lambda i: (0, i)),
            pl.BlockSpec((length, KD), lambda i: (0, 0)),
            pl.BlockSpec((length, VD), lambda i: (0, 0)),
            pl.BlockSpec((1, 2 * length), lambda i: (0, 0)),
        ],
        out_shape=[
            jax.ShapeDtypeStruct((KD, length), jnp.bfloat16),
            jax.ShapeDtypeStruct((length, KD), jnp.bfloat16),
            jax.ShapeDtypeStruct((length, VD), jnp.bfloat16),
            jax.ShapeDtypeStruct((1, 2 * length), jnp.float32),
        ],
        scratch_shapes=[
            pltpu.VMEM((BLOCK, 2 * length), jnp.float32),
            pltpu.VMEM((BLOCK, 2 * length), jnp.float32),
            pltpu.VMEM((length, KD), jnp.float32),
            pltpu.VMEM((length, VD), jnp.float32),
        ],
        compiler_params=pltpu.CompilerParams(vmem_limit_bytes=48 * 2**20),
        cost_estimate=pl.CostEstimate(
            flops=10 * length * length * 256,
            bytes_accessed=16 * length * (KD + VD),
            transcendentals=length * length,
        ),
    )(table, queries, key_rows, keys, value_rows, heads, grad_heads, lse)


def ordered(own, other, is_first, axis):
    return jnp.concatenate(
        [jnp.where(is_first, own, other), jnp.where(is_first, other, own)], axis=axis
    )


class Places:
    def __init__(self, windows, local_rows):
        self.dp = lax.axis_size("dp")
        self.seq = lax.axis_size("seq")
        self.windows = windows
        self.rows = local_rows
        self.length = local_rows * self.seq
        self.group = self.seq // (2 * windows)
        self.heads = H // (2 * self.group)
        self.core = lax.axis_index("dp") % 2
        self.is_first = self.core == 0
        self.place = lax.axis_index("seq") % self.group
        self.part = self.rows // (2 * self.group)
        self.head_start = (self.core * self.group + self.place) * self.heads

    def swap(self, array):
        return lax.ppermute(array, "dp", [(i, i ^ 1) for i in range(self.dp)])

    def rows_to_windows(self, own):
        kept, sent = own
        return ordered(kept, self.swap(sent), self.is_first, 0)

    def halves(self, array, axis):
        size = array.shape[axis] // 2
        kept = lax.dynamic_slice_in_dim(array, self.core * size, size, axis)
        sent = lax.dynamic_slice_in_dim(array, (1 - self.core) * size, size, axis)
        return (kept, sent)

    def exchange(self, array):
        return lax.all_to_all(array, "seq", split_axis=0, concat_axis=0, tiled=True)

    def inputs_to_windows(self, inputs):
        features = inputs.shape[2]
        both = self.rows_to_windows(self.halves(inputs, 1))
        return self.exchange(both.reshape(self.seq, self.part, features))

    def gather_rows(self, array):
        features = array.shape[2]
        array = array[:, None]
        if self.group > 1:
            hops = [
                (i, i - i % self.group + (i + 1) % self.group) for i in range(self.seq)
            ]
            pieces = [array]
            for _ in range(self.group - 1):
                pieces.append(lax.ppermute(pieces[-1], "seq", hops))
            pieces = jnp.concatenate(pieces, axis=1)
            order = (self.place - jnp.arange(self.group)) % self.group
            array = jnp.take(pieces, order, axis=1)
        array = ordered(
            array[:, None], self.swap(array)[:, None], self.is_first, 1
        )
        return array.reshape(self.length, features)

    def sum_rows(self, partial):
        features = partial.shape[1]
        partial = partial.reshape(self.seq, 2, self.group * self.part, features)
        kept, sent = self.halves(partial, 1)
        total = kept[:, 0].astype(jnp.float32) + self.swap(
            sent[:, 0].astype(jnp.bfloat16)
        ).astype(jnp.float32)
        if self.group > 1:
            total = lax.psum_scatter(
                total.reshape(self.seq, self.group, self.part, features),
                "seq",
                scatter_dimension=1,
                axis_index_groups=[
                    list(range(i, i + self.group)) for i in range(0, self.seq, self.group)
                ],
                tiled=True,
            )
            total = total[:, 0]
        return total.astype(jnp.bfloat16)

    def sums_to_rows(self, array):
        features = array.shape[2]
        back = self.exchange(array).reshape(2 * self.windows, self.group * self.part, features)
        kept, sent = self.halves(back, 0)
        return ordered(kept, self.swap(sent), self.is_first, 1)

    def heads_to_rows(self, chunk):
        count = chunk.shape[1]
        back = self.exchange(chunk).reshape(
            2 * self.windows, 1, self.group, count, VD, self.rows
        )
        kept, sent = self.halves(back, 0)
        return ordered(kept, self.swap(sent), self.is_first, 1)

    def rows_to_heads(self, chunk):
        count = chunk.shape[3]
        kept, sent = self.halves(chunk, 1)
        both = self.rows_to_windows((kept[:, 0], sent[:, 0]))
        return self.exchange(both.reshape(self.seq, count, VD, self.rows))

    def to_lanes(self, array):
        if self.rows == 128:
            return array
        together = 128 // self.rows
        array = array.reshape(self.seq // together, together, VD, self.rows)
        return jnp.swapaxes(array, 1, 2).reshape(self.seq // together, VD, 128)

    def from_lanes(self, array):
        if self.rows == 128:
            return array
        together = 128 // self.rows
        array = array.reshape(self.seq // together, VD, together, self.rows)
        return jnp.swapaxes(array, 1, 2).reshape(self.seq, VD, self.rows)


def gather_weights(params):
    devices = lax.axis_size(("dp", "seq"))
    index = lax.axis_index(("dp", "seq"))
    dp, seq = lax.axis_size("dp"), lax.axis_size("seq")
    shard = params.shape[0]
    own_rows = ROWS // devices
    extra = shard - own_rows * D
    rest = extra * devices
    tail = params[shard - TAIL :].astype(jnp.bfloat16)
    before = lax.ppermute(tail, ("dp", "seq"), [(i, i + 1) for i in range(devices - 1)])
    joined = jnp.concatenate([before.astype(jnp.float32), params])
    piece = lax.dynamic_slice_in_dim(joined, TAIL - extra * index, own_rows * D)
    piece = piece.astype(jnp.bfloat16).reshape(own_rows, D)
    tail = tail.reshape(TAIL // D, D)
    owners = -(-QKV_ROWS // own_rows)
    if dp == 2 and 2 * owners <= seq and own_rows == 368:
        other = lax.ppermute(
            piece[176:368], ("dp", "seq"), [(i, i + seq) for i in range(owners)]
        )
        half = jnp.where(lax.axis_index("dp") == 0, piece[:192], other)
        hop = seq // 2
        far = lax.ppermute(half[96:], "seq", [(i, i + hop) for i in range(owners)])
        quarter = jnp.where(lax.axis_index("seq") < hop, half[:96], far)
        spread = lax.all_gather(
            jnp.concatenate([quarter, tail]), ("dp", "seq"), axis=0, tiled=True
        ).reshape(2, 2, hop, 112, D)
        special = spread[1, 1, hop - 1, 96:]
        spread = spread[:, :, :owners, :96]
        early = jnp.concatenate(
            [spread[0, 0], spread[0, 1], spread[1, 0, :, 16:], spread[1, 1]], axis=1
        ).reshape(owners * own_rows, D)
        everything = lax.all_gather(piece, ("dp", "seq"), axis=0, tiled=True)
    else:
        everything = lax.all_gather(
            jnp.concatenate([piece, tail]), ("dp", "seq"), axis=0
        )
        special = everything[-1, own_rows:]
        everything = everything[:, :own_rows].reshape(ROWS, D)
        early = everything
    special = special.astype(jnp.float32).reshape(-1)[TAIL - rest :]
    return (early, everything, special)


def sum_everywhere(array):
    for axis in ("dp", "seq"):
        devices, step = (lax.axis_size(axis), 1)
        while step < devices:
            array = array + lax.ppermute(array, axis, [(i, i ^ step) for i in range(devices)])
            step *= 2
    return array


def scatter_sums(rows):
    return lax.psum_scatter(rows, ("dp", "seq"), scatter_dimension=0, tiled=True)


def to_owners(buffer, piece, first):
    devices = lax.axis_size(("dp", "seq"))
    index = lax.axis_index(("dp", "seq"))
    own_rows = ROWS // devices
    count = piece.shape[0]
    rounds = {}
    for i in range(devices):
        low, high = (own_rows * i, own_rows * (i + 1) + TAIL // D)
        nearest = (low - first) // count
        for t in range(max(nearest, 0), devices):
            if first + count * t < high and first + count * (t + 1) > low:
                rounds.setdefault(t - nearest, []).append((t, i))
    for pairs in rounds.values():
        moved = lax.ppermute(piece, ("dp", "seq"), pairs)
        places = [0] * devices
        for source, i in pairs:
            places[i] = MARGIN + first + count * source - own_rows * i
        place = jnp.array(places, jnp.int32)[index]
        buffer = lax.dynamic_update_slice_in_dim(buffer, moved, place, 0)
    return buffer


def own_entries(buffer, special):
    devices = lax.axis_size(("dp", "seq"))
    index = lax.axis_index(("dp", "seq"))
    own_rows = ROWS // devices
    rest = special.shape[0]
    extra = rest // devices
    held = buffer[MARGIN : MARGIN + own_rows + TAIL // D].astype(jnp.float32)
    after = held[own_rows:].reshape(-1)
    after = jnp.where(index == devices - 1, jnp.pad(special, (0, TAIL - rest)), after)
    joined = jnp.concatenate([held[:own_rows].reshape(-1), after])
    return lax.dynamic_slice_in_dim(joined, extra * index, own_rows * D + extra)


def body(block_input, skip_input, species, cotangent, params, first_moment, second_moment):
    windows, local_rows, _ = block_input.shape
    at = Places(windows, local_rows)
    length = at.length
    own = at.heads
    scale = 1.0 / math.sqrt(KD)
    f32, bf16 = jnp.float32, jnp.bfloat16

    moved = at.inputs_to_windows(block_input)
    early, everything, special = gather_weights(params)
    pos_low = special[: F * H].reshape(F, H)
    up_bias = special[F * H : F * H + FF]
    vectors = special[F * H + FF :].reshape(12, D)

    def columns(matrix, width):
        return lax.dynamic_slice_in_dim(matrix, at.head_start * width, own * width, 1)

    w_query = columns(early[:512].reshape(D, H * KD), KD)
    w_key = columns(early[512:1024].reshape(D, H * KD), KD)
    w_value = columns(early[1024:2560].reshape(D, H * VD), VD)
    w_out = everything[2560:4096]
    w_up = everything[4096:7168].reshape(D, FF)
    w_down = everything[7168:10240]
    w_point = everything[10240:11776]

    pos_basis = position_basis(length)
    own_pos = lax.dynamic_slice_in_dim(pos_low, at.head_start, own, 1)
    tables = jnp.dot(own_pos.T, pos_basis.T, precision=highest)
    tables = jnp.roll(jnp.pad(tables, ((0, 0), (0, 1))), 1 - BLOCK, axis=1)
    tables = jnp.broadcast_to(tables[:, None, :], (own, 8, 2 * length))

    low_part, _, _ = layer_stats(moved.astype(f32), vectors[0], vectors[1])
    low_all = at.gather_rows(low_part.astype(bf16))
    queries = (
        jnp.einsum("rd,dk->kr", low_all, w_query, preferred_element_type=f32) * scale
    ).astype(bf16)
    keys = jnp.einsum("rd,dk->kr", low_all, w_key, preferred_element_type=f32).astype(bf16)
    values = jnp.einsum("rd,dk->kr", low_all, w_value, preferred_element_type=f32).astype(bf16)
    queries = queries.reshape(own, KD, length)
    keys = keys.reshape(own, KD, length)
    values = values.reshape(own, VD, length)
    key_rows = jnp.swapaxes(keys, 1, 2)
    value_rows = jnp.swapaxes(values, 1, 2)

    heads_out, lse, chunks = ([], [], [])
    for head in range(own):
        result, log_total = attention_forward(
            tables[head], queries[head], key_rows[head], values[head]
        )
        heads_out.append(result)
        lse.append(log_total)
        chunks.append(at.heads_to_rows(at.from_lanes(result)[:, None]))
    heads = jnp.concatenate(chunks, axis=3).reshape(windows, H * VD, local_rows)

    inputs = block_input.astype(f32)
    _, stats_one, inverse_one = layer_stats(inputs, vectors[0], vectors[1])
    attention = jnp.einsum("wcr,cd->wrd", heads, w_out, preferred_element_type=f32) + vectors[4]
    hidden_one = inputs + attention
    normed_two, stats_two, inverse_two = layer_stats(hidden_one, vectors[2], vectors[3])
    low_two = normed_two.astype(bf16)
    before = jnp.einsum("wrd,df->wrf", low_two, w_up, preferred_element_type=f32) + up_bias
    activated = jax.nn.gelu(before, approximate=False).astype(bf16)
    hidden_two = hidden_one + (
        jnp.einsum("wrf,fd->wrd", activated, w_down, preferred_element_type=f32) + vectors[5]
    )
    summed = jnp.repeat(hidden_two, 2, axis=1) + skip_input.astype(f32)
    padded = padded_2(summed.astype(bf16), (("seq", 1),), 1)
    convolved = (
        vectors[7] * padded[:, :-2] + vectors[8] * padded[:, 1:-1] + vectors[9] * padded[:, 2:]
    )
    conv_low = convolved.astype(bf16)
    pointed = jnp.einsum("wrd,de->wre", conv_low, w_point, preferred_element_type=f32) + vectors[6]
    is_mouse = (species == 1).astype(f32)[:, None]
    species_gain = (1.0 - is_mouse) * vectors[10] + is_mouse * vectors[11]
    block_out = (summed + species_gain[:, None, :] * pointed).astype(bf16)

    upstream = cotangent.astype(f32)
    grad_point = (species_gain[:, None, :] * upstream).astype(bf16)
    gain_rows = jnp.sum(upstream * pointed, axis=1)
    grad_human = jnp.sum((1.0 - is_mouse) * gain_rows, axis=0)
    grad_mouse = jnp.sum(is_mouse * gain_rows, axis=0)
    grad_w_point = jnp.einsum("wrd,wre->de", conv_low, grad_point, preferred_element_type=f32)
    grad_point_bias = jnp.sum(grad_point.astype(f32), axis=(0, 1))
    grad_conv = jnp.einsum("wre,de->wrd", grad_point, w_point, preferred_element_type=f32)
    grad_conv = grad_conv.astype(bf16)
    grad_padded = padded_2(grad_conv, (("seq", 1),), 1)
    skip_grad = (
        upstream
        + vectors[7] * grad_padded[:, 2:]
        + vectors[8] * grad_padded[:, 1:-1]
        + vectors[9] * grad_padded[:, :-2]
    )
    grad_conv_wide = grad_conv.astype(f32)
    grad_tap_zero = jnp.sum(grad_conv_wide * padded[:, :-2], axis=(0, 1))
    grad_tap_one = jnp.sum(grad_conv_wide * padded[:, 1:-1], axis=(0, 1))
    grad_tap_two = jnp.sum(grad_conv_wide * padded[:, 2:], axis=(0, 1))
    grad_hidden = jnp.sum(skip_grad.reshape(windows, local_rows, 2, D), axis=2)
    grad_down_low = grad_hidden.astype(bf16)
    grad_w_down = jnp.einsum("wrf,wrd->fd", activated, grad_down_low, preferred_element_type=f32)
    grad_down_bias = jnp.sum(grad_down_low.astype(f32), axis=(0, 1))
    grad_active = jnp.einsum("wrd,fd->wrf", grad_down_low, w_down, preferred_element_type=f32)
    grad_before = (grad_active * gelu_slope(before)).astype(bf16)
    grad_w_up = jnp.einsum("wrd,wrf->df", low_two, grad_before, preferred_element_type=f32)
    grad_up_bias = jnp.sum(grad_before.astype(f32), axis=(0, 1))
    grad_norm_two = jnp.einsum("wrf,df->wrd", grad_before, w_up, preferred_element_type=f32)
    grad_mid = grad_hidden + norm_back(grad_norm_two, stats_two, inverse_two, vectors[2])
    grad_gain_two = jnp.sum(grad_norm_two * stats_two, axis=(0, 1))
    grad_bias_two = jnp.sum(grad_norm_two, axis=(0, 1))
    grad_attn_low = grad_mid.astype(bf16)
    grad_w_out = jnp.einsum("wcr,wrd->cd", heads, grad_attn_low, preferred_element_type=f32)
    grad_out_bias = jnp.sum(grad_attn_low.astype(f32), axis=(0, 1))
    grad_heads = jnp.einsum("wrd,cd->wcr", grad_attn_low, w_out, preferred_element_type=f32)
    grad_heads = grad_heads.astype(bf16).reshape(windows, 2, at.group, own, VD, local_rows)

    middle = jnp.concatenate(
        [
            grad_up_bias,
            grad_gain_two,
            grad_bias_two,
            grad_out_bias,
            grad_down_bias,
            grad_point_bias,
            grad_tap_zero,
            grad_tap_one,
            grad_tap_two,
            grad_human,
            grad_mouse,
        ]
    )
    middle = sum_everywhere(middle)
    later_rows = jnp.zeros((ROWS - QKV_ROWS, D), bf16)
    start = 0
    for matrix in (grad_w_out, grad_w_up, grad_w_down, grad_w_point):
        matrix = matrix.astype(bf16).reshape(-1, D)
        later_rows = lax.dynamic_update_slice_in_dim(later_rows, matrix, start, 0)
        start += matrix.shape[0]
    grad_heads = [grad_heads[:, :, :, head : head + 1] for head in range(own)]
    later_rows, grad_heads[1:] = lax.optimization_barrier((later_rows, grad_heads[1:]))
    own_rows = ROWS // lax.axis_size(("dp", "seq"))
    buffer = jnp.zeros((own_rows + TAIL // D + 2 * MARGIN, D), bf16)
    later_piece = scatter_sums(later_rows)

    dq, dk, dv, dt = ([], [], [], [])
    for head in range(own):
        chunk = at.rows_to_heads(grad_heads[head])
        pieces = attention_backward(
            tables[head],
            queries[head],
            key_rows[head],
            keys[head],
            value_rows[head],
            heads_out[head],
            at.to_lanes(chunk[:, 0]),
            lse[head],
        )
        for piece, held in zip(pieces, (dq, dk, dv, dt), strict=True):
            held.append(piece)
    grad_query = jnp.concatenate(dq, axis=0)
    grad_key = jnp.concatenate(dk, axis=1)
    grad_value = jnp.concatenate(dv, axis=1)
    partial = (
        jnp.einsum("kr,dk->rd", grad_query, w_query, preferred_element_type=f32)
        + jnp.einsum("rk,dk->rd", grad_key, w_key, preferred_element_type=f32)
        + jnp.einsum("rk,dk->rd", grad_value, w_value, preferred_element_type=f32)
    )
    grad_norm_one = at.sums_to_rows(at.sum_rows(partial)).astype(f32)
    grad_w_query = jnp.einsum("rd,kr->dk", low_all, grad_query, preferred_element_type=f32)
    grad_w_key = jnp.einsum("rd,rk->dk", low_all, grad_key, preferred_element_type=f32)
    grad_w_value = jnp.einsum("rd,rk->dk", low_all, grad_value, preferred_element_type=f32)

    def all_columns(matrix, width):
        whole = jnp.zeros((D, H * width), bf16)
        return lax.dynamic_update_slice_in_dim(
            whole, matrix.astype(bf16), at.head_start * width, 1
        ).reshape(-1, D)

    input_grad = grad_mid + norm_back(grad_norm_one, stats_one, inverse_one, vectors[0])
    grad_gain_one = jnp.sum(grad_norm_one * stats_one, axis=(0, 1))
    grad_bias_one = jnp.sum(grad_norm_one, axis=(0, 1))
    grad_tables = jnp.roll(jnp.concatenate(dt, axis=0), BLOCK - 1, axis=1)[:, : 2 * length - 1]
    grad_pos = jnp.dot(pos_basis.T, grad_tables.T, precision=highest)
    grad_pos = lax.dynamic_update_slice_in_dim(
        jnp.zeros((F, H), f32), grad_pos, at.head_start, 1
    )
    late = jnp.concatenate([grad_pos.reshape(-1), grad_gain_one, grad_bias_one])
    late = sum_everywhere(late)
    special_grads = jnp.concatenate(
        [late[: F * H], middle[:FF], late[F * H :], middle[FF:]]
    )
    first_rows = jnp.concatenate(
        [
            all_columns(grad_w_query, KD),
            all_columns(grad_w_key, KD),
            all_columns(grad_w_value, VD),
        ],
        axis=0,
    )
    first_rows, later_piece = lax.optimization_barrier((first_rows, later_piece))
    buffer = to_owners(buffer, later_piece, QKV_ROWS)
    buffer = to_owners(buffer, scatter_sums(first_rows), 0)
    reduced = own_entries(buffer, special_grads)
    shard_len = params.shape[0]
    position = lax.axis_index(("dp", "seq")) * shard_len + jnp.arange(shard_len)
    param_new, first_new, second_new = adam_update(
        params, first_moment, second_moment, reduced, position
    )
    return (
        block_out,
        input_grad,
        skip_grad,
        param_new,
        first_new,
        second_new,
        param_new.astype(bf16),
    )


def solution(mesh):
    return jax.shard_map(
        body,
        mesh=mesh,
        in_specs=(
            P("dp", "seq", None),
            P("dp", "seq", None),
            P("dp"),
            P("dp", "seq", None),
            P(("dp", "seq")),
            P(("dp", "seq")),
            P(("dp", "seq")),
        ),
        out_specs=(
            P("dp", "seq", None),
            P("dp", "seq", None),
            P("dp", "seq", None),
            P(("dp", "seq")),
            P(("dp", "seq")),
            P(("dp", "seq")),
            P(("dp", "seq")),
        ),
        check_vma=False,
    )
```

profile of v0, /device:TPU:16, one launch (start us, length us, event | category | flops | bytes accessed | tf_op | source)
XLA Modules:
  0.0 1393.3 jit_solution(4205611061835872357)
XLA Ops:
  70.7 110.8 %all-to-all-done = bf16[16,64,1536]{2,1,0:T(8,128)(2,1)S(1)} async-done(((bf16[16,64,1536]{2,1,0:T(8,128)(2,1)}), bf16[16,64,1536]{2,1,0:T(8,128)(2,1)S(1)}, u32[]{:S(2)}, u32[]{:S(2)}) %all-to-all-start) | async-done | bytes 3145760 | tf_op jit(solution)/shard_map/all_to_all | solution.py:368
  278.0 21.9 %all-to-all-done.1 = bf16[16,1,192,128]{3,2,1,0:T(8,128)(2,1)} async-done(((bf16[16,1,192,128]{3,2,1,0:T(8,128)(2,1)}), bf16[16,1,192,128]{3,2,1,0:T(8,128)(2,1)}, u32[]{:S(2)}, u32[]{:S(2)}) %all-to-all-start.1) | async-done | bytes 786464 | tf_op jit(solution)/shard_map/all_to_all | solution.py:368
  320.1 28.5 %all-to-all-done.2 = bf16[16,1,192,128]{3,2,1,0:T(8,128)(2,1)} async-done(((bf16[16,1,192,128]{3,2,1,0:T(8,128)(2,1)}), bf16[16,1,192,128]{3,2,1,0:T(8,128)(2,1)}, u32[]{:S(2)}, u32[]{:S(2)}) %all-to-all-start.2) | async-done | bytes 786464 | tf_op jit(solution)/shard_map/all_to_all | solution.py:368
  367.9 21.2 %all-to-all-done.3 = bf16[16,1,192,128]{3,2,1,0:T(8,128)(2,1)S(1)} async-done(((bf16[16,1,192,128]{3,2,1,0:T(8,128)(2,1)}), bf16[16,1,192,128]{3,2,1,0:T(8,128)(2,1)S(1)}, u32[]{:S(2)}, u32[]{:S(2)}) %all-to-all-start.3) | async-done | bytes 786464 | tf_op jit(solution)/shard_map/all_to_all | solution.py:368
  404.5 29.5 %all-to-all-done.4 = bf16[16,1,192,128]{3,2,1,0:T(8,128)(2,1)S(1)} async-done(((bf16[16,1,192,128]{3,2,1,0:T(8,128)(2,1)}), bf16[16,1,192,128]{3,2,1,0:T(8,128)(2,1)S(1)}, u32[]{:S(2)}, u32[]{:S(2)}) %all-to-all-start.4) | async-done | bytes 786464 | tf_op jit(solution)/shard_map/all_to_all | solution.py:368
  488.2 21.1 %fusion.59 = (u8[128,3072]{1,0:T(8,128)(4,1)S(1)}, u8[128,3072]{1,0:T(8,128)(4,1)S(1)}, f32[8,128,3072]{2,1,0:T(8,128)}) fusion(f32[3072]{0:T(1024)S(1)} %copy-done.86, bf16[1536,3072,1]{1,0,2:T(8,128)(2,1)} %reshape.356, f32[8,128,1536]{2,1,0:T(8,128)} %copy-done.58, f32[1536]{0:T(1024)S(1)} %copy-done.104, f32[1536]{0:T(1024)S(1)} %copy-done.91, ...), kind=kOutput, calls=%fused_computation.133 | convolution fusion | flops 9714794496 | bytes 29130752 | tf_op jit(solution)/shard_map/wrd,df->wrf/dot_general | solution.py:599
  509.3 30.3 %fusion.5 = bf16[8,128,3072]{2,1,0:T(8,128)(2,1)S(1)} fusion(f32[8,128,3072]{2,1,0:T(8,128)} %get-tuple-element.173, f32[3072]{0:T(1024)S(1)} %copy-done.86, u8[128,3072]{1,0:T(8,128)(4,1)S(1)} %get-tuple-element.68, u8[128,3072]{1,0:T(8,128)(4,1)S(1)} %get-tuple-element.67), kind=kLoop, calls=%fused_computation.19 | loop fusion | flops 223346688 | bytes 19673088 | tf_op jit(solution)/shard_map/convert_element_type | solution.py:600
  560.5 15.6 %reshape.340 = f32[8,256,1536]{2,1,0:T(8,128)} reshape(f32[8,128,2,1536]{3,2,1,0:T(2,128)} %broadcast_in_dim.103) | data formatting | bytes 25165824 | tf_op jit(solution)/shard_map/reshape | solution.py:604
  621.7 48.0 %fusion.18 = (f32[1536]{0:T(1024)}, f32[1536]{0:T(1024)}, f32[1536]{0:T(1024)}, f32[8,256,1536]{2,1,0:T(8,128)}, bf16[8,256,1536]{2,1,0:T(8,128)(2,1)}, /*index=5*/f32[1536]{0:T(1024)}, f32[8,1536]{1,0:T(8,128)}) fusion(bf16[8,256,1536]{2,1,0:T(8,128)(2,1)} %copy-done.113, bf16[8,1,1536]{2,1,0:T(2,128)(2,1)S(1)} %collective-permute-done.10, ...), kind=kOutput, calls=%fused_computation.32 | convolution fusion | flops 9846110208 | bytes 68108288 | tf_op jit(solution)/shard_map/wrd,de->wre/dot_general | solution.py:610
  669.7 14.9 %reshape.341 = f32[8,128,2,1536]{3,2,1,0:T(2,128)} reshape(f32[8,256,1536]{2,1,0:T(8,128)} %get-tuple-element.110) | data formatting | bytes 25165824 | tf_op jit(solution)/shard_map/reshape | solution.py:635
  684.7 19.6 %reduce_sum.229 = f32[8,128,1536]{2,1,0:T(8,128)} reduce(f32[8,128,2,1536]{3,2,1,0:T(2,128)} %reshape.341, f32[]{:T(128)} %constant.57.clone.1), dimensions={2}, to_apply=%region_4.5 | reduce | flops 1572864 | bytes 18874372 | tf_op jit(solution)/shard_map/reduce_sum | solution.py:635
  704.3 21.5 %convert_reduce_fusion.1 = (f32[3072]{0:T(1024)}, bf16[8,128,3072]{2,1,0:T(8,128)(2,1)}) fusion(f32[8,128,3072]{2,1,0:T(8,128)} %get-tuple-element.173, f32[3072]{0:T(1024)S(1)} %copy-done.86, bf16[11776,1536]{1,0:T(8,128)(2,1)} %all-gather.5.cloned.1.call-done, f32[8,128,1536]{2,1,0:T(8,128)} %reduce_sum.229), kind=kOutput, calls=%fused_computation.39 | convolution fusion | flops 9706140672 | bytes 34627584 | tf_op jit(solution)/shard_map/wrd,fd->wrf/dot_general | solution.py:639
  725.8 17.7 %multiply_reduce_fusion = (f32[1536]{0:T(1024)}, f32[8,128]{1,0:T(8,128)S(1)}, f32[8,128]{1,0:T(8,128)S(1)}, f32[1536]{0:T(1024)}, f32[8,128,1536]{2,1,0:T(8,128)}) fusion(f32[8,128,1536]{2,1,0:T(8,128)S(1)} %bitcast.203, f32[8,128]{1,0:T(8,128)S(1)} %add_rsqrt_fusion.2, f32[8,128]{1,0:T(8,128)S(1)} %broadcast_multiply_fusion.7, f32[1536]{0:T(1024)S(1)} %copy-done.91, ...), kind=kOutput, calls=%fused_computation.102 | convolution fusion | flops 9677826048 | bytes 28346368 | tf_op jit(solution)/shard_map/wrf,df->wrd/dot_general | solution.py:643
  743.5 15.6 %bitcast_convert_fusion.1 = bf16[1536,3072]{1,0:T(8,128)(2,1)} fusion(bf16[8,128,3072]{2,1,0:T(8,128)(2,1)} %get-tuple-element.176, f32[8,128,1536]{2,1,0:T(8,128)S(1)} %bitcast.203, f32[1536]{0:T(1024)S(1)} %copy-done.105, f32[1536]{0:T(1024)S(1)} %copy-done.91, f32[8,128]{1,0:T(8,128)S(1)} %add_rsqrt_fusion.2, f32[8,128]{1,0:T(8,128)S(1)} %broadcast_multiply_fusion.7), kind=kOutput, calls=%fused_computation.10 | convolution fusion | flops 9676259328 | bytes 22040576 | tf_op jit(solution)/shard_map/wrd,wrf->df/dot_general | solution.py:641
  815.1 16.5 %fusion.25 = bf16[9216,1536]{1,0:T(8,128)(2,1)} fusion(bf16[9216,1536]{1,0:T(8,128)(2,1)} %constant_dynamic-update-slice_fusion.14, bf16[8,128,3072]{2,1,0:T(8,128)(2,1)} %copy-done.68, f32[8,128,1536]{2,1,0:T(8,128)} %reduce_sum.229), kind=kOutput, calls=%fused_computation.56 | convolution fusion | flops 9669967872 | bytes 22020096 | tf_op jit(solution)/shard_map/wrf,wrd->fd/dot_general | solution.py:637
  831.7 18.6 %fusion.30 = bf16[9216,1536]{1,0:T(8,128)(2,1)} fusion(bf16[9216,1536]{1,0:T(8,128)(2,1)} %fusion.25, bf16[8,256,1536]{2,1,0:T(8,128)(2,1)} %param.19, f32[8,1536]{1,0:T(8,128)S(1)} %copy-done.88, bf16[8,256,1536]{2,1,0:T(8,128)(2,1)S(1)} %bitcast.210, bf16[8,1,1536]{2,1,0:T(2,128)(2,1)S(1)} %collective-permute-done.10, ...), kind=kOutput, calls=%fused_computation.74 | convolution fusion | flops 9722658816 | bytes 17418240 | tf_op jit(solution)/shard_map/wrd,wre->de/dot_general | solution.py:620
  923.0 19.8 %shard_map.211 = (bf16[64,2048]{1,0:T(8,128)(2,1)S(1)}, bf16[2048,64]{1,0:T(8,128)(2,1)S(1)}, bf16[2048,192]{1,0:T(8,128)(2,1)S(1)}, f32[1,4096]{1,0:T(1,128)S(1)}) custom-call(f32[8,4096]{1,0:T(8,128)S(1)} %copy-done.33, bf16[64,2048]{1,0:T(8,128)(2,1)S(1)} %copy-done.21, bf16[2048,64]{1,0:T(8,128)(2,1)S(1)} %copy-done.12, bf16[64,2048]{1,0:T(8,128)(2,1)S(1)} %copy-done.25, ...), custom_call_target="tpu_custom_call" | custom-call | flops 10737418240 | bytes 8388608 | tf_op jit(solution)/shard_map/pallas_call | solution.py:293
  944.7 19.7 %shard_map.212 = (bf16[64,2048]{1,0:T(8,128)(2,1)S(1)}, bf16[2048,64]{1,0:T(8,128)(2,1)S(1)}, bf16[2048,192]{1,0:T(8,128)(2,1)S(1)}, f32[1,4096]{1,0:T(1,128)S(1)}) custom-call(f32[8,4096]{1,0:T(8,128)S(1)} %copy-done.31, bf16[64,2048]{1,0:T(8,128)(2,1)S(1)} %copy-done.19, bf16[2048,64]{1,0:T(8,128)(2,1)S(1)} %copy-done.10, bf16[64,2048]{1,0:T(8,128)(2,1)S(1)} %copy-done.24, ...), custom_call_target="tpu_custom_call" | custom-call | flops 10737418240 | bytes 8388608 | tf_op jit(solution)/shard_map/pallas_call | solution.py:293
  981.7 19.7 %shard_map.213 = (bf16[64,2048]{1,0:T(8,128)(2,1)S(1)}, bf16[2048,64]{1,0:T(8,128)(2,1)S(1)}, bf16[2048,192]{1,0:T(8,128)(2,1)S(1)}, f32[1,4096]{1,0:T(1,128)S(1)}) custom-call(f32[8,4096]{1,0:T(8,128)S(1)} %copy-done.29, bf16[64,2048]{1,0:T(8,128)(2,1)S(1)} %copy-done.17, bf16[2048,64]{1,0:T(8,128)(2,1)S(1)} %copy-done.8, bf16[64,2048]{1,0:T(8,128)(2,1)S(1)} %copy-done.23, ...), custom_call_target="tpu_custom_call" | custom-call | flops 10737418240 | bytes 8388608 | tf_op jit(solution)/shard_map/pallas_call | solution.py:293
  1013.7 19.6 %shard_map.214 = (bf16[64,2048]{1,0:T(8,128)(2,1)S(1)}, bf16[2048,64]{1,0:T(8,128)(2,1)S(1)}, bf16[2048,192]{1,0:T(8,128)(2,1)S(1)}, f32[1,4096]{1,0:T(1,128)S(1)}) custom-call(f32[8,4096]{1,0:T(8,128)S(1)} %copy-done.27, bf16[64,2048]{1,0:T(8,128)(2,1)S(1)} %copy-done.15, bf16[2048,64]{1,0:T(8,128)(2,1)S(1)} %copy-done.6, bf16[64,2048]{1,0:T(8,128)(2,1)S(1)} %copy-done.22, ...), custom_call_target="tpu_custom_call" | custom-call | flops 10737418240 | bytes 8388608 | tf_op jit(solution)/shard_map/pallas_call | solution.py:293
  1123.4 57.9 %reduce-scatter.3.cloned.1.call-done = bf16[288,1536]{1,0:T(8,128)(2,1)} async-done(((bf16[9216,1536]{1,0:T(8,128)(2,1)}), bf16[288,1536]{1,0:T(8,128)(2,1)}) %reduce-scatter.3.cloned.1.call-update) | async-done | bytes 884752 | tf_op jit(solution)/shard_map/reduce_scatter | solution.py:501
  1181.9 24.4 %all-to-all-done.9 = bf16[16,64,1536]{2,1,0:T(8,128)(2,1)} async-done(((bf16[16,64,1536]{2,1,0:T(8,128)(2,1)}), bf16[16,64,1536]{2,1,0:T(8,128)(2,1)}, u32[]{:S(2)}, u32[]{:S(2)}) %all-to-all-start.9) | async-done | bytes 3145760 | tf_op jit(solution)/shard_map/all_to_all | solution.py:368
  1289.7 23.7 %collective-permute-done.20 = bf16[288,1536]{1,0:T(8,128)(2,1)S(1)} collective-permute-done((bf16[288,1536]{1,0:T(8,128)(2,1)}, bf16[288,1536]{1,0:T(8,128)(2,1)S(1)}, u32[]{:S(2)}, u32[]{:S(2)}) %collective-permute-start.20) | collective-permute-done | bytes 884768 | tf_op jit(solution)/shard_map/ppermute | solution.py:517
  1314.3 35.8 %reduce-scatter.5.cloned.1.call-done = bf16[80,1536]{1,0:T(8,128)(2,1)} async-done(((bf16[2560,1536]{1,0:T(8,128)(2,1)}), bf16[80,1536]{1,0:T(8,128)(2,1)}) %reduce-scatter.5.cloned.1.call-update) | async-done | bytes 245776 | tf_op jit(solution)/shard_map/reduce_scatter | solution.py:501
  (572 shorter events, 688.5 us)
Async XLA Ops:
  7.2 177.4 %all-gather.3.cloned.1.call-start = ((), (), s32[]{:S(2)}) async-start(), calls=%async_computation.12 | async-start | bytes 11354112 | tf_op jit(solution)/shard_map/all_gather | solution.py:471
  42.7 410.3 %all-gather.5.cloned.1.call-start = ((), (), s32[]{:S(2)}) async-start(), calls=%async_computation.13 | async-start | bytes 37306368 | tf_op jit(solution)/shard_map/all_gather | solution.py:479
  55.0 126.5 %all-to-all-start = ((bf16[16,64,1536]{2,1,0:T(8,128)(2,1)}), bf16[16,64,1536]{2,1,0:T(8,128)(2,1)S(1)}, u32[]{:S(2)}, u32[]{:S(2)}) async-start(bf16[16,64,1536]{2,1,0:T(8,128)(2,1)} %pad_maximum_fusion.10), calls=%async_computation | async-start | bytes 6291456 | tf_op jit(solution)/shard_map/all_to_all | solution.py:368
  188.6 24.4 %collective-permute-start.4 = (bf16[16,1,64,1536]{3,2,0,1:T(8,128)(2,1)}, bf16[16,1,64,1536]{3,2,0,1:T(8,128)(2,1)}, u32[]{:S(2)}, u32[]{:S(2)}) collective-permute-start(bf16[16,1,64,1536]{3,2,0,1:T(8,128)(2,1)} %fusion.83), channel_id=1, source_target_pairs={{0,16},{16,0},{1,17},{17,1},{2,18},{18,2},{3,19},{19,3},{4,20},{20... | collective-permute-start | bytes 9437192 | tf_op jit(solution)/shard_map/ppermute | solution.py:355
  251.7 48.2 %all-to-all-start.1 = ((bf16[16,1,192,128]{3,2,1,0:T(8,128)(2,1)}), bf16[16,1,192,128]{3,2,1,0:T(8,128)(2,1)}, u32[]{:S(2)}, u32[]{:S(2)}) async-start(bf16[16,1,192,128]{3,2,1,0:T(8,128)(2,1)} %bitcast.16), calls=%async_computation.1 | async-start | bytes 1572864 | tf_op jit(solution)/shard_map/all_to_all | solution.py:368
  299.9 48.6 %all-to-all-start.2 = ((bf16[16,1,192,128]{3,2,1,0:T(8,128)(2,1)}), bf16[16,1,192,128]{3,2,1,0:T(8,128)(2,1)}, u32[]{:S(2)}, u32[]{:S(2)}) async-start(bf16[16,1,192,128]{3,2,1,0:T(8,128)(2,1)} %bitcast.22), calls=%async_computation.2 | async-start | bytes 1572864 | tf_op jit(solution)/shard_map/all_to_all | solution.py:368
  348.5 40.6 %all-to-all-start.3 = ((bf16[16,1,192,128]{3,2,1,0:T(8,128)(2,1)}), bf16[16,1,192,128]{3,2,1,0:T(8,128)(2,1)S(1)}, u32[]{:S(2)}, u32[]{:S(2)}) async-start(bf16[16,1,192,128]{3,2,1,0:T(8,128)(2,1)} %bitcast.28), calls=%async_computation.3 | async-start | bytes 1572864 | tf_op jit(solution)/shard_map/all_to_all | solution.py:368
  389.1 44.9 %all-to-all-start.4 = ((bf16[16,1,192,128]{3,2,1,0:T(8,128)(2,1)}), bf16[16,1,192,128]{3,2,1,0:T(8,128)(2,1)S(1)}, u32[]{:S(2)}, u32[]{:S(2)}) async-start(bf16[16,1,192,128]{3,2,1,0:T(8,128)(2,1)} %bitcast.34), calls=%async_computation.4 | async-start | bytes 1572864 | tf_op jit(solution)/shard_map/all_to_all | solution.py:368
  399.6 781.7 %reduce-scatter.3.cloned.1.call-start = ((), (), s32[]{:S(2)}) async-start(), calls=%async_computation.14 | async-start | bytes 29196288 | tf_op jit(solution)/shard_map/reduce_scatter | solution.py:501
  400.7 33.4 %collective-permute-start.5 = (bf16[8,1,1,1,192,128]{5,4,0,3,2,1:T(8,128)(2,1)S(1)}, bf16[8,1,1,1,192,128]{5,4,0,3,2,1:T(8,128)(2,1)S(1)}, u32[]{:S(2)}, u32[]{:S(2)}) collective-permute-start(bf16[8,1,1,1,192,128]{5,4,0,3,2,1:T(8,128)(2,1)S(1)} %dynamic-slice_bitcast_fusion.7), channel_id=1, source_target_pairs={{0,16},{16,0},{1,17},{17,1},{2,18},{18,2},{3,19},{19,3},{4,20},{20... | collective-permute-start | bytes 1179656 | tf_op jit(solution)/shard_map/ppermute | solution.py:355
  403.9 31.3 %collective-permute-start.6 = (bf16[8,1,1,1,192,128]{5,4,0,3,2,1:T(8,128)(2,1)}, bf16[8,1,1,1,192,128]{5,4,0,3,2,1:T(8,128)(2,1)S(1)}, u32[]{:S(2)}, u32[]{:S(2)}) collective-permute-start(bf16[8,1,1,1,192,128]{5,4,0,3,2,1:T(8,128)(2,1)} %dynamic-slice_bitcast_fusion.6), channel_id=1, source_target_pairs={{0,16},{16,0},{1,17},{17,1},{2,18},{18,2},{3,19},{19,3},{4,20},{20... | collective-permute-start | bytes 1179656 | tf_op jit(solution)/shard_map/ppermute | solution.py:355
  404.4 31.9 %collective-permute-start.7 = (bf16[8,1,1,1,192,128]{5,4,0,3,2,1:T(8,128)(2,1)S(1)}, bf16[8,1,1,1,192,128]{5,4,0,3,2,1:T(8,128)(2,1)S(1)}, u32[]{:S(2)}, u32[]{:S(2)}) collective-permute-start(bf16[8,1,1,1,192,128]{5,4,0,3,2,1:T(8,128)(2,1)S(1)} %dynamic-slice_bitcast_fusion.5), channel_id=1, source_target_pairs={{0,16},{16,0},{1,17},{17,1},{2,18},{18,2},{3,19},{19,3},{4,20},{20... | collective-permute-start | bytes 1179656 | tf_op jit(solution)/shard_map/ppermute | solution.py:355
  588.3 27.5 %collective-permute-start.10 = (bf16[8,1,1536]{2,1,0:T(2,128)(2,1)S(1)}, bf16[8,1,1536]{2,1,0:T(2,128)(2,1)S(1)}, u32[]{:S(2)}, u32[]{:S(2)}) collective-permute-start(bf16[8,1,1536]{2,1,0:T(2,128)(2,1)S(1)} %get-tuple-element.118), channel_id=1, source_target_pairs={{1,0},{2,1},{3,2},{4,3},{5,4},{6,5},{7,6},{8,7},{9,8},{10,9},{11,1... | collective-permute-start | bytes 73736 | tf_op jit(solution)/shard_map/ppermute | solution.py:41
  856.2 29.3 %all-to-all-start.5 = ((bf16[16,1,192,128]{3,2,1,0:T(8,128)(2,1)}), bf16[16,1,192,128]{3,2,1,0:T(8,128)(2,1)}, u32[]{:S(2)}, u32[]{:S(2)}) async-start(bf16[16,1,192,128]{3,2,1,0:T(8,128)(2,1)} %maximum_bitcast_fusion), calls=%async_computation.5 | async-start | bytes 1572864 | tf_op jit(solution)/shard_map/all_to_all | solution.py:368
  885.4 25.9 %all-to-all-start.6 = ((bf16[16,1,192,128]{3,2,1,0:T(8,128)(2,1)}), bf16[16,1,192,128]{3,2,1,0:T(8,128)(2,1)}, u32[]{:S(2)}, u32[]{:S(2)}) async-start(bf16[16,1,192,128]{3,2,1,0:T(8,128)(2,1)} %maximum_bitcast_fusion.1), calls=%async_computation.6 | async-start | bytes 1572864 | tf_op jit(solution)/shard_map/all_to_all | solution.py:368
  911.3 56.1 %all-to-all-start.7 = ((bf16[16,1,192,128]{3,2,1,0:T(8,128)(2,1)}), bf16[16,1,192,128]{3,2,1,0:T(8,128)(2,1)}, u32[]{:S(2)}, u32[]{:S(2)}) async-start(bf16[16,1,192,128]{3,2,1,0:T(8,128)(2,1)} %maximum_bitcast_fusion.2), calls=%async_computation.7 | async-start | bytes 1572864 | tf_op jit(solution)/shard_map/all_to_all | solution.py:368
  967.5 42.6 %all-to-all-start.8 = ((bf16[16,1,192,128]{3,2,1,0:T(8,128)(2,1)}), bf16[16,1,192,128]{3,2,1,0:T(8,128)(2,1)S(1)}, u32[]{:S(2)}, u32[]{:S(2)}) async-start(bf16[16,1,192,128]{3,2,1,0:T(8,128)(2,1)} %maximum_bitcast_fusion.3), calls=%async_computation.8 | async-start | bytes 1572864 | tf_op jit(solution)/shard_map/all_to_all | solution.py:368
  1072.4 31.1 %collective-permute-start.17 = (bf16[16,64,1536]{2,1,0:T(8,128)(2,1)}, bf16[16,64,1536]{2,1,0:T(8,128)(2,1)}, u32[]{:S(2)}, u32[]{:S(2)}) collective-permute-start(bf16[16,64,1536]{2,1,0:T(8,128)(2,1)} %fusion.55), channel_id=1, source_target_pairs={{0,16},{16,0},{1,17},{17,1},{2,18},{18,2},{3,19},{19,3},{4,20},{20... | collective-permute-start | bytes 9437192 | tf_op jit(solution)/shard_map/ppermute | solution.py:355
  1108.1 98.1 %all-to-all-start.9 = ((bf16[16,64,1536]{2,1,0:T(8,128)(2,1)}), bf16[16,64,1536]{2,1,0:T(8,128)(2,1)}, u32[]{:S(2)}, u32[]{:S(2)}) async-start(bf16[16,64,1536]{2,1,0:T(8,128)(2,1)} %fusion.48), calls=%async_computation.9 | async-start | bytes 6291456 | tf_op jit(solution)/shard_map/all_to_all | solution.py:368
  1116.8 233.3 %reduce-scatter.5.cloned.1.call-start = ((), (), s32[]{:S(2)}) async-start(), calls=%async_computation.15 | async-start | bytes 8110080 | tf_op jit(solution)/shard_map/reduce_scatter | solution.py:501
  1240.5 25.1 %collective-permute-start.37 = (f32[18432]{0:T(1024)S(1)}, f32[18432]{0:T(1024)S(1)}, u32[]{:S(2)}, u32[]{:S(2)}) collective-permute-start(f32[18432]{0:T(1024)S(1)} %add.389), channel_id=1, source_target_pairs={{0,8},{1,9},{2,10},{3,11},{4,12},{5,13},{6,14},{7,15},{8,0},{9,1},... | collective-permute-start | bytes 221192 | tf_op jit(solution)/shard_map/ppermute | solution.py:495
  1241.5 24.2 %collective-permute-start.29 = (f32[4608]{0:T(1024)S(1)}, f32[4608]{0:T(1024)S(1)}, u32[]{:S(2)}, u32[]{:S(2)}) collective-permute-start(f32[4608]{0:T(1024)S(1)} %fusion.139), channel_id=1, source_target_pairs={{0,1},{1,0},{2,3},{3,2},{4,5},{5,4},{6,7},{7,6},{8,9},{9,8},{10,11... | collective-permute-start | bytes 55304 | tf_op jit(solution)/shard_map/ppermute | solution.py:495
  1276.3 37.0 %collective-permute-start.20 = (bf16[288,1536]{1,0:T(8,128)(2,1)}, bf16[288,1536]{1,0:T(8,128)(2,1)S(1)}, u32[]{:S(2)}, u32[]{:S(2)}) collective-permute-start(bf16[288,1536]{1,0:T(8,128)(2,1)} %reduce-scatter.3.cloned.1.call-done), channel_id=1, source_target_pairs={{0,7},{1,8},{2,9},{3,10},{5,11},{6,12},{7,13},{9,14},{10,15},{11,1... | collective-permute-start | bytes 2654216 | tf_op jit(solution)/shard_map/ppermute | solution.py:517
  1277.6 73.9 %collective-permute-start.21 = (bf16[288,1536]{1,0:T(8,128)(2,1)}, bf16[288,1536]{1,0:T(8,128)(2,1)}, u32[]{:S(2)}, u32[]{:S(2)}) collective-permute-start(bf16[288,1536]{1,0:T(8,128)(2,1)} %reduce-scatter.3.cloned.1.call-done), channel_id=1, source_target_pairs={{1,7},{2,8},{3,9},{4,10},{6,11},{7,12},{8,13},{10,14},{11,15},{12,... | collective-permute-start | bytes 2654216 | tf_op jit(solution)/shard_map/ppermute | solution.py:517
  (167 other events, 3260.8 us)
Sparse Core Ops, SparseCore 0:
  42.8 141.7 all-gather.2
  188.1 264.8 all-gather.4
  850.4 330.8 reduce-scatter.2
  1186.7 163.3 reduce-scatter.4
where the time goes:
time: 1410 us; the launch traced here: 1390 us
  waiting for transfers between devices  436 us (31%)
  matrix products  289 us (20%)
  local copies, waits for them, and re-layouts  234 us (17%)
  starting transfers between devices  135 us (10%)
  other arithmetic  135 us (10%)
  Pallas kernels  131 us (9%)
  between operations  33 us (2%)
    all_to_all x10, waiting for transfers between devices, exchange(): return lax.all_to_all(array, 'seq', split_axis=0, concat_axis=0, tiled=True)  262 us
    reduce_scatter x2, waiting for transfers between devices, scatter_sums(): lax.psum_scatter(rows, ('dp', 'seq'), scatter_dimension=0, tiled=True)  93.7 us
    all_to_all x10, starting transfers between devices, exchange(): return lax.all_to_all(array, 'seq', split_axis=0, concat_axis=0, tiled=True)  84.3 us
    pallas_call x4, Pallas kernels, attention_backward(): pl.pallas_call(functools.partial(backward_kernel, blocks=blocks), grid=(b...  78.9 us
    pallas_call x4, Pallas kernels, attention_forward(): pl.pallas_call(functools.partial(forward_kernel, blocks=blocks), grid=(bl...  52.6 us
    dot_general x1, matrix products, body(): jnp.einsum('wrd,de->wre', conv_low, w_point, preferred_element_type=f32)  48 us
    unnamed x287, local copies, waits for them, and re-layouts  38.1 us
    convert_element_type x1, other arithmetic, body(): activated = jax.nn.gelu(before, approximate=False).astype(bf16)  30.3 us
  transfers between devices with their start and end apart: 52, of which 25 were waited for; matrix products, arithmetic and copies ran while one was open for 17% of the time, Pallas kernels for 9%

commit v1 on v0

v1 whole, which is shorter than its diff:
```python
import functools
import math

import jax
import jax.numpy as jnp
from jax import lax
from jax.experimental import pallas as pl
from jax.experimental.pallas import tpu as pltpu
from jax.sharding import PartitionSpec as P

D = 1536
H = 8
KD = 64
VD = 192
FF = 3072
F = 192
STEP = 10
BLOCK = 256
PAIR = 2
CHUNK = 512
WIDE = 768
LANES = 128
ROWS = 11776
QKV_ROWS = 2560
TAIL = 24576
MARGIN = 288
UNIT = 16
UNITS = 288


eps_norm = 1e-05
beta_one = 0.5
beta_two = 0.5
adam_eps = 1e-08
decay_rate = 0.01
highest = lax.Precision.HIGHEST


def edge_rows(array):
    devices = lax.axis_size("seq")
    up = [(i, i + 1) for i in range(devices - 1)]
    first = lax.ppermute(array[1], "seq", up)
    last = lax.ppermute(array[0], "seq", [(j, i) for i, j in up])
    return (first, last)


def segment_ends():
    counts = [
        D * H * KD,
        D * H * KD,
        D * H * VD,
        H * VD * D,
        D * FF,
        FF * D,
        D * D,
        F * H,
        FF,
        12 * D,
    ]
    limits = []
    running = 0
    for amount in counts:
        running = running + amount
        limits.append(running)
    return limits


def rate_at(position):
    limits = segment_ends()
    step_rates = [
        2.0 / math.sqrt(D),
        2.0 / math.sqrt(D),
        2.0 / math.sqrt(D),
        8.0 / math.sqrt(H * VD),
        2.0 / math.sqrt(D),
        2.0 / math.sqrt(FF),
        2.0 / math.sqrt(D),
        3.0 / math.sqrt(F),
        0.4,
        0.4,
    ]
    result = jnp.full(position.shape, step_rates[-1], jnp.float32)
    for segment in range(len(limits) - 2, -1, -1):
        result = jnp.where(position < limits[segment], step_rates[segment], result)
    return result


def adam_update(param_old, first_old, second_old, gradient, position):
    step_rate = rate_at(position)
    first_new = beta_one * first_old + (1.0 - beta_one) * gradient
    second_new = beta_two * second_old + (1.0 - beta_two) * gradient * gradient
    first_hat = first_new / (1.0 - beta_one**STEP)
    second_hat = second_new / (1.0 - beta_two**STEP)
    param_new = param_old - step_rate * (
        first_hat / (jnp.sqrt(second_hat) + adam_eps) + decay_rate * param_old
    )
    return (param_new, first_new, second_new)


def position_basis(length):
    offsets = jnp.arange(2 * length - 1).astype(jnp.float32) - (length - 1)
    halves = F // 2
    ladder = jnp.arange(halves).astype(jnp.float32) / max(halves - 1, 1)
    lifetimes = jnp.exp(ladder * math.log(length))
    decays = jnp.exp(-jnp.abs(offsets)[:, None] * (math.log(2.0) / lifetimes)[None, :])
    return jnp.concatenate([decays, jnp.sign(offsets)[:, None] * decays], axis=1)


def layer_stats(inputs, norm_gain, norm_bias):
    centered = inputs - jnp.mean(inputs, axis=-1, keepdims=True)
    inverse = lax.rsqrt(jnp.mean(centered * centered, axis=-1, keepdims=True) + eps_norm)
    normed = centered * inverse
    return (normed * norm_gain + norm_bias, normed, inverse)


def norm_back(upstream, normed, inverse, norm_gain):
    scaled = upstream * norm_gain
    return inverse * (
        scaled
        - jnp.mean(scaled, axis=-1, keepdims=True)
        - normed * jnp.mean(scaled * normed, axis=-1, keepdims=True)
    )


def spread_rows(first_row, bands):
    start = pltpu.roll(first_row, 0, 1, stride=1, stride_axis=0)
    bands[0:8, :] = start
    height = 8
    while height < BLOCK:
        bands[height : 2 * height, :] = pltpu.roll(bands[0:height, :], height, 1)
        height *= 2


def collect_rows(bands, width):
    height = BLOCK // 2
    while height >= 8:
        bands[0:height, :] = bands[0:height, :] + pltpu.roll(
            bands[height : 2 * height, :], width - height, 1
        )
        height //= 2
    total = bands[0:1, :]
    for row in range(1, 8):
        total = total + pltpu.roll(bands[row : row + 1, :], width - row, 1)
    return total


def forward_kernel(
    table_ref, q_ref, k_ref, v_ref, out_ref, lse_ref, bands, key_rows, scores, *, blocks
):
    block = pl.program_id(0)

    @pl.when(block == 0)
    def _():
        for head in range(PAIR):
            spread_rows(table_ref[head], bands.at[head])
            key_rows[head] = k_ref[head * KD : (head + 1) * KD, :].T

    results = []
    for head in range(PAIR):
        queries = q_ref[head * KD : (head + 1) * KD, :]
        top = jnp.full((1, BLOCK), -jnp.inf, jnp.float32)
        for j in range(blocks):
            at = pl.multiple_of((block - j + blocks - 1) * BLOCK, BLOCK)
            span = slice(j * BLOCK, (j + 1) * BLOCK)
            part = (
                jnp.dot(key_rows[head, span, :], queries, preferred_element_type=jnp.float32)
                + bands[head, :, pl.ds(at, BLOCK)]
            )
            scores[span, :] = part
            top = jnp.maximum(top, jnp.max(part, axis=0, keepdims=True))
        total = jnp.zeros((1, BLOCK), jnp.float32)
        result = jnp.zeros((VD, BLOCK), jnp.float32)
        for j in range(blocks):
            span = slice(j * BLOCK, (j + 1) * BLOCK)
            grown = jnp.exp(scores[span, :] - top)
            total = total + jnp.sum(grown, axis=0, keepdims=True)
            result = result + jnp.dot(
                v_ref[head * VD : (head + 1) * VD, span],
                grown.astype(jnp.bfloat16),
                preferred_element_type=jnp.float32,
            )
        results.append(result * (1.0 / total))
        lse_ref[head : head + 1, :] = top + jnp.log(total)
    out_ref[...] = jnp.concatenate(results, axis=0).T.astype(jnp.bfloat16)


def attention_forward(tables, queries, keys, values):
    length = keys.shape[1]
    blocks = length // BLOCK
    return pl.pallas_call(
        functools.partial(forward_kernel, blocks=blocks),
        grid=(blocks,),
        in_specs=[
            pl.BlockSpec((PAIR, 8, 2 * length), lambda i: (0, 0, 0)),
            pl.BlockSpec((PAIR * KD, BLOCK), lambda i: (0, i)),
            pl.BlockSpec((PAIR * KD, length), lambda i: (0, 0)),
            pl.BlockSpec((PAIR * VD, length), lambda i: (0, 0)),
        ],
        out_specs=[
            pl.BlockSpec((BLOCK, PAIR * VD), lambda i: (i, 0)),
            pl.BlockSpec((PAIR, BLOCK), lambda i: (0, i)),
        ],
        out_shape=[
            jax.ShapeDtypeStruct((length, PAIR * VD), jnp.bfloat16),
            jax.ShapeDtypeStruct((PAIR, length), jnp.float32),
        ],
        scratch_shapes=[
            pltpu.VMEM((PAIR, BLOCK, 2 * length), jnp.float32),
            pltpu.VMEM((PAIR, length, KD), jnp.bfloat16),
            pltpu.VMEM((length, BLOCK), jnp.float32),
        ],
        compiler_params=pltpu.CompilerParams(vmem_limit_bytes=48 * 2**20),
        cost_estimate=pl.CostEstimate(
            flops=(4 * PAIR * length * length * 256) // 16,
            bytes_accessed=(8 * PAIR * length * (KD + VD)) // 16,
            transcendentals=PAIR * length * length // 16,
        ),
    )(tables, queries, keys, values)


def backward_kernel(
    table_ref,
    q_ref,
    k_ref,
    v_ref,
    out_ref,
    grad_ref,
    lse_ref,
    dq_ref,
    dk_ref,
    dv_ref,
    dt_ref,
    bands,
    grad_bands,
    key_rows,
    value_rows,
    dk_sum,
    dv_sum,
    *,
    blocks,
):
    block = pl.program_id(0)

    @pl.when(block == 0)
    def _():
        for head in range(PAIR):
            spread_rows(table_ref[head], bands.at[head])
            key_rows[head] = k_ref[head * KD : (head + 1) * KD, :].T
            value_rows[head] = v_ref[head * VD : (head + 1) * VD, :].T
        grad_bands[...] = jnp.zeros_like(grad_bands)
        dk_sum[...] = jnp.zeros_like(dk_sum)
        dv_sum[...] = jnp.zeros_like(dv_sum)

    grad_t = grad_ref[...].T
    out_t = out_ref[...].T
    products = grad_t.astype(jnp.float32) * out_t.astype(jnp.float32)
    results = []
    for head in range(PAIR):
        wide = slice(head * VD, (head + 1) * VD)
        delta = jnp.sum(products[wide, :], axis=0, keepdims=True)
        grad_here = grad_t[wide, :]
        grad_rows = grad_here.T
        queries = q_ref[head * KD : (head + 1) * KD, :]
        query_rows = queries.T
        lse = lse_ref[head : head + 1, :]
        dq = jnp.zeros((KD, BLOCK), jnp.float32)
        for j in range(blocks):
            span = slice(j * BLOCK, (j + 1) * BLOCK)
            at = pl.multiple_of((block - j + blocks - 1) * BLOCK, BLOCK)
            part = (
                jnp.dot(key_rows[head, span, :], queries, preferred_element_type=jnp.float32)
                + bands[head, :, pl.ds(at, BLOCK)]
            )
            soft = jnp.exp(part - lse)
            grad_soft = jnp.dot(
                value_rows[head, span, :], grad_here, preferred_element_type=jnp.float32
            )
            grad_scores = soft * (grad_soft - delta)
            grad_bands[head, :, pl.ds(at, BLOCK)] = (
                grad_bands[head, :, pl.ds(at, BLOCK)] + grad_scores
            )
            low = grad_scores.astype(jnp.bfloat16)
            dv_sum[head, span, :] = dv_sum[head, span, :] + jnp.dot(
                soft.astype(jnp.bfloat16), grad_rows, preferred_element_type=jnp.float32
            )
            dk_sum[head, span, :] = dk_sum[head, span, :] + jnp.dot(
                low, query_rows, preferred_element_type=jnp.float32
            )
            dq = dq + jnp.dot(
                k_ref[head * KD : (head + 1) * KD, span], low, preferred_element_type=jnp.float32
            )
        results.append(dq)
    dq_ref[...] = jnp.concatenate(results, axis=0).T.astype(jnp.bfloat16)

    @pl.when(block == blocks - 1)
    def _():
        dk_ref[...] = jnp.concatenate(
            [dk_sum[head] for head in range(PAIR)], axis=1
        ).astype(jnp.bfloat16)
        dv_ref[...] = jnp.concatenate(
            [dv_sum[head] for head in range(PAIR)], axis=1
        ).astype(jnp.bfloat16)
        for head in range(PAIR):
            dt_ref[head : head + 1, :] = collect_rows(
                grad_bands.at[head], grad_bands.shape[2]
            )


def attention_backward(tables, queries, keys, values, heads, grad_heads, lse):
    length = keys.shape[1]
    blocks = length // BLOCK
    return pl.pallas_call(
        functools.partial(backward_kernel, blocks=blocks),
        grid=(blocks,),
        in_specs=[
            pl.BlockSpec((PAIR, 8, 2 * length), lambda i: (0, 0, 0)),
            pl.BlockSpec((PAIR * KD, BLOCK), lambda i: (0, i)),
            pl.BlockSpec((PAIR * KD, length), lambda i: (0, 0)),
            pl.BlockSpec((PAIR * VD, length), lambda i: (0, 0)),
            pl.BlockSpec((BLOCK, PAIR * VD), lambda i: (i, 0)),
            pl.BlockSpec((BLOCK, PAIR * VD), lambda i: (i, 0)),
            pl.BlockSpec((PAIR, BLOCK), lambda i: (0, i)),
        ],
        out_specs=[
            pl.BlockSpec((BLOCK, PAIR * KD), lambda i: (i, 0)),
            pl.BlockSpec((length, PAIR * KD), lambda i: (0, 0)),
            pl.BlockSpec((length, PAIR * VD), lambda i: (0, 0)),
            pl.BlockSpec((PAIR, 2 * length), lambda i: (0, 0)),
        ],
        out_shape=[
            jax.ShapeDtypeStruct((length, PAIR * KD), jnp.bfloat16),
            jax.ShapeDtypeStruct((length, PAIR * KD), jnp.bfloat16),
            jax.ShapeDtypeStruct((length, PAIR * VD), jnp.bfloat16),
            jax.ShapeDtypeStruct((PAIR, 2 * length), jnp.float32),
        ],
        scratch_shapes=[
            pltpu.VMEM((PAIR, BLOCK, 2 * length), jnp.float32),
            pltpu.VMEM((PAIR, BLOCK, 2 * length), jnp.float32),
            pltpu.VMEM((PAIR, length, KD), jnp.bfloat16),
            pltpu.VMEM((PAIR, length, VD), jnp.bfloat16),
            pltpu.VMEM((PAIR, length, KD), jnp.float32),
            pltpu.VMEM((PAIR, length, VD), jnp.float32),
        ],
        compiler_params=pltpu.CompilerParams(vmem_limit_bytes=56 * 2**20),
        cost_estimate=pl.CostEstimate(
            flops=(10 * PAIR * length * length * 256) // 16,
            bytes_accessed=(16 * PAIR * length * (KD + VD)) // 16,
            transcendentals=PAIR * length * length // 16,
        ),
    )(tables, queries, keys, values, heads, grad_heads, lse)


def whole_block(array):
    zeros = (0,) * array.ndim
    return pl.BlockSpec(array.shape, lambda i: zeros, pipeline_mode=pl.Buffered(1))


LEFT, DOWN = ((96, 1, UNIT, D), (0, 0)), ((96, 2, UNIT, D), (1, 0))
OUT, POINT = ((48, 2, UNIT, D), (4, 0)), ((48, 2, UNIT, D), (5, 0))


def weight_block(weight):
    shape, place = weight
    return pl.BlockSpec(shape, lambda *i: place + (0, 0), pipeline_mode=pl.Buffered(1))


def up_half(half):
    return pl.BlockSpec(
        (96, 1, UNIT, D), lambda i: (0, half, 0, 0), pipeline_mode=pl.Buffered(1)
    )


def unit_rows(first, rows):
    first, units = (first // (2 * UNIT), rows // (2 * UNIT))
    return pl.BlockSpec(
        (pl.Element(units), pl.Element(2), pl.Element(UNIT), pl.Element(D)),
        lambda i: (first, 0, 0, 0),
        pipeline_mode=pl.Buffered(1),
    )


def up_units_kernel(lower_ref, upper_ref, out_ref, *, steps):
    units = out_ref.shape[0]

    def put(rows_ref):
        rows = rows_ref[...].astype(jnp.float32).reshape(units, 2, 2, 8, D)
        out_ref[...] = (
            jnp.swapaxes(rows, 1, 2).reshape(units, 2, UNIT, D).astype(jnp.bfloat16)
        )

    pl.when(pl.program_id(0) < steps)(lambda: put(lower_ref))
    pl.when(pl.program_id(0) >= steps)(lambda: put(upper_ref))


def up_units(lower, upper):
    units = 8
    start = UP_ROWS[0] // UNIT // (2 * units)
    steps = lower.shape[0] // (2 * units) - start
    return pl.pallas_call(
        functools.partial(up_units_kernel, steps=steps),
        grid=(96 // units,),
        in_specs=[
            pl.BlockSpec(
                (2 * units, UNIT, D), lambda i: (start + jnp.minimum(i, steps - 1), 0, 0)
            ),
            pl.BlockSpec((2 * units, UNIT, D), lambda i: (jnp.maximum(i - steps, 0), 0, 0)),
        ],
        out_specs=pl.BlockSpec((units, 2, UNIT, D), lambda i: (i, 0, 0, 0)),
        out_shape=jax.ShapeDtypeStruct((96, 2, UNIT, D), jnp.bfloat16),
        compiler_params=pltpu.CompilerParams(vmem_limit_bytes=32 * 2**20),
    )(lower, upper)


OUT_ROWS, UP_ROWS, DOWN_ROWS, POINT_ROWS = (2560, D), (4096, FF), (1280, FF), (4352, D)


def step_block(array, count):
    shape = (count,) + array.shape[1:]
    rest = (0,) * (array.ndim - 1)
    return pl.BlockSpec(shape, lambda i: (i,) + rest)


def times_transposed(left, right):
    return lax.dot_general(
        left, right, (((1,), (1,)), ((), ())), preferred_element_type=jnp.float32
    )


def dense_kernel(
    core_ref,
    inputs_ref,
    own_a,
    own_b,
    other_a,
    other_b,
    vectors_ref,
    up_bias_ref,
    w_out_ref,
    w_left_ref,
    w_right_ref,
    w_down_ref,
    heads_ref,
    hidden_ref,
    low_ref,
    active_ref,
    slope_ref,
    after_ref,
    *,
    count,
    rows,
):
    core = core_ref[0]
    total = count * rows
    width = own_a.shape[2]
    hidden = inputs_ref[...].reshape(total, D).astype(jnp.float32) + vectors_ref[4:5, :]
    for number, piece in enumerate((own_a, own_b, other_a, other_b)):
        group = core if number < 2 else 1 - core
        at = pl.multiple_of(group * (2 * width) + (number % 2) * width, 128)
        unit = group * 24 + (number % 2) * 12
        held = piece[...]
        heads_ref[:, :, pl.ds(at, width)] = held
        hidden = hidden + jnp.dot(
            held.reshape(total, width),
            w_out_ref[pl.ds(unit, 12)].reshape(width, D),
            preferred_element_type=jnp.float32,
        )
    hidden_ref[...] = hidden.reshape(count, rows, D)
    normed, _, _ = layer_stats(hidden, vectors_ref[2:3, :], vectors_ref[3:4, :])
    low = normed.astype(jnp.bfloat16)
    low_ref[...] = low.reshape(count, rows, D)
    after = hidden + vectors_ref[5:6, :]
    for number in range(FF // WIDE):
        span = slice(number * WIDE, (number + 1) * WIDE)
        half = (w_left_ref, w_right_ref)[number * WIDE // D]
        start = number * WIDE % D
        units = slice(number * WIDE // 32, (number + 1) * WIDE // 32)
        before = (
            jnp.dot(
                low,
                half[:, 0, :, start : start + WIDE].reshape(D, WIDE),
                preferred_element_type=jnp.float32,
            )
            + up_bias_ref[:, span]
        )
        phi = 0.5 * (1.0 + lax.erf(before * (1.0 / math.sqrt(2.0))))
        slope = phi + before * jnp.exp(-0.5 * before * before) * (1.0 / math.sqrt(2.0 * math.pi))
        active = (before * phi).astype(jnp.bfloat16)
        active_ref[:, :, span] = active.reshape(count, rows, WIDE)
        slope_ref[:, :, span] = slope.astype(jnp.bfloat16).reshape(count, rows, WIDE)
        after = after + jnp.dot(
            active, w_down_ref[units].reshape(WIDE, D), preferred_element_type=jnp.float32
        )
    after_ref[...] = after.reshape(count, rows, D)


def dense_forward(core, inputs, pieces, vectors, up_bias, weights):
    windows, rows, _ = inputs.shape
    count = max(1, 256 // rows)
    shapes = [
        jax.ShapeDtypeStruct((windows, rows, D), jnp.bfloat16),
        jax.ShapeDtypeStruct((windows, rows, D), jnp.float32),
        jax.ShapeDtypeStruct((windows, rows, D), jnp.bfloat16),
        jax.ShapeDtypeStruct((windows, rows, FF), jnp.bfloat16),
        jax.ShapeDtypeStruct((windows, rows, FF), jnp.bfloat16),
        jax.ShapeDtypeStruct((windows, rows, D), jnp.float32),
    ]
    lower, upper, w_up = weights
    return pl.pallas_call(
        functools.partial(dense_kernel, count=count, rows=rows),
        grid=(windows // count,),
        in_specs=[pl.BlockSpec(memory_space=pltpu.SMEM), step_block(inputs, count)]
        + [step_block(piece, count) for piece in pieces]
        + [whole_block(vectors), whole_block(up_bias)]
        + [unit_rows(*OUT_ROWS), up_half(0), up_half(1), unit_rows(*DOWN_ROWS)],
        out_specs=[step_block(shape, count) for shape in shapes],
        out_shape=shapes,
        compiler_params=pltpu.CompilerParams(vmem_limit_bytes=60 * 2**20),
        cost_estimate=pl.CostEstimate(
            flops=(2 * windows * rows * D * (D + 2 * FF)) // 16,
            bytes_accessed=(2 * D * (D + 2 * FF) + 26 * windows * rows * D) // 16,
            transcendentals=2 * windows * rows * FF // 16,
        ),
    )(core, inputs, *pieces, vectors, up_bias, lower, w_up, w_up, upper)


def shifted(rows, first, last):
    count = rows.shape[0]
    place = lax.broadcasted_iota(jnp.int32, rows.shape, 0)
    earlier = jnp.where(place == 0, first, pltpu.roll(rows, 1, 0))
    later = jnp.where(place == count - 1, last, pltpu.roll(rows, count - 1, 0))
    return (earlier, later)


def point_kernel(
    after_ref,
    skip_ref,
    upstream_ref,
    first_ref,
    last_ref,
    gain_ref,
    vectors_ref,
    w_ref,
    out_ref,
    grad_conv_ref,
    grad_w_ref,
    gain_rows_ref,
    sums_ref,
    doubled,
    summed,
    grad_w,
    *,
    rows,
):
    step = pl.program_id(0)

    @pl.when(step == 0)
    def _():
        grad_w[...] = jnp.zeros_like(grad_w)
        sums_ref[...] = jnp.zeros_like(sums_ref)

    for number in range(D // LANES):
        span = slice(number * LANES, (number + 1) * LANES)
        after = after_ref[0, :, span]
        doubled[number, pl.ds(0, rows, stride=2), :] = after
        doubled[number, pl.ds(1, rows, stride=2), :] = after
        summed[:, span] = doubled[number] + skip_ref[0, :, span].astype(jnp.float32)
    low = summed[...].astype(jnp.bfloat16).astype(jnp.float32)
    earlier, later = shifted(
        low, first_ref[0].astype(jnp.float32), last_ref[0].astype(jnp.float32)
    )
    conv = (
        vectors_ref[7:8, :] * earlier + vectors_ref[8:9, :] * low + vectors_ref[9:10, :] * later
    ).astype(jnp.bfloat16)
    conv_t = conv.T
    grad_conv = jnp.zeros((2 * rows, D), jnp.float32)
    for number in range(D // CHUNK):
        span = slice(number * CHUNK, (number + 1) * CHUNK)
        weight = w_ref[:, :, :, span].reshape(D, CHUNK)
        gain = gain_ref[0, :, span]
        upstream = upstream_ref[0, :, span].astype(jnp.float32)
        pointed = (
            jnp.dot(conv, weight, preferred_element_type=jnp.float32) + vectors_ref[6:7, span]
        )
        out_ref[0, :, span] = (summed[:, span] + gain * pointed).astype(jnp.bfloat16)
        gain_rows_ref[0, :, span] = jnp.sum(upstream * pointed, axis=0, keepdims=True)
        grad_point = (gain * upstream).astype(jnp.bfloat16)
        sums_ref[0:1, span] = sums_ref[0:1, span] + jnp.sum(
            grad_point.astype(jnp.float32), axis=0, keepdims=True
        )
        grad_conv = grad_conv + times_transposed(grad_point, weight)
        grad_w[:, span] = grad_w[:, span] + jnp.dot(
            conv_t, grad_point, preferred_element_type=jnp.float32
        )
    grad_low = grad_conv.astype(jnp.bfloat16)
    grad_conv_ref[0] = grad_low
    grad_wide = grad_low.astype(jnp.float32)
    for number, rows_here in enumerate((earlier, low, later)):
        sums_ref[number + 1 : number + 2, :] = sums_ref[number + 1 : number + 2, :] + jnp.sum(
            grad_wide * rows_here, axis=0, keepdims=True
        )

    @pl.when(step == pl.num_programs(0) - 1)
    def _():
        grad_w_ref[...] = grad_w[...].astype(jnp.bfloat16).reshape(POINT[0])


def point_layer(after, skip, upstream, first, last, gains, vectors, weights):
    windows, rows, _ = after.shape
    shapes = [
        jax.ShapeDtypeStruct((windows, 2 * rows, D), jnp.bfloat16),
        jax.ShapeDtypeStruct((windows, 2 * rows, D), jnp.bfloat16),
        jax.ShapeDtypeStruct((UNITS, 2, UNIT, D), jnp.bfloat16),
        jax.ShapeDtypeStruct((windows, 1, D), jnp.float32),
        jax.ShapeDtypeStruct((8, D), jnp.float32),
    ]
    moving = (after, skip, upstream, first, last, gains)
    return pl.pallas_call(
        functools.partial(point_kernel, rows=rows),
        grid=(windows,),
        in_specs=[step_block(array, 1) for array in moving]
        + [whole_block(vectors), unit_rows(*POINT_ROWS)],
        out_specs=[
            step_block(shapes[0], 1),
            step_block(shapes[1], 1),
            weight_block(POINT),
            step_block(shapes[3], 1),
            whole_block(shapes[4]),
        ],
        out_shape=shapes,
        scratch_shapes=[
            pltpu.VMEM((D // LANES, 2 * rows, LANES), jnp.float32),
            pltpu.VMEM((2 * rows, D), jnp.float32),
            pltpu.VMEM((D, D), jnp.float32),
        ],
        compiler_params=pltpu.CompilerParams(vmem_limit_bytes=60 * 2**20),
        cost_estimate=pl.CostEstimate(
            flops=(12 * windows * rows * D * D) // 16,
            bytes_accessed=(4 * D * D + 20 * windows * rows * D) // 16,
            transcendentals=0,
        ),
    )(*moving, vectors, weights[1])


def dense_back_kernel(
    core_ref,
    upstream_ref,
    grad_conv_ref,
    first_ref,
    last_ref,
    slope_ref,
    hidden_ref,
    vectors_ref,
    w_out_ref,
    w_left_ref,
    w_right_ref,
    w_down_ref,
    skip_grad_ref,
    grad_mid_ref,
    grad_down_ref,
    grad_before_ref,
    grad_att_ref,
    own_a,
    own_b,
    other_a,
    other_b,
    sums_ref,
    up_sums_ref,
    doubled,
    *,
    count,
    rows,
):
    core = core_ref[0]
    total = count * rows
    width = own_a.shape[2]

    @pl.when(pl.program_id(0) == 0)
    def _():
        sums_ref[...] = jnp.zeros_like(sums_ref)
        up_sums_ref[...] = jnp.zeros_like(up_sums_ref)

    grads = []
    for window in range(count):
        here = grad_conv_ref[window].astype(jnp.float32)
        earlier, later = shifted(
            here, first_ref[window].astype(jnp.float32), last_ref[window].astype(jnp.float32)
        )
        skip_grad = (
            upstream_ref[window].astype(jnp.float32)
            + vectors_ref[7:8, :] * later
            + vectors_ref[8:9, :] * here
            + vectors_ref[9:10, :] * earlier
        )
        skip_grad_ref[window] = skip_grad
        for number in range(D // LANES):
            doubled[number] = skip_grad[:, number * LANES : (number + 1) * LANES]
        grads.append(
            jnp.concatenate(
                [
                    doubled[number, pl.ds(0, rows, stride=2), :]
                    + doubled[number, pl.ds(1, rows, stride=2), :]
                    for number in range(D // LANES)
                ],
                axis=1,
            )
        )
    grad = jnp.concatenate(grads, axis=0)
    low = grad.astype(jnp.bfloat16)
    grad_down_ref[...] = low.reshape(count, rows, D)
    sums_ref[0:1, :] = sums_ref[0:1, :] + jnp.sum(
        low.astype(jnp.float32), axis=0, keepdims=True
    )
    grad_norm = jnp.zeros((total, D), jnp.float32)
    for number in range(FF // WIDE):
        span = slice(number * WIDE, (number + 1) * WIDE)
        half = (w_left_ref, w_right_ref)[number * WIDE // D]
        start = number * WIDE % D
        units = slice(number * WIDE // 32, (number + 1) * WIDE // 32)
        slope = slope_ref[:, :, span].reshape(total, WIDE).astype(jnp.float32)
        grad_active = times_transposed(low, w_down_ref[units].reshape(WIDE, D))
        grad_before = (grad_active * slope).astype(jnp.bfloat16)
        grad_before_ref[:, :, span] = grad_before.reshape(count, rows, WIDE)
        up_sums_ref[0:1, span] = up_sums_ref[0:1, span] + jnp.sum(
            grad_before.astype(jnp.float32), axis=0, keepdims=True
        )
        grad_norm = grad_norm + times_transposed(
            grad_before, half[:, 0, :, start : start + WIDE].reshape(D, WIDE)
        )
    hidden = hidden_ref[...].reshape(total, D)
    gain = vectors_ref[2:3, :]
    _, stats, inverse = layer_stats(hidden, gain, vectors_ref[3:4, :])
    sums_ref[1:2, :] = sums_ref[1:2, :] + jnp.sum(grad_norm * stats, axis=0, keepdims=True)
    sums_ref[2:3, :] = sums_ref[2:3, :] + jnp.sum(grad_norm, axis=0, keepdims=True)
    mid = grad + norm_back(grad_norm, stats, inverse, gain)
    grad_mid_ref[...] = mid.reshape(count, rows, D)
    mid_low = mid.astype(jnp.bfloat16)
    grad_att_ref[...] = mid_low.reshape(count, rows, D)
    sums_ref[3:4, :] = sums_ref[3:4, :] + jnp.sum(
        mid_low.astype(jnp.float32), axis=0, keepdims=True
    )
    for number, piece in enumerate((own_a, own_b, other_a, other_b)):
        group = core if number < 2 else 1 - core
        unit = group * 24 + (number % 2) * 12
        piece[...] = (
            times_transposed(mid_low, w_out_ref[pl.ds(unit, 12)].reshape(width, D))
            .astype(jnp.bfloat16)
            .reshape(count, rows, width)
        )


def dense_backward(
    core, upstream, grad_conv, first, last, slope, hidden, vectors, weights
):
    windows, rows, _ = hidden.shape
    count = max(1, 256 // rows)
    width = H * VD // 4
    shapes = (
        [
            jax.ShapeDtypeStruct((windows, 2 * rows, D), jnp.float32),
            jax.ShapeDtypeStruct((windows, rows, D), jnp.float32),
            jax.ShapeDtypeStruct((windows, rows, D), jnp.bfloat16),
            jax.ShapeDtypeStruct((windows, rows, FF), jnp.bfloat16),
            jax.ShapeDtypeStruct((windows, rows, D), jnp.bfloat16),
        ]
        + [jax.ShapeDtypeStruct((windows, rows, width), jnp.bfloat16)] * 4
        + [jax.ShapeDtypeStruct((8, D), jnp.float32), jax.ShapeDtypeStruct((8, FF), jnp.float32)]
    )
    moving = (upstream, grad_conv, first, last, slope, hidden)
    lower, upper, w_up = weights
    return pl.pallas_call(
        functools.partial(dense_back_kernel, count=count, rows=rows),
        grid=(windows // count,),
        in_specs=[pl.BlockSpec(memory_space=pltpu.SMEM)]
        + [step_block(array, count) for array in moving]
        + [whole_block(vectors)]
        + [unit_rows(*OUT_ROWS), up_half(0), up_half(1), unit_rows(*DOWN_ROWS)],
        out_specs=[step_block(shape, count) for shape in shapes[:9]]
        + [whole_block(shape) for shape in shapes[9:]],
        out_shape=shapes,
        scratch_shapes=[pltpu.VMEM((D // LANES, 2 * rows, LANES), jnp.float32)],
        compiler_params=pltpu.CompilerParams(vmem_limit_bytes=62 * 2**20),
        cost_estimate=pl.CostEstimate(
            flops=(2 * windows * rows * D * (D + 2 * FF)) // 16,
            bytes_accessed=(2 * D * (D + 2 * FF) + 40 * windows * rows * D) // 16,
            transcendentals=0,
        ),
    )(core, *moving, vectors, lower, w_up, w_up, upper)


def weight_grad_kernel(left_ref, right_ref, *refs):
    out_ref = refs[-1]
    total = left_ref.shape[0] * left_ref.shape[1]
    left = left_ref[...].reshape(total, left_ref.shape[2])
    right = right_ref[...].reshape(total, D)
    out_ref[...] = (
        jnp.dot(left.T, right, preferred_element_type=jnp.float32)
        .astype(jnp.bfloat16)
        .reshape(out_ref.shape)
    )


def weight_grad(left, right, held, place):
    windows, rows, depth = left.shape
    halves = right.shape[2] // D
    step = D // 4
    count = step // UNIT // (2 // halves)
    first = place[0][0] * place[1][0] // count
    return pl.pallas_call(
        weight_grad_kernel,
        grid=(halves, depth // step),
        in_specs=[
            pl.BlockSpec((windows, rows, step), lambda h, m: (0, 0, m)),
            pl.BlockSpec((windows, rows, D), lambda h, m: (0, 0, h)),
            pl.BlockSpec(memory_space=pl.ANY),
        ],
        out_specs=pl.BlockSpec(
            (count, 2 // halves, UNIT, D), lambda h, m: (first + m, h, 0, 0)
        ),
        out_shape=jax.ShapeDtypeStruct(held.shape, held.dtype),
        input_output_aliases={2: 0},
        compiler_params=pltpu.CompilerParams(vmem_limit_bytes=48 * 2**20),
        cost_estimate=pl.CostEstimate(
            flops=(2 * windows * rows * depth * right.shape[2]) // 16,
            bytes_accessed=(2 * (windows * rows * (depth + right.shape[2]) + depth * right.shape[2])) // 16,
            transcendentals=0,
        ),
    )(left, right, held)


def ordered(own, other, is_first, axis):
    return jnp.concatenate(
        [jnp.where(is_first, own, other), jnp.where(is_first, other, own)], axis=axis
    )


class Places:
    def __init__(self, windows, local_rows):
        self.dp = lax.axis_size("dp")
        self.seq = lax.axis_size("seq")
        self.windows = windows
        self.rows = local_rows
        self.length = local_rows * self.seq
        self.group = self.seq // (2 * windows)
        self.heads = H // (2 * self.group)
        self.core = lax.axis_index("dp") % 2
        self.is_first = self.core == 0
        self.place = lax.axis_index("seq") % self.group
        self.part = self.rows // (2 * self.group)
        self.head_start = (self.core * self.group + self.place) * self.heads

    def swap(self, array):
        return lax.ppermute(array, "dp", [(i, i ^ 1) for i in range(self.dp)])

    def rows_to_windows(self, own):
        kept, sent = own
        return ordered(kept, self.swap(sent), self.is_first, 0)

    def halves(self, array, axis):
        size = array.shape[axis] // 2
        kept = lax.dynamic_slice_in_dim(array, self.core * size, size, axis)
        sent = lax.dynamic_slice_in_dim(array, (1 - self.core) * size, size, axis)
        return (kept, sent)

    def exchange(self, array):
        return lax.all_to_all(array, "seq", split_axis=0, concat_axis=0, tiled=True)

    def inputs_to_windows(self, inputs):
        both = self.rows_to_windows(self.halves(inputs, 1))
        return both.reshape(self.seq, self.part, inputs.shape[2])

    def gather_rows(self, array):
        features = array.shape[2]
        array = array[:, None]
        if self.group > 1:
            hops = [
                (i, i - i % self.group + (i + 1) % self.group) for i in range(self.seq)
            ]
            pieces = [array]
            for _ in range(self.group - 1):
                pieces.append(lax.ppermute(pieces[-1], "seq", hops))
            pieces = jnp.concatenate(pieces, axis=1)
            order = (self.place - jnp.arange(self.group)) % self.group
            array = jnp.take(pieces, order, axis=1)
        array = ordered(
            array[:, None], self.swap(array)[:, None], self.is_first, 1
        )
        return array.reshape(self.length, features)

    def sum_rows(self, partial):
        features = partial.shape[1]
        partial = partial.reshape(self.seq, 2, self.group * self.part, features)
        kept, sent = self.halves(partial, 1)
        total = kept[:, 0].astype(jnp.float32) + self.swap(
            sent[:, 0].astype(jnp.bfloat16)
        ).astype(jnp.float32)
        if self.group > 1:
            total = lax.psum_scatter(
                total.reshape(self.seq, self.group, self.part, features),
                "seq",
                scatter_dimension=1,
                axis_index_groups=[
                    list(range(i, i + self.group)) for i in range(0, self.seq, self.group)
                ],
                tiled=True,
            )
            total = total[:, 0]
        return total.astype(jnp.bfloat16)

    def sums_to_rows(self, array):
        features = array.shape[2]
        back = array.reshape(2 * self.windows, self.group * self.part, features)
        kept, sent = self.halves(back, 0)
        return ordered(kept, self.swap(sent), self.is_first, 1)

    def heads_to_rows(self, chunk):
        count = chunk.shape[1]
        back = self.exchange(chunk.reshape(self.seq, self.rows, count))
        kept, sent = self.halves(
            back.reshape(2 * self.windows, self.group, self.rows, count), 0
        )
        return (kept, self.swap(sent))

    def rows_to_heads(self, kept, sent):
        count = kept.shape[3]
        both = self.rows_to_windows((kept, sent))
        back = self.exchange(both.reshape(self.seq, self.rows, count))
        return back.reshape(self.length, count)


def gather_weights(params, sent):
    devices = lax.axis_size(("dp", "seq"))
    index = lax.axis_index(("dp", "seq"))
    dp, seq = lax.axis_size("dp"), lax.axis_size("seq")
    shard = params.shape[0]
    own_rows = ROWS // devices
    extra = shard - own_rows * D
    rest = extra * devices
    tail = params[shard - TAIL :].astype(jnp.bfloat16)
    before = lax.ppermute(tail, ("dp", "seq"), [(i, i + 1) for i in range(devices - 1)])
    joined = jnp.concatenate([before.astype(jnp.float32), params])
    piece = lax.dynamic_slice_in_dim(joined, TAIL - extra * index, own_rows * D)
    piece = piece.astype(jnp.bfloat16).reshape(own_rows, D)
    special = jnp.where(index == devices - 1, tail, jnp.zeros_like(tail))
    for axis, bit in axis_bits("dp"):
        special = special + partner(special, axis, bit)
    special = jnp.broadcast_to(special.reshape(1, TAIL // D, D), (seq, TAIL // D, D))
    special = lax.all_to_all(special, "seq", split_axis=0, concat_axis=0, tiled=True)[seq - 1]
    special, sent = lax.optimization_barrier((special, sent))
    ready = lax.all_to_all(sent, "seq", split_axis=0, concat_axis=0, tiled=True)
    special = special.astype(jnp.float32).reshape(-1)[TAIL - rest :]
    if own_rows % UNIT == 0:
        here = piece.reshape(own_rows // UNIT, UNIT, D)
        other = jnp.swapaxes(piece.reshape(own_rows // UNIT, 8, 2, D), 1, 2).reshape(here.shape)
        row = own_rows * index + UNIT * jnp.arange(own_rows // UNIT)
        inside = (row >= UP_ROWS[0]) & (row < UP_ROWS[0] + UP_ROWS[1])
        piece = jnp.where(inside[:, None, None], other, here).reshape(piece.shape)
    half = own_rows // 2
    if dp == 2 and half % 8 == 0:
        second = lax.axis_index("dp") == 1
        given = jnp.where(second, piece[:half], piece[half:])
        taken = partner(given, "dp", 0)
        low = jnp.where(second, taken, piece[:half])
        high = jnp.where(second, piece[half:], taken)
        lower = lax.all_gather(low, ("seq", "dp"), axis=0, tiled=True)
        high, lower, ready = lax.optimization_barrier((high, lower, ready))
        upper = lax.all_gather(high, ("seq", "dp"), axis=0, tiled=True)
    else:
        everything = lax.all_gather(piece, ("dp", "seq"), axis=0, tiled=True)
        lower, upper = (everything[: ROWS // 2], everything[ROWS // 2 :])
    if own_rows % UNIT == 0:
        w_up = up_units(lower.reshape(-1, UNIT, D), upper.reshape(-1, UNIT, D))
    else:
        w_up = jnp.concatenate([lower[UP_ROWS[0] :], upper[: UP_ROWS[0] + UP_ROWS[1] - ROWS // 2]])
        w_up = jnp.swapaxes(w_up.reshape(96, UNIT, 2, D), 1, 2)
    views = [array.reshape(-1, 2, UNIT, D) for array in (lower, upper)]
    return (lower, (*views, w_up), special, ready)


def axis_bits(axis):
    return [(axis, bit) for bit in range(lax.axis_size(axis).bit_length() - 2, -1, -1)]


def partner(array, axis, bit):
    pairs = [(i, i ^ (1 << bit)) for i in range(lax.axis_size(axis))]
    return lax.ppermute(array, axis, pairs)


def turned(number):
    along = axis_bits("seq")[::-1]
    return (along, along[1:2] + along[:1] + along[2:], along[2:] + along[:2])[number % 3]


def halves_apart(rows, first, outer, inner):
    units = rows.shape[0] // (2 * UNIT)
    here = rows.reshape(units, 2 * UNIT, D)
    other = jnp.swapaxes(rows.reshape(units, outer, inner, D), 1, 2).reshape(here.shape)
    inside = first + 2 * UNIT * jnp.arange(units) < 2 * D
    return jnp.where(inside[:, None, None], other, here).reshape(rows.shape)


class Sums:
    def __init__(self, rows):
        self.bits = axis_bits("dp") + axis_bits("seq")
        self.states = [rows.reshape((2,) * len(self.bits) + (-1, D))]
        self.left = [list(self.bits)]
        self.orders = [axis_bits("dp")[::-1]]
        self.steps = len(self.bits)

    def send(self):
        self.steps -= 1
        if not self.orders[0]:
            band = D // 3
            self.states = [self.states[0][..., k * band : (k + 1) * band] for k in range(3)]
            self.left = [list(self.left[0]) for _ in range(3)]
            self.orders = [turned(k) for k in range(3)]
        for k, state in enumerate(self.states):
            axis, bit = self.orders[k][0]
            self.orders[k] = self.orders[k][1:]
            dim = self.left[k].index((axis, bit))
            self.left[k].pop(dim)
            mine = (lax.axis_index(axis) >> bit) & 1
            sent = lax.dynamic_index_in_dim(state, 1 - mine, dim, False)
            kept = lax.dynamic_index_in_dim(state, mine, dim, False)
            self.states[k] = (kept, sent, axis, bit)

    def before(self, array):
        sent, array = lax.optimization_barrier(([state[1] for state in self.states], array))
        self.states = [
            (kept, there, axis, bit)
            for (kept, _, axis, bit), there in zip(self.states, sent, strict=True)
        ]
        return array

    def move(self):
        self.states = [
            (kept, partner(sent, axis, bit), axis, bit) for kept, sent, axis, bit in self.states
        ]

    def add(self):
        self.states = [
            (kept.astype(jnp.float32) + other.astype(jnp.float32)).astype(jnp.bfloat16)
            for kept, other, _, _ in self.states
        ]

    def finish(self, left=0):
        while self.steps > left:
            self.send()
            self.move()
            self.add()
        return jnp.concatenate(self.states, axis=1) if left == 0 else None


PARTS = ((4096, 6144), (2560, 1536), (10240, 1536))
QKV_PARTS = ((0, 2560),)


def moves(parts, more):
    devices = lax.axis_size(("dp", "seq"))
    own_rows = ROWS // devices
    count = sum(rows for _, rows in parts) // devices
    found, start = ([], 0)
    for first, rows in parts:
        for t in range(devices):
            low, high = (max(count * t, start), min(count * (t + 1), start + rows))
            if low >= high:
                continue
            row = first + low - start
            for i in range(devices):
                if row < own_rows * (i + 1) + more and row + high - low > own_rows * i:
                    found.append((i, t, high - low, row - own_rows * i, low - count * t))
        start += rows
    rounds = []
    for move in found:
        for held in rounds:
            if all(move[0] != other[0] and move[1] != other[1] for other in held):
                held.append(move)
                break
        else:
            rounds.append([move])
    return (rounds, count)


def per_device(values):
    index = lax.axis_index(("dp", "seq"))
    result = jnp.zeros((), jnp.int32)
    for place, value in values:
        if value != 0:
            result = jnp.where(index == place, value, result)
    return result


def add_rows(buffer, moved, place, count):
    row = lax.broadcasted_iota(jnp.int32, moved.shape, 0)
    moved = jnp.where(row < count, moved, jnp.zeros_like(moved))
    there = lax.dynamic_slice_in_dim(buffer, place, moved.shape[0], 0)
    return lax.dynamic_update_slice_in_dim(buffer, there + moved, place, 0)


def to_owners(buffer, share, parts):
    rounds, most = moves(parts, TAIL // D)
    share = jnp.pad(share, ((0, most), (0, 0)))
    for held in rounds:
        start = per_device([(t, offset) for _, t, _, _, offset in held])
        moved = lax.ppermute(
            lax.dynamic_slice_in_dim(share, start, most, 0),
            ("dp", "seq"),
            [(t, i) for i, t, _, _, _ in held],
        )
        place = per_device([(i, MARGIN + low) for i, _, _, low, _ in held])
        count = per_device([(i, rows) for i, _, rows, _, _ in held])
        buffer = add_rows(buffer, moved, place, count)
    return buffer


def own_entries(buffer, special):
    devices = lax.axis_size(("dp", "seq"))
    index = lax.axis_index(("dp", "seq"))
    own_rows = ROWS // devices
    rest = special.shape[0]
    extra = rest // devices
    held = buffer[MARGIN : MARGIN + own_rows + TAIL // D].astype(jnp.float32)
    after = held[own_rows:].reshape(-1)
    after = jnp.where(index == devices - 1, jnp.pad(special, (0, TAIL - rest)), after)
    joined = jnp.concatenate([held[:own_rows].reshape(-1), after])
    return lax.dynamic_slice_in_dim(joined, extra * index, own_rows * D + extra)


def body(block_input, skip_input, species, cotangent, params, first_moment, second_moment):
    windows, local_rows, _ = block_input.shape
    at = Places(windows, local_rows)
    length = at.length
    own = at.heads
    scale = 1.0 / math.sqrt(KD)
    f32, bf16 = jnp.float32, jnp.bfloat16

    early, weights, special, moved = gather_weights(params, at.inputs_to_windows(block_input))
    pos_low = special[: F * H].reshape(F, H)
    up_bias = special[F * H : F * H + FF]
    vectors = special[F * H + FF :].reshape(12, D)

    def columns(matrix, width):
        return lax.dynamic_slice_in_dim(matrix, at.head_start * width, own * width, 1)

    w_own = jnp.concatenate(
        [
            columns(early[:512].reshape(D, H * KD), KD) * jnp.asarray(scale, bf16),
            columns(early[512:1024].reshape(D, H * KD), KD),
            columns(early[1024:2560].reshape(D, H * VD), VD),
        ],
        axis=1,
    )
    pos_basis = position_basis(length)
    own_pos = lax.dynamic_slice_in_dim(pos_low, at.head_start, own, 1)
    tables = jnp.dot(own_pos.T, pos_basis.T, precision=highest)
    tables = jnp.roll(jnp.pad(tables, ((0, 0), (0, 1))), 1 - BLOCK, axis=1)
    tables = jnp.broadcast_to(tables[:, None, :], (own, 8, 2 * length))

    low_part, _, _ = layer_stats(moved.astype(f32), vectors[0], vectors[1])
    low_all = at.gather_rows(low_part.astype(bf16))
    projected = jnp.einsum("rd,dk->kr", low_all, w_own, preferred_element_type=f32).astype(bf16)
    queries, keys, values = (
        projected[: own * KD],
        projected[own * KD : 2 * own * KD],
        projected[2 * own * KD :],
    )

    operands, saved, pieces = ([], [], ([], []))
    for pair in range(own // PAIR):
        narrow = slice(pair * PAIR * KD, (pair + 1) * PAIR * KD)
        wide = slice(pair * PAIR * VD, (pair + 1) * PAIR * VD)
        given = (
            tables[pair * PAIR : (pair + 1) * PAIR],
            queries[narrow],
            keys[narrow],
            values[wide],
        )
        result, log_total = attention_forward(*given)
        operands.append(given)
        saved.append((result, log_total))
        for held, part in zip(pieces, at.heads_to_rows(result), strict=True):
            held.append(part)
    pairs = own // PAIR
    pieces = [
        held[pair][:, place] for held in pieces for place in range(at.group) for pair in range(pairs)
    ]

    core = jnp.asarray(at.core, jnp.int32).reshape(1)
    heads, hidden_one, low_two, activated, slope, hidden_two = dense_forward(
        core, block_input, pieces, vectors, up_bias[None], weights
    )
    ends = [
        (hidden_two[:, row : row + 1] + skip_input[:, up : up + 1].astype(f32)).astype(bf16)
        for row, up in ((0, 0), (local_rows - 1, 2 * local_rows - 1))
    ]
    first, last = edge_rows(ends)
    is_mouse = (species == 1).astype(f32)[:, None]
    species_gain = (1.0 - is_mouse) * vectors[10] + is_mouse * vectors[11]
    block_out, grad_conv, dense_grads, gain_rows, point_sums = point_layer(
        hidden_two,
        skip_input,
        cotangent,
        first,
        last,
        species_gain[:, None, :],
        vectors,
        weights,
    )
    gain_rows = gain_rows[:, 0]
    grad_human = jnp.sum((1.0 - is_mouse) * gain_rows, axis=0)
    grad_mouse = jnp.sum(is_mouse * gain_rows, axis=0)
    first, last = edge_rows([grad_conv[:, :1], grad_conv[:, 2 * local_rows - 1 :]])
    (
        skip_grad,
        grad_mid,
        grad_down_low,
        grad_before,
        grad_attn_low,
        *grad_pieces,
        dense_sums,
        up_sums,
    ) = dense_backward(
        core,
        cotangent,
        grad_conv,
        first,
        last,
        slope,
        hidden_one,
        vectors,
        weights,
    )
    grad_pieces = [
        jnp.stack(
            [
                grad_pieces[2 * group + place * pairs + pair]
                for place in range(at.group)
            ],
            axis=1,
        )
        for group in range(2)
        for pair in range(pairs)
    ]

    middle = jnp.concatenate(
        [
            up_sums[0],
            dense_sums[1],
            dense_sums[2],
            dense_sums[3],
            dense_sums[0],
            point_sums[:4].reshape(-1),
            grad_human,
            grad_mouse,
        ]
    )
    devices = lax.axis_size(("dp", "seq"))
    chunks = [at.rows_to_heads(grad_pieces[pair], grad_pieces[pairs + pair]) for pair in range(pairs)]
    dense_grads = weight_grad(activated, grad_down_low, dense_grads, DOWN)
    dense_grads = weight_grad(low_two, grad_before, dense_grads, LEFT)
    dense_grads = weight_grad(heads, grad_attn_low, dense_grads, OUT).reshape(-1, D)
    even = dense_grads.shape[0] // devices % (2 * UNIT) == 0
    if not even:
        dense_grads = halves_apart(dense_grads, 0, 2, UNIT)
    dense_grads, chunks[0] = lax.optimization_barrier((dense_grads, chunks[0]))
    dense = lax.psum_scatter(dense_grads, ("dp", "seq"), scatter_dimension=0, tiled=True)

    dq, dk, dv, dt = ([], [], [], [])
    for pair in range(pairs):
        result, log_total = saved[pair]
        grads = attention_backward(*operands[pair], result, chunks[pair], log_total)
        for piece, held in zip(grads, (dq, dk, dv, dt), strict=True):
            held.append(piece)
    grad_own = jnp.concatenate(dq + dk + dv, axis=1)
    partial = jnp.einsum("rk,dk->rd", grad_own, w_own, preferred_element_type=f32).astype(bf16)
    partial, grad_own = lax.optimization_barrier((partial, grad_own))
    back = at.exchange(at.sum_rows(partial))
    grad_w_own = jnp.einsum("rd,rk->dk", low_all, grad_own, preferred_element_type=f32)
    grad_w_query = grad_w_own[:, : own * KD] * scale
    grad_w_key = grad_w_own[:, own * KD : 2 * own * KD]
    grad_w_value = grad_w_own[:, 2 * own * KD :]

    def all_columns(matrix, width):
        whole = jnp.zeros((D, H * width), bf16)
        return lax.dynamic_update_slice_in_dim(
            whole, matrix.astype(bf16), at.head_start * width, 1
        ).reshape(-1, D)

    first_rows = jnp.concatenate(
        [
            all_columns(grad_w_query, KD),
            all_columns(grad_w_key, KD),
            all_columns(grad_w_value, VD),
        ],
        axis=0,
    )
    first_sums = Sums(first_rows)
    first_sums.finish(2)
    first_sums.states, back = lax.optimization_barrier((first_sums.states, back))
    grad_norm_one = at.sums_to_rows(back).astype(f32)
    _, stats_one, inverse_one = layer_stats(block_input.astype(f32), vectors[0], vectors[1])
    input_grad = grad_mid + norm_back(grad_norm_one, stats_one, inverse_one, vectors[0])
    grad_gain_one = jnp.sum(grad_norm_one * stats_one, axis=(0, 1))
    grad_bias_one = jnp.sum(grad_norm_one, axis=(0, 1))
    grad_tables = jnp.roll(jnp.concatenate(dt, axis=0), BLOCK - 1, axis=1)[:, : 2 * length - 1]
    grad_pos = jnp.dot(pos_basis.T, grad_tables.T, precision=highest)
    grad_pos = lax.dynamic_update_slice_in_dim(
        jnp.zeros((F, H), f32), grad_pos, at.head_start, 1
    )
    late = jnp.concatenate([grad_pos.reshape(-1), grad_gain_one, grad_bias_one])
    summed = jnp.concatenate([late, middle])
    for axis, bit in axis_bits("dp") + axis_bits("seq"):
        summed = summed + partner(summed, axis, bit)
    late, middle = (summed[: late.shape[0]], summed[late.shape[0] :])
    special_grads = jnp.concatenate(
        [late[: F * H], middle[:FF], late[F * H :], middle[FF:]]
    )
    share = dense
    if even:
        share = halves_apart(share, lax.axis_index(("dp", "seq")) * share.shape[0], 2, UNIT)
    buffer = jnp.zeros((ROWS // devices + TAIL // D + 2 * MARGIN, D), bf16)
    buffer = to_owners(buffer, share, PARTS)
    buffer = to_owners(buffer, first_sums.finish(), QKV_PARTS)
    reduced = own_entries(buffer, special_grads)
    shard_len = params.shape[0]
    position = lax.axis_index(("dp", "seq")) * shard_len + jnp.arange(shard_len)
    param_new, first_new, second_new = adam_update(
        params, first_moment, second_moment, reduced, position
    )
    return (
        block_out,
        input_grad,
        skip_grad,
        param_new,
        first_new,
        second_new,
        param_new.astype(bf16),
    )


def solution(mesh):
    return jax.shard_map(
        body,
        mesh=mesh,
        in_specs=(
            P("dp", "seq", None),
            P("dp", "seq", None),
            P("dp"),
            P("dp", "seq", None),
            P(("dp", "seq")),
            P(("dp", "seq")),
            P(("dp", "seq")),
        ),
        out_specs=(
            P("dp", "seq", None),
            P("dp", "seq", None),
            P("dp", "seq", None),
            P(("dp", "seq")),
            P(("dp", "seq")),
            P(("dp", "seq")),
            P(("dp", "seq")),
        ),
        check_vma=False,
    )
```

time: 1410 us -> 1130 us (0.80)
  matrix products: 289 us -> 43 us
  Pallas kernels: 131 us -> 307 us
  blocking collectives: 0 us -> 140 us
  local copies, waits for them, and re-layouts: 234 us -> 106 us
  waiting for transfers between devices: 436 us -> 312 us
  other arithmetic: 135 us -> 84.2 us
  starting transfers between devices: 135 us -> 108 us
  between operations: 33 us -> 15.8 us
    dot_general x21 -> x3, matrix products: 276 us -> 28.5 us  [the longest x1 10.3 us: body(): jnp.einsum('rd,rk->dk', low_all, grad_own, preferred_element_type=f32)]
    pallas_call x0 -> x7, Pallas kernels: none -> 181 us  [the longest x1 47.7 us: dense_backward(): pl.pallas_call(functools.partial(dense_back_kernel, count=count, rows=row...]
    all_to_all x10 -> x5, waiting for transfers between devices: 262 us -> 117 us  [exchange(): return lax.all_to_all(array, 'seq', split_axis=0, concat_axis=0, tiled=True)]
    all_to_all x0 -> x1, blocking collectives: none -> 140 us  [gather_weights(): ready = lax.all_to_all(sent, 'seq', split_axis=0, concat_axis=0, tiled=True)]
    ppermute x25 -> x34, waiting for transfers between devices: 55.2 us -> 155 us  [the longest x20 105 us: partner(): return lax.ppermute(array, axis, pairs)]
    reduce_scatter x2 -> x1, waiting for transfers between devices: 93.7 us -> 0.02 us  [body(): lax.psum_scatter(dense_grads, ('dp', 'seq'), scatter_dimension=0, tiled=T...]
    reshape x9 -> x4, local copies, waits for them, and re-layouts: 75.4 us -> 10.6 us  [the longest x1 3.72 us: body(): early[:512].reshape(D, H * KD)]
    all_to_all x10 -> x5, starting transfers between devices: 84.3 us -> 34.8 us  [exchange(): return lax.all_to_all(array, 'seq', split_axis=0, concat_axis=0, tiled=True)]
  transfers between devices with their start and end apart: 52 -> 52, of which waited for: 25 -> 23; matrix products, arithmetic and copies ran while one was open for 17% -> 17% of each run, Pallas kernels for 9% -> 15%
where the time goes in v1:
time: 1130 us; the launch traced here: 1120 us
  waiting for transfers between devices  312 us (28%)
  Pallas kernels  307 us (27%)
  blocking collectives  140 us (12%)
  starting transfers between devices  108 us (10%)
  local copies, waits for them, and re-layouts  106 us (9%)
  other arithmetic  84.2 us (7%)
  matrix products  43 us (4%)
  between operations  15.8 us (1%)
    all_to_all x1, blocking collectives, gather_weights(): ready = lax.all_to_all(sent, 'seq', split_axis=0, concat_axis=0, tiled=True)  140 us
    all_to_all x5, waiting for transfers between devices, exchange(): return lax.all_to_all(array, 'seq', split_axis=0, concat_axis=0, tiled=True)  117 us
    ppermute x20, waiting for transfers between devices, partner(): return lax.ppermute(array, axis, pairs)  105 us
    pallas_call x2, Pallas kernels, attention_backward(): pl.pallas_call(functools.partial(backward_kernel, blocks=blocks), grid=(b...  81.4 us
    pallas_call x1, Pallas kernels, dense_backward(): pl.pallas_call(functools.partial(dense_back_kernel, count=count, rows=row...  47.7 us
    pallas_call x2, Pallas kernels, attention_forward(): pl.pallas_call(functools.partial(forward_kernel, blocks=blocks), grid=(bl...  44.8 us
    pallas_call x1, Pallas kernels, point_layer(): pl.pallas_call(functools.partial(point_kernel, rows=rows), grid=(windows,...  43.7 us
    ppermute x10, waiting for transfers between devices, to_owners(): lax.ppermute(lax.dynamic_slice_in_dim(share, start, most, 0), ('dp', 'seq...  43.7 us
  transfers between devices with their start and end apart: 52, of which 23 were waited for; matrix products, arithmetic and copies ran while one was open for 17% of the time, Pallas kernels for 15%

profile of v1, /device:TPU:16, one launch (start us, length us, event | category | flops | bytes accessed | tf_op | source)
XLA Modules:
  0.0 1116.7 jit_solution(17712808598434480816)
XLA Ops:
  33.3 30.2 %all-to-all-done = bf16[16,16,1536]{2,1,0:T(8,128)(2,1)} async-done(((bf16[16,16,1536]{2,1,0:T(8,128)(2,1)}), bf16[16,16,1536]{2,1,0:T(8,128)(2,1)}, u32[]{:S(2)}, u32[]{:S(2)}) %all-to-all-start) | async-done | bytes 786464 | tf_op jit(solution)/shard_map/all_to_all | solution.py:947
  66.6 140.3 %all_to_all.35 = bf16[16,64,1536]{2,1,0:T(8,128)(2,1)S(1)} all-to-all(bf16[16,64,1536]{2,1,0:T(8,128)(2,1)S(1)} %pad_maximum_fusion.6), channel_id=1, replica_groups=mesh['dp'=2,'seq'=16] {'seq'}, dimensions={0} | all-to-all | bytes 6291456 | tf_op jit(solution)/shard_map/all_to_all | solution.py:949
  247.7 8.9 convolution_convert_fusion.1
  257.8 22.4 %shard_map.127 = (bf16[2048,384]{1,0:T(8,128)(2,1)}, f32[2,2048]{1,0:T(2,128)S(1)}) custom-call(f32[2,8,4096]{2,1,0:T(8,128)S(1)} %broadcast_in_dim.103.table_ref, bf16[128,2048]{1,0:T(8,128)(2,1)S(1)} %get-tuple-element.132.q_ref, bf16[128,2048]{1,0:T(8,128)(2,1)S(1)} %get-tuple-element.131.k_ref, bf16[384,2048]{1,0:T(8,128)(2,1)S(1)} %get-tuple-element.129.v_ref), custom_call_target="tpu_custom_call" | custom-call | flops 536870912 | bytes 524288 | tf_op jit(solution)/shard_map/pallas_call | solution.py:190
  282.0 11.4 %all-to-all-start.3 = ((bf16[16,128,384]{2,1,0:T(8,128)(2,1)}), bf16[16,128,384]{2,1,0:T(8,128)(2,1)}, u32[]{:S(2)}, u32[]{:S(2)}) async-start(bf16[16,128,384]{2,1,0:T(8,128)(2,1)} %bitcast.10), calls=%async_computation.3 | async-start | bytes 3145728 | tf_op jit(solution)/shard_map/all_to_all | solution.py:865
  293.4 22.4 %shard_map.126 = (bf16[2048,384]{1,0:T(8,128)(2,1)}, f32[2,2048]{1,0:T(2,128)S(1)}) custom-call(f32[2,8,4096]{2,1,0:T(8,128)S(1)} %broadcast_in_dim.97.table_ref, bf16[128,2048]{1,0:T(8,128)(2,1)S(1)} %get-tuple-element.134.q_ref, bf16[128,2048]{1,0:T(8,128)(2,1)S(1)} %get-tuple-element.133.k_ref, bf16[384,2048]{1,0:T(8,128)(2,1)S(1)} %get-tuple-element.130.v_ref), custom_call_target="tpu_custom_call" | custom-call | flops 536870912 | bytes 524288 | tf_op jit(solution)/shard_map/pallas_call | solution.py:190
  315.8 47.1 %all-to-all-done.3 = bf16[16,128,384]{2,1,0:T(8,128)(2,1)} async-done(((bf16[16,128,384]{2,1,0:T(8,128)(2,1)}), bf16[16,128,384]{2,1,0:T(8,128)(2,1)}, u32[]{:S(2)}, u32[]{:S(2)}) %all-to-all-start.3) | async-done | bytes 1572896 | tf_op jit(solution)/shard_map/all_to_all | solution.py:865
  371.8 33.3 %all-to-all-done.2 = bf16[16,128,384]{2,1,0:T(8,128)(2,1)S(1)} async-done(((bf16[16,128,384]{2,1,0:T(8,128)(2,1)}), bf16[16,128,384]{2,1,0:T(8,128)(2,1)S(1)}, u32[]{:S(2)}, u32[]{:S(2)}) %all-to-all-start.2) | async-done | bytes 1572896 | tf_op jit(solution)/shard_map/all_to_all | solution.py:865
  420.4 42.8 %shard_map.129 = (bf16[8,128,1536]{2,1,0:T(8,128)(2,1)}, f32[8,128,1536]{2,1,0:T(8,128)}, bf16[8,128,1536]{2,1,0:T(8,128)(2,1)}, bf16[8,128,3072]{2,1,0:T(8,128)...) custom-call(s32[1]{0:T(128)} %bitcast.core_ref, bf16[8,128,1536]{2,1,0:T(8,128)(2,1)} %inputs_ref.1, ...), custom_call_target="tpu_custom_call" | custom-call | flops 1509949440 | bytes 4030464 | tf_op jit(solution)/shard_map/pallas_call | solution.py:508
  474.6 43.7 %shard_map.130 = (bf16[8,256,1536]{2,1,0:T(8,128)(2,1)}, bf16[8,256,1536]{2,1,0:T(8,128)(2,1)}, bf16[288,2,16,1536]{3,2,1,0:T(8,128)(2,1)}, f32[8,1,1536]{2,1,0:T(1,128)}, f32[8,1536]{1,0:T(8,128)}) custom-call(f32[8,128,1536]{2,1,0:T(8,128)} %get-tuple-element.61.after_ref, bf16[8,256,1536]{2,1,0:T(8,128)(2,1)} %skip_ref.1, ...), custom_call_target="tpu_custom_call" | custom-call | flops 1811939328 | bytes 2555904 | tf_op jit(solution)/shard_map/pallas_call | solution.py:617
  533.9 47.7 %shard_map.131 = (f32[8,256,1536]{2,1,0:T(8,128)}, f32[8,128,1536]{2,1,0:T(8,128)}, bf16[8,128,1536]{2,1,0:T(8,128)(2,1)}, bf16[8,128,3072]{2,1,0:T(8,128)(2,1)}...) custom-call(s32[1]{0:T(128)} %bitcast.core_ref, ...), custom_call_target="tpu_custom_call" | custom-call | flops 1509949440 | bytes 5406720 | tf_op jit(solution)/shard_map/pallas_call | solution.py:770
  591.3 14.2 %shard_map.132.refs_0_ = bf16[288,2,16,1536]{3,2,1,0:T(8,128)(2,1)} custom-call(bf16[8,128,3072]{2,1,0:T(8,128)(2,1)} %get-tuple-element.71.left_ref, bf16[8,128,1536]{2,1,0:T(8,128)(2,1)S(1)} %copy-done.8, bf16[288,2,16,1536]{3,2,1,0:T(8,128)(2,1)} %get-tuple-element.73.refs_0_), custom_call_target="tpu_custom_call", output_to_operand_aliasing={{}: (2, {})} | custom-call | flops 603979776 | bytes 1179648 | tf_op jit(solution)/shard_map/pallas_call | solution.py:808
  605.5 15.9 %shard_map.133.refs_0_ = bf16[288,2,16,1536]{3,2,1,0:T(8,128)(2,1)} custom-call(bf16[8,128,1536]{2,1,0:T(8,128)(2,1)S(1)} %copy-done.7, bf16[8,128,3072]{2,1,0:T(8,128)(2,1)} %get-tuple-element.70.right_ref, bf16[288,2,16,1536]{3,2,1,0:T(8,128)(2,1)} %shard_map.132.refs_0_), custom_call_target="tpu_custom_call", output_to_operand_aliasing={{}: (2, {})} | custom-call | flops 603979776 | bytes 1179648 | tf_op jit(solution)/shard_map/pallas_call | solution.py:808
  621.4 8.9 shard_map.134
  642.5 36.7 %all-to-all-done.5 = bf16[16,128,384]{2,1,0:T(8,128)(2,1)S(1)} async-done(((bf16[16,128,384]{2,1,0:T(8,128)(2,1)}), bf16[16,128,384]{2,1,0:T(8,128)(2,1)S(1)}, u32[]{:S(2)}, u32[]{:S(2)}) %all-to-all-start.5) | async-done | bytes 1572896 | tf_op jit(solution)/shard_map/all_to_all | solution.py:865
  680.4 40.7 %shard_map.136 = (bf16[2048,128]{1,0:T(8,128)(2,1)}, bf16[2048,128]{1,0:T(8,128)(2,1)}, bf16[2048,384]{1,0:T(8,128)(2,1)}, f32[2,4096]{1,0:T(2,128)}) custom-call(f32[2,8,4096]{2,1,0:T(8,128)} %copy-done.10, bf16[128,2048]{1,0:T(8,128)(2,1)} %copy-done.6, bf16[128,2048]{1,0:T(8,128)(2,1)} %copy-done.5, bf16[384,2048]{1,0:T(8,128)(2,1)} %copy-done.2, ...), custom_call_target="tpu_custom_call" | custom-call | flops 1342177280 | bytes 1048576 | tf_op jit(solution)/shard_map/pallas_call | solution.py:312
  721.1 40.6 %shard_map.135 = (bf16[2048,128]{1,0:T(8,128)(2,1)}, bf16[2048,128]{1,0:T(8,128)(2,1)}, bf16[2048,384]{1,0:T(8,128)(2,1)}, f32[2,4096]{1,0:T(2,128)}) custom-call(f32[2,8,4096]{2,1,0:T(8,128)} %copy-done.11, bf16[128,2048]{1,0:T(8,128)(2,1)} %copy-done.4, bf16[128,2048]{1,0:T(8,128)(2,1)} %copy-done.3, bf16[384,2048]{1,0:T(8,128)(2,1)} %copy-done.1, ...), custom_call_target="tpu_custom_call" | custom-call | flops 1342177280 | bytes 1048576 | tf_op jit(solution)/shard_map/pallas_call | solution.py:312
  766.8 9.2 convolution_convert_fusion
  779.7 10.3 fusion.74
  836.8 9.5 fusion.20
  864.9 53.8 %collective-permute-done.18 = bf16[2,2,2,80,512]{4,3,2,1,0:T(8,128)(2,1)S(1)} collective-permute-done((bf16[2,2,2,80,512]{4,3,2,1,0:T(8,128)(2,1)S(1)}, bf16[2,2,2,80,512]{4,3,2,1,0:T(8,128)(2,1)S(1)}, u32[]{:S(2)}, u32[]{:S(2)}) %collective-permute-start.18) | collective-permute-done | bytes 655392 | tf_op jit(solution)/shard_map/ppermute | solution.py:985
  920.3 21.5 %collective-permute-done.19 = bf16[2,2,80,512]{3,2,1,0:T(8,128)(2,1)S(1)} collective-permute-done((bf16[2,2,80,512]{3,2,1,0:T(8,128)(2,1)S(1)}, bf16[2,2,80,512]{3,2,1,0:T(8,128)(2,1)S(1)}, u32[]{:S(2)}, u32[]{:S(2)}) %collective-permute-start.19) | collective-permute-done | bytes 327712 | tf_op jit(solution)/shard_map/ppermute | solution.py:985
  1022.2 43.7 %collective-permute-done.22 = bf16[288,1536]{1,0:T(8,128)(2,1)S(1)} collective-permute-done((bf16[288,1536]{1,0:T(8,128)(2,1)S(1)}, bf16[288,1536]{1,0:T(8,128)(2,1)S(1)}, u32[]{:S(2)}, u32[]{:S(2)}) %collective-permute-start.22) | collective-permute-done | bytes 884768 | tf_op jit(solution)/shard_map/ppermute | solution.py:1104
  1100.8 9.1 fusion.66
  (431 shorter events, 336.4 us)
Async XLA Ops:
  7.2 200.7 %all-gather.3.cloned.1.call-start = ((), (), s32[]{:S(2)}) async-start(), calls=%async_computation.8 | async-start | bytes 18653184 | tf_op jit(solution)/shard_map/all_gather | solution.py:964
  26.3 37.2 %all-to-all-start = ((bf16[16,16,1536]{2,1,0:T(8,128)(2,1)}), bf16[16,16,1536]{2,1,0:T(8,128)(2,1)}, u32[]{:S(2)}, u32[]{:S(2)}) async-start(bf16[16,16,1536]{2,1,0:T(8,128)(2,1)} %broadcast_in_dim.96), calls=%async_computation | async-start | bytes 1572864 | tf_op jit(solution)/shard_map/all_to_all | solution.py:947
  31.9 375.9 %all-gather.5.cloned.1.call-start = ((), (), s32[]{:S(2)}) async-start(), calls=%async_computation.9 | async-start | bytes 18653184 | tf_op jit(solution)/shard_map/all_gather | solution.py:966
  33.2 31.1 %collective-permute-start.1 = (bf16[8,64,1536]{2,1,0:T(8,128)(2,1)}, bf16[8,64,1536]{2,1,0:T(8,128)(2,1)}, u32[]{:S(2)}, u32[]{:S(2)}) collective-permute-start(bf16[8,64,1536]{2,1,0:T(8,128)(2,1)} %constant_dynamic-slice_fusion.9), channel_id=1, source_target_pairs={{0,16},{16,0},{1,17},{17,1},{2,18},{18,2},{3,19},{19,3},{4,20},{20... | collective-permute-start | bytes 4718600 | tf_op jit(solution)/shard_map/ppermute | solution.py:852
  212.0 29.6 %collective-permute-start.4 = (bf16[16,1,64,1536]{3,2,0,1:T(8,128)(2,1)}, bf16[16,1,64,1536]{3,2,0,1:T(8,128)(2,1)}, u32[]{:S(2)}, u32[]{:S(2)}) collective-permute-start(bf16[16,1,64,1536]{3,2,0,1:T(8,128)(2,1)} %fusion.50), channel_id=1, source_target_pairs={{0,16},{16,0},{1,17},{17,1},{2,18},{18,2},{3,19},{19,3},{4,20},{20... | collective-permute-start | bytes 9437192 | tf_op jit(solution)/shard_map/ppermute | solution.py:852
  282.0 81.0 %all-to-all-start.3 = ((bf16[16,128,384]{2,1,0:T(8,128)(2,1)}), bf16[16,128,384]{2,1,0:T(8,128)(2,1)}, u32[]{:S(2)}, u32[]{:S(2)}) async-start(bf16[16,128,384]{2,1,0:T(8,128)(2,1)} %bitcast.10), calls=%async_computation.3 | async-start | bytes 3145728 | tf_op jit(solution)/shard_map/all_to_all | solution.py:865
  363.0 42.2 %all-to-all-start.2 = ((bf16[16,128,384]{2,1,0:T(8,128)(2,1)}), bf16[16,128,384]{2,1,0:T(8,128)(2,1)S(1)}, u32[]{:S(2)}, u32[]{:S(2)}) async-start(bf16[16,128,384]{2,1,0:T(8,128)(2,1)} %bitcast.9), calls=%async_computation.2 | async-start | bytes 3145728 | tf_op jit(solution)/shard_map/all_to_all | solution.py:865
  371.8 47.4 %collective-permute-start.6 = (bf16[8,1,128,384]{3,2,0,1:T(8,128)(2,1)}, bf16[8,1,128,384]{3,2,0,1:T(8,128)(2,1)S(1)}, u32[]{:S(2)}, u32[]{:S(2)}) collective-permute-start(bf16[8,1,128,384]{3,2,0,1:T(8,128)(2,1)} %get-tuple-element.148), channel_id=1, source_target_pairs={{0,16},{16,0},{1,17},{17,1},{2,18},{18,2},{3,19},{19,3},{4,20},{20... | collective-permute-start | bytes 2359304 | tf_op jit(solution)/shard_map/ppermute | solution.py:852
  586.8 43.5 %all-to-all-start.4 = ((bf16[16,128,384]{2,1,0:T(8,128)(2,1)}), bf16[16,128,384]{2,1,0:T(8,128)(2,1)}, u32[]{:S(2)}, u32[]{:S(2)}) async-start(bf16[16,128,384]{2,1,0:T(8,128)(2,1)} %maximum_bitcast_fusion), calls=%async_computation.4 | async-start | bytes 3145728 | tf_op jit(solution)/shard_map/all_to_all | solution.py:865
  591.3 401.5 %reduce-scatter.2.cloned.1.call-start = ((), (), s32[]{:S(2)}) async-start(), calls=%async_computation.10 | async-start | bytes 29196288 | tf_op jit(solution)/shard_map/reduce_scatter | solution.py:1265
  635.2 44.0 %all-to-all-start.5 = ((bf16[16,128,384]{2,1,0:T(8,128)(2,1)}), bf16[16,128,384]{2,1,0:T(8,128)(2,1)S(1)}, u32[]{:S(2)}, u32[]{:S(2)}) async-start(bf16[16,128,384]{2,1,0:T(8,128)(2,1)} %maximum_bitcast_fusion.1), calls=%async_computation.5 | async-start | bytes 3145728 | tf_op jit(solution)/shard_map/all_to_all | solution.py:865
  779.7 23.8 %collective-permute-start.20 = (bf16[16,64,1536]{2,1,0:T(8,128)(2,1)}, bf16[16,64,1536]{2,1,0:T(8,128)(2,1)}, u32[]{:S(2)}, u32[]{:S(2)}) collective-permute-start(bf16[16,64,1536]{2,1,0:T(8,128)(2,1)} %dynamic-slice_bitcast_fusion.1), channel_id=1, source_target_pairs={{0,16},{16,0},{1,17},{17,1},{2,18},{18,2},{3,19},{19,3},{4,20},{20... | collective-permute-start | bytes 9437192 | tf_op jit(solution)/shard_map/ppermute | solution.py:852
  809.1 133.5 %all-to-all-start.6 = ((bf16[16,64,1536]{2,1,0:T(8,128)(2,1)}), bf16[16,64,1536]{2,1,0:T(8,128)(2,1)}, u32[]{:S(2)}, u32[]{:S(2)}) async-start(bf16[16,64,1536]{2,1,0:T(8,128)(2,1)} %fusion.19), calls=%async_computation.6 | async-start | bytes 6291456 | tf_op jit(solution)/shard_map/all_to_all | solution.py:865
  828.3 31.4 %collective-permute-start.16 = (bf16[2,2,2,80,512]{4,3,0,1,2:T(8,128)(2,1)}, bf16[2,2,2,80,512]{4,3,0,1,2:T(8,128)(2,1)}, u32[]{:S(2)}, u32[]{:S(2)}) collective-permute-start(bf16[2,2,2,80,512]{4,3,0,1,2:T(8,128)(2,1)} %bitcast.144), channel_id=1, source_target_pairs={{0,2},{1,3},{2,0},{3,1},{4,6},{5,7},{6,4},{7,5},{8,10},{9,11},{10,... | collective-permute-start | bytes 1966088 | tf_op jit(solution)/shard_map/ppermute | solution.py:985
  835.3 27.4 %collective-permute-start.14 = (bf16[2,2,2,80,512]{4,3,0,1,2:T(8,128)(2,1)}, bf16[2,2,2,80,512]{4,3,0,1,2:T(8,128)(2,1)}, u32[]{:S(2)}, u32[]{:S(2)}) collective-permute-start(bf16[2,2,2,80,512]{4,3,0,1,2:T(8,128)(2,1)} %bitcast.145), channel_id=1, source_target_pairs={{0,1},{1,0},{2,3},{3,2},{4,5},{5,4},{6,7},{7,6},{8,9},{9,8},{10,11... | collective-permute-start | bytes 1966088 | tf_op jit(solution)/shard_map/ppermute | solution.py:985
  849.7 68.9 %collective-permute-start.18 = (bf16[2,2,2,80,512]{4,3,2,1,0:T(8,128)(2,1)S(1)}, bf16[2,2,2,80,512]{4,3,2,1,0:T(8,128)(2,1)S(1)}, u32[]{:S(2)}, u32[]{:S(2)}) collective-permute-start(bf16[2,2,2,80,512]{4,3,2,1,0:T(8,128)(2,1)S(1)} %dynamic-slice_bitcast_fusion.4), channel_id=1, source_target_pairs={{0,4},{1,5},{2,6},{3,7},{4,0},{5,1},{6,2},{7,3},{8,12},{9,13},{10,... | collective-permute-start | bytes 1966088 | tf_op jit(solution)/shard_map/ppermute | solution.py:985
  861.2 58.2 %collective-permute-start.17 = (bf16[2,2,80,512]{3,2,0,1:T(8,128)(2,1)S(1)}, bf16[2,2,80,512]{3,2,0,1:T(8,128)(2,1)S(1)}, u32[]{:S(2)}, u32[]{:S(2)}) collective-permute-start(bf16[2,2,80,512]{3,2,0,1:T(8,128)(2,1)S(1)} %dynamic-slice_bitcast_fusion.6), channel_id=1, source_target_pairs={{0,1},{1,0},{2,3},{3,2},{4,5},{5,4},{6,7},{7,6},{8,9},{9,8},{10,11... | collective-permute-start | bytes 983048 | tf_op jit(solution)/shard_map/ppermute | solution.py:985
  864.1 55.4 %collective-permute-start.15 = (bf16[2,2,80,512]{3,2,0,1:T(8,128)(2,1)S(1)}, bf16[2,2,80,512]{3,2,0,1:T(8,128)(2,1)S(1)}, u32[]{:S(2)}, u32[]{:S(2)}) collective-permute-start(bf16[2,2,80,512]{3,2,0,1:T(8,128)(2,1)S(1)} %dynamic-slice_bitcast_fusion.7), channel_id=1, source_target_pairs={{0,2},{1,3},{2,0},{3,1},{4,6},{5,7},{6,4},{7,5},{8,10},{9,11},{10,... | collective-permute-start | bytes 983048 | tf_op jit(solution)/shard_map/ppermute | solution.py:985
  975.9 114.8 %collective-permute-start.32 = (bf16[80,1536]{1,0:T(8,128)(2,1)S(1)}, bf16[80,1536]{1,0:T(8,128)(2,1)}, u32[]{:S(2)}, u32[]{:S(2)}) collective-permute-start(bf16[80,1536]{1,0:T(8,128)(2,1)S(1)} %pad_maximum_fusion.10), channel_id=1, source_target_pairs={{0,0},{4,1},{9,2},{13,3},{18,4},{23,5},{27,6}} | collective-permute-start | bytes 737288 | tf_op jit(solution)/shard_map/ppermute | solution.py:1104
  977.2 115.2 %collective-permute-start.33 = (bf16[80,1536]{1,0:T(8,128)(2,1)S(1)}, bf16[80,1536]{1,0:T(8,128)(2,1)}, u32[]{:S(2)}, u32[]{:S(2)}) collective-permute-start(bf16[80,1536]{1,0:T(8,128)(2,1)S(1)} %pad_maximum_fusion.10), channel_id=1, source_target_pairs={{1,0},{5,1},{10,2},{14,3},{19,4},{24,5},{28,6}} | collective-permute-start | bytes 737288 | tf_op jit(solution)/shard_map/ppermute | solution.py:1104
  992.7 27.2 %collective-permute-start.42 = (f32[23040]{0:T(1024)S(1)}, f32[23040]{0:T(1024)}, u32[]{:S(2)}, u32[]{:S(2)}) collective-permute-start(f32[23040]{0:T(1024)S(1)} %add.421), channel_id=1, source_target_pairs={{0,1},{1,0},{2,3},{3,2},{4,5},{5,4},{6,7},{7,6},{8,9},{9,8},{10,11... | collective-permute-start | bytes 276488 | tf_op jit(solution)/shard_map/ppermute | solution.py:985
  1001.5 73.3 %collective-permute-start.23 = (bf16[288,1536]{1,0:T(8,128)(2,1)}, bf16[288,1536]{1,0:T(8,128)(2,1)}, u32[]{:S(2)}, u32[]{:S(2)}) collective-permute-start(bf16[288,1536]{1,0:T(8,128)(2,1)} %broadcast_select_fusion.4), channel_id=1, source_target_pairs={{1,11},{2,12},{3,13},{4,14},{5,15},{7,16},{8,17},{9,18},{11,19},{1... | collective-permute-start | bytes 2654216 | tf_op jit(solution)/shard_map/ppermute | solution.py:1104
  1010.8 55.0 %collective-permute-start.22 = (bf16[288,1536]{1,0:T(8,128)(2,1)S(1)}, bf16[288,1536]{1,0:T(8,128)(2,1)S(1)}, u32[]{:S(2)}, u32[]{:S(2)}) collective-permute-start(bf16[288,1536]{1,0:T(8,128)(2,1)S(1)} %get-tuple-element.158), channel_id=1, source_target_pairs={{0,11},{1,12},{2,13},{3,14},{4,15},{6,16},{7,17},{8,18},{10,19},{1... | collective-permute-start | bytes 2654216 | tf_op jit(solution)/shard_map/ppermute | solution.py:1104
  1019.9 73.7 %collective-permute-start.34 = (bf16[80,1536]{1,0:T(8,128)(2,1)S(1)}, bf16[80,1536]{1,0:T(8,128)(2,1)}, u32[]{:S(2)}, u32[]{:S(2)}) collective-permute-start(bf16[80,1536]{1,0:T(8,128)(2,1)S(1)} %pad_maximum_fusion.10), channel_id=1, source_target_pairs={{2,0},{6,1},{11,2},{15,3},{20,4},{25,5},{29,6}} | collective-permute-start | bytes 737288 | tf_op jit(solution)/shard_map/ppermute | solution.py:1104
  (105 other events, 1278.4 us)
Sparse Core Ops, SparseCore 0:
  24.1 183.7 all-gather.2
  210.8 151.2 all-gather.4
  630.5 329.6 reduce-scatter.1

commit v2 on v1

--- a/solution.py
+++ b/solution.py
@@ -927,7 +927,18 @@
         return back.reshape(self.length, count)
 
 
-def gather_weights(params, sent):
+def bias_tables(special, at):
+    length, own = (at.length, at.heads)
+    pos_low = special[: F * H].reshape(F, H)
+    pos_basis = position_basis(length)
+    own_pos = lax.dynamic_slice_in_dim(pos_low, at.head_start, own, 1)
+    tables = jnp.dot(own_pos.T, pos_basis.T, precision=highest)
+    tables = jnp.roll(jnp.pad(tables, ((0, 0), (0, 1))), 1 - BLOCK, axis=1)
+    tables = jnp.broadcast_to(tables[:, None, :], (own, 8, 2 * length))
+    return (pos_basis, tables)
+
+
+def gather_weights(params, sent, at):
     devices = lax.axis_size(("dp", "seq"))
     index = lax.axis_index(("dp", "seq"))
     dp, seq = lax.axis_size("dp"), lax.axis_size("seq")
@@ -948,6 +959,7 @@
     special, sent = lax.optimization_barrier((special, sent))
     ready = lax.all_to_all(sent, "seq", split_axis=0, concat_axis=0, tiled=True)
     special = special.astype(jnp.float32).reshape(-1)[TAIL - rest :]
+    pos_basis, tables = bias_tables(special, at)
     if own_rows % UNIT == 0:
         here = piece.reshape(own_rows // UNIT, UNIT, D)
         other = jnp.swapaxes(piece.reshape(own_rows // UNIT, 8, 2, D), 1, 2).reshape(here.shape)
@@ -962,7 +974,7 @@
         low = jnp.where(second, taken, piece[:half])
         high = jnp.where(second, piece[half:], taken)
         lower = lax.all_gather(low, ("seq", "dp"), axis=0, tiled=True)
-        high, lower, ready = lax.optimization_barrier((high, lower, ready))
+        high, lower, ready, tables = lax.optimization_barrier((high, lower, ready, tables))
         upper = lax.all_gather(high, ("seq", "dp"), axis=0, tiled=True)
     else:
         everything = lax.all_gather(piece, ("dp", "seq"), axis=0, tiled=True)
@@ -973,7 +985,7 @@
         w_up = jnp.concatenate([lower[UP_ROWS[0] :], upper[: UP_ROWS[0] + UP_ROWS[1] - ROWS // 2]])
         w_up = jnp.swapaxes(w_up.reshape(96, UNIT, 2, D), 1, 2)
     views = [array.reshape(-1, 2, UNIT, D) for array in (lower, upper)]
-    return (lower, (*views, w_up), special, ready)
+    return (lower, (*views, w_up), special, ready, pos_basis, tables)
 
 
 def axis_bits(axis):
@@ -1089,27 +1101,31 @@
     return result
 
 
-def add_rows(buffer, moved, place, count):
-    row = lax.broadcasted_iota(jnp.int32, moved.shape, 0)
-    moved = jnp.where(row < count, moved, jnp.zeros_like(moved))
-    there = lax.dynamic_slice_in_dim(buffer, place, moved.shape[0], 0)
-    return lax.dynamic_update_slice_in_dim(buffer, there + moved, place, 0)
-
-
 def to_owners(buffer, share, parts):
     rounds, most = moves(parts, TAIL // D)
-    share = jnp.pad(share, ((0, most), (0, 0)))
+    starts = [value for held in rounds for move in held for value in move[2:]]
+    size = math.gcd(UNIT, MARGIN, most, buffer.shape[0], *starts)
+    blocks = most // size
+    share = jnp.pad(share.reshape(blocks, size, D), ((0, blocks), (0, 0), (0, 0)))
+    buffer = buffer.reshape(-1, size, D)
+    arrived = []
     for held in rounds:
-        start = per_device([(t, offset) for _, t, _, _, offset in held])
-        moved = lax.ppermute(
-            lax.dynamic_slice_in_dim(share, start, most, 0),
-            ("dp", "seq"),
-            [(t, i) for i, t, _, _, _ in held],
-        )
-        place = per_device([(i, MARGIN + low) for i, _, _, low, _ in held])
-        count = per_device([(i, rows) for i, _, rows, _, _ in held])
-        buffer = add_rows(buffer, moved, place, count)
-    return buffer
+        start = per_device([(t, offset // size) for _, t, _, _, offset in held])
+        arrived.append(
+            lax.ppermute(
+                lax.dynamic_slice_in_dim(share, start, blocks, 0),
+                ("dp", "seq"),
+                [(t, i) for i, t, _, _, _ in held],
+            )
+        )
+    for held, moved in zip(rounds, arrived, strict=True):
+        place = per_device([(i, (MARGIN + low) // size) for i, _, _, low, _ in held])
+        count = per_device([(i, rows // size) for i, _, rows, _, _ in held])
+        inside = jnp.arange(blocks) < count
+        moved = jnp.where(inside[:, None, None], moved, jnp.zeros_like(moved))
+        there = lax.dynamic_slice_in_dim(buffer, place, blocks, 0)
+        buffer = lax.dynamic_update_slice_in_dim(buffer, there + moved, place, 0)
+    return buffer.reshape(-1, D)
 
 
 def own_entries(buffer, special):
@@ -1133,8 +1149,9 @@
     scale = 1.0 / math.sqrt(KD)
     f32, bf16 = jnp.float32, jnp.bfloat16
 
-    early, weights, special, moved = gather_weights(params, at.inputs_to_windows(block_input))
-    pos_low = special[: F * H].reshape(F, H)
+    early, weights, special, moved, pos_basis, tables = gather_weights(
+        params, at.inputs_to_windows(block_input), at
+    )
     up_bias = special[F * H : F * H + FF]
     vectors = special[F * H + FF :].reshape(12, D)
 
@@ -1149,12 +1166,6 @@
         ],
         axis=1,
     )
-    pos_basis = position_basis(length)
-    own_pos = lax.dynamic_slice_in_dim(pos_low, at.head_start, own, 1)
-    tables = jnp.dot(own_pos.T, pos_basis.T, precision=highest)
-    tables = jnp.roll(jnp.pad(tables, ((0, 0), (0, 1))), 1 - BLOCK, axis=1)
-    tables = jnp.broadcast_to(tables[:, None, :], (own, 8, 2 * length))
-
     low_part, _, _ = layer_stats(moved.astype(f32), vectors[0], vectors[1])
     low_all = at.gather_rows(low_part.astype(bf16))
     projected = jnp.einsum("rd,dk->kr", low_all, w_own, preferred_element_type=f32).astype(bf16)
@@ -1268,6 +1279,8 @@
     for pair in range(pairs):
         result, log_total = saved[pair]
         grads = attention_backward(*operands[pair], result, chunks[pair], log_total)
+        if pair + 1 < pairs:
+            grads, chunks[pair + 1] = lax.optimization_barrier((grads, chunks[pair + 1]))
         for piece, held in zip(grads, (dq, dk, dv, dt), strict=True):
             held.append(piece)
     grad_own = jnp.concatenate(dq + dk + dv, axis=1)

time: 1130 us -> 1080 us (0.956)
  blocking collectives: 140 us -> 0 us
  waiting for transfers between devices: 312 us -> 400 us
  starting transfers between devices: 108 us -> 125 us
    all_to_all x1 -> x0, blocking collectives: 140 us -> none  [gather_weights(): ready = lax.all_to_all(sent, 'seq', split_axis=0, concat_axis=0, tiled=True)]
    all_to_all x0 -> x1, waiting for transfers between devices: none -> 124 us  [gather_weights(): ready = lax.all_to_all(sent, 'seq', split_axis=0, concat_axis=0, tiled=True)]
    all_to_all x5, waiting for transfers between devices: 117 us -> 82.1 us  [exchange(): return lax.all_to_all(array, 'seq', split_axis=0, concat_axis=0, tiled=True)]
    ppermute x20, waiting for transfers between devices: 105 us -> 85 us  [partner(): return lax.ppermute(array, axis, pairs)]
    dynamic_update_slice x2 -> x0, local copies, waits for them, and re-layouts: 12 us -> none  [add_rows(): return lax.dynamic_update_slice_in_dim(buffer, there + moved, place, 0)]
  transfers between devices with their start and end apart: 52 -> 53, of which waited for: 23 -> 25; matrix products, arithmetic and copies ran while one was open for 17% -> 16% of each run, Pallas kernels for 15% -> 16%
where the time goes in v2:
time: 1080 us; the launch traced here: 1070 us
  waiting for transfers between devices  400 us (37%)
  Pallas kernels  308 us (29%)
  starting transfers between devices  125 us (12%)
  local copies, waits for them, and re-layouts  95.5 us (9%)
  other arithmetic  78.5 us (7%)
  matrix products  42.9 us (4%)
  between operations  15.7 us (1%)
    all_to_all x1, waiting for transfers between devices, gather_weights(): ready = lax.all_to_all(sent, 'seq', split_axis=0, concat_axis=0, tiled=True)  124 us
    ppermute x20, waiting for transfers between devices, partner(): return lax.ppermute(array, axis, pairs)  85 us
    all_to_all x5, waiting for transfers between devices, exchange(): return lax.all_to_all(array, 'seq', split_axis=0, concat_axis=0, tiled=True)  82.1 us
    pallas_call x2, Pallas kernels, attention_backward(): pl.pallas_call(functools.partial(backward_kernel, blocks=blocks), grid=(b...  81.6 us
    pallas_call x1, Pallas kernels, dense_backward(): pl.pallas_call(functools.partial(dense_back_kernel, count=count, rows=row...  47.8 us
    ppermute x10, waiting for transfers between devices, to_owners(): lax.ppermute(lax.dynamic_slice_in_dim(share, start, blocks, 0), ('dp', 's...  47.7 us
    pallas_call x2, Pallas kernels, attention_forward(): pl.pallas_call(functools.partial(forward_kernel, blocks=blocks), grid=(bl...  44.8 us
    pallas_call x1, Pallas kernels, point_layer(): pl.pallas_call(functools.partial(point_kernel, rows=rows), grid=(windows,...  43.7 us
  transfers between devices with their start and end apart: 53, of which 25 were waited for; matrix products, arithmetic and copies ran while one was open for 16% of the time, Pallas kernels for 16%

profile of v2, /device:TPU:16, one launch (start us, length us, event | category | flops | bytes accessed | tf_op | source)
XLA Modules:
  0.0 1065.3 jit_solution(631875121645378597)
XLA Ops:
  33.3 30.3 %all-to-all-done = bf16[16,16,1536]{2,1,0:T(8,128)(2,1)} async-done(((bf16[16,16,1536]{2,1,0:T(8,128)(2,1)}), bf16[16,16,1536]{2,1,0:T(8,128)(2,1)}, u32[]{:S(2)}, u32[]{:S(2)}) %all-to-all-start) | async-done | bytes 786464 | tf_op jit(solution)/shard_map/all_to_all | solution.py:958
  83.5 124.2 %all-to-all-done.1 = bf16[16,64,1536]{2,1,0:T(8,128)(2,1)S(1)} async-done(((bf16[16,64,1536]{2,1,0:T(8,128)(2,1)}), bf16[16,64,1536]{2,1,0:T(8,128)(2,1)S(1)}, u32[]{:S(2)}, u32[]{:S(2)}) %all-to-all-start.1) | async-done | bytes 3145760 | tf_op jit(solution)/shard_map/all_to_all | solution.py:960
  259.0 22.4 %shard_map.127 = (bf16[2048,384]{1,0:T(8,128)(2,1)}, f32[2,2048]{1,0:T(2,128)S(1)}) custom-call(f32[2,8,4096]{2,1,0:T(8,128)S(1)} %get-tuple-element.171.table_ref, bf16[128,2048]{1,0:T(8,128)(2,1)S(1)} %get-tuple-element.144.q_ref, bf16[128,2048]{1,0:T(8,128)(2,1)S(1)} %get-tuple-element.143.k_ref, bf16[384,2048]{1,0:T(8,128)(2,1)S(1)} %get-tuple-element.141.v_ref), custom_call_target="tpu_custom_call" | custom-call | flops 536870912 | bytes 524288 | tf_op jit(solution)/shard_map/pallas_call | solution.py:190
  282.0 11.2 %all-to-all-start.3 = ((bf16[16,128,384]{2,1,0:T(8,128)(2,1)}), bf16[16,128,384]{2,1,0:T(8,128)(2,1)}, u32[]{:S(2)}, u32[]{:S(2)}) async-start(bf16[16,128,384]{2,1,0:T(8,128)(2,1)} %bitcast.10), calls=%async_computation.3 | async-start | bytes 3145728 | tf_op jit(solution)/shard_map/all_to_all | solution.py:865
  294.6 22.4 %shard_map.126 = (bf16[2048,384]{1,0:T(8,128)(2,1)}, f32[2,2048]{1,0:T(2,128)S(1)}) custom-call(f32[2,8,4096]{2,1,0:T(8,128)S(1)} %copy-done.11, bf16[128,2048]{1,0:T(8,128)(2,1)S(1)} %copy-done.6, bf16[128,2048]{1,0:T(8,128)(2,1)S(1)} %get-tuple-element.145.k_ref, bf16[384,2048]{1,0:T(8,128)(2,1)S(1)} %copy-done.2), custom_call_target="tpu_custom_call" | custom-call | flops 536870912 | bytes 524288 | tf_op jit(solution)/shard_map/pallas_call | solution.py:190
  317.0 48.5 %all-to-all-done.3 = bf16[16,128,384]{2,1,0:T(8,128)(2,1)} async-done(((bf16[16,128,384]{2,1,0:T(8,128)(2,1)}), bf16[16,128,384]{2,1,0:T(8,128)(2,1)}, u32[]{:S(2)}, u32[]{:S(2)}) %all-to-all-start.3) | async-done | bytes 1572896 | tf_op jit(solution)/shard_map/all_to_all | solution.py:865
  374.4 33.6 %all-to-all-done.2 = bf16[16,128,384]{2,1,0:T(8,128)(2,1)S(1)} async-done(((bf16[16,128,384]{2,1,0:T(8,128)(2,1)}), bf16[16,128,384]{2,1,0:T(8,128)(2,1)S(1)}, u32[]{:S(2)}, u32[]{:S(2)}) %all-to-all-start.2) | async-done | bytes 1572896 | tf_op jit(solution)/shard_map/all_to_all | solution.py:865
  423.3 42.8 %shard_map.129 = (bf16[8,128,1536]{2,1,0:T(8,128)(2,1)}, f32[8,128,1536]{2,1,0:T(8,128)}, bf16[8,128,1536]{2,1,0:T(8,128)(2,1)}, bf16[8,128,3072]{2,1,0:T(8,128)...) custom-call(s32[1]{0:T(128)} %bitcast.core_ref, bf16[8,128,1536]{2,1,0:T(8,128)(2,1)} %inputs_ref.1, ...), custom_call_target="tpu_custom_call" | custom-call | flops 1509949440 | bytes 4030464 | tf_op jit(solution)/shard_map/pallas_call | solution.py:508
  477.5 43.7 %shard_map.130 = (bf16[8,256,1536]{2,1,0:T(8,128)(2,1)}, bf16[8,256,1536]{2,1,0:T(8,128)(2,1)}, bf16[288,2,16,1536]{3,2,1,0:T(8,128)(2,1)}, f32[8,1,1536]{2,1,0:T(1,128)}, f32[8,1536]{1,0:T(8,128)}) custom-call(f32[8,128,1536]{2,1,0:T(8,128)} %get-tuple-element.68.after_ref, bf16[8,256,1536]{2,1,0:T(8,128)(2,1)} %skip_ref.1, ...), custom_call_target="tpu_custom_call" | custom-call | flops 1811939328 | bytes 2555904 | tf_op jit(solution)/shard_map/pallas_call | solution.py:617
  536.7 47.8 %shard_map.131 = (f32[8,256,1536]{2,1,0:T(8,128)}, f32[8,128,1536]{2,1,0:T(8,128)}, bf16[8,128,1536]{2,1,0:T(8,128)(2,1)}, bf16[8,128,3072]{2,1,0:T(8,128)(2,1)}...) custom-call(s32[1]{0:T(128)} %bitcast.core_ref, ...), custom_call_target="tpu_custom_call" | custom-call | flops 1509949440 | bytes 5406720 | tf_op jit(solution)/shard_map/pallas_call | solution.py:770
  594.2 14.2 %shard_map.132.refs_0_ = bf16[288,2,16,1536]{3,2,1,0:T(8,128)(2,1)} custom-call(bf16[8,128,3072]{2,1,0:T(8,128)(2,1)} %get-tuple-element.78.left_ref, bf16[8,128,1536]{2,1,0:T(8,128)(2,1)S(1)} %copy-done.8, bf16[288,2,16,1536]{3,2,1,0:T(8,128)(2,1)} %get-tuple-element.80.refs_0_), custom_call_target="tpu_custom_call", output_to_operand_aliasing={{}: (2, {})} | custom-call | flops 603979776 | bytes 1179648 | tf_op jit(solution)/shard_map/pallas_call | solution.py:808
  608.4 15.9 %shard_map.133.refs_0_ = bf16[288,2,16,1536]{3,2,1,0:T(8,128)(2,1)} custom-call(bf16[8,128,1536]{2,1,0:T(8,128)(2,1)S(1)} %copy-done.7, bf16[8,128,3072]{2,1,0:T(8,128)(2,1)} %get-tuple-element.77.right_ref, bf16[288,2,16,1536]{3,2,1,0:T(8,128)(2,1)} %shard_map.132.refs_0_), custom_call_target="tpu_custom_call", output_to_operand_aliasing={{}: (2, {})} | custom-call | flops 603979776 | bytes 1179648 | tf_op jit(solution)/shard_map/pallas_call | solution.py:808
  624.2 8.9 shard_map.134
  645.4 40.8 %shard_map.135 = (bf16[2048,128]{1,0:T(8,128)(2,1)}, bf16[2048,128]{1,0:T(8,128)(2,1)}, bf16[2048,384]{1,0:T(8,128)(2,1)}, f32[2,4096]{1,0:T(2,128)}) custom-call(f32[2,8,4096]{2,1,0:T(8,128)} %get-tuple-element.172.table_ref, bf16[128,2048]{1,0:T(8,128)(2,1)} %get-tuple-element.146.q_ref, bf16[128,2048]{1,0:T(8,128)(2,1)} %copy-done.5, ...), custom_call_target="tpu_custom_call" | custom-call | flops 1342177280 | bytes 1048576 | tf_op jit(solution)/shard_map/pallas_call | solution.py:312
  687.4 40.9 %shard_map.136 = (bf16[2048,128]{1,0:T(8,128)(2,1)}, bf16[2048,128]{1,0:T(8,128)(2,1)}, bf16[2048,384]{1,0:T(8,128)(2,1)}, f32[2,4096]{1,0:T(2,128)}) custom-call(f32[2,8,4096]{2,1,0:T(8,128)} %copy-done.10, bf16[128,2048]{1,0:T(8,128)(2,1)} %copy-done.4, bf16[128,2048]{1,0:T(8,128)(2,1)} %copy-done.3, bf16[384,2048]{1,0:T(8,128)(2,1)} %copy-done.1, ...), custom_call_target="tpu_custom_call" | custom-call | flops 1342177280 | bytes 1048576 | tf_op jit(solution)/shard_map/pallas_call | solution.py:312
  732.6 9.2 convolution_convert_fusion
  745.5 10.3 fusion.74
  804.2 9.5 fusion.20
  818.7 22.0 %collective-permute-done.16 = bf16[2,2,2,80,512]{4,3,0,1,2:T(8,128)(2,1)} collective-permute-done((bf16[2,2,2,80,512]{4,3,0,1,2:T(8,128)(2,1)}, bf16[2,2,2,80,512]{4,3,0,1,2:T(8,128)(2,1)}, u32[]{:S(2)}, u32[]{:S(2)}) %collective-permute-start.16) | collective-permute-done | bytes 655392 | tf_op jit(solution)/shard_map/ppermute | solution.py:997
  859.3 20.8 %collective-permute-done.19 = bf16[2,2,80,512]{3,2,1,0:T(8,128)(2,1)S(1)} collective-permute-done((bf16[2,2,80,512]{3,2,1,0:T(8,128)(2,1)S(1)}, bf16[2,2,80,512]{3,2,1,0:T(8,128)(2,1)S(1)}, u32[]{:S(2)}, u32[]{:S(2)}) %collective-permute-start.19) | collective-permute-done | bytes 327712 | tf_op jit(solution)/shard_map/ppermute | solution.py:997
  889.4 13.7 %collective-permute-done.26 = bf16[2,80,512]{2,1,0:T(8,128)(2,1)S(1)} collective-permute-done((bf16[2,80,512]{2,1,0:T(8,128)(2,1)S(1)}, bf16[2,80,512]{2,1,0:T(8,128)(2,1)S(1)}, u32[]{:S(2)}, u32[]{:S(2)}) %collective-permute-start.26) | collective-permute-done | bytes 163872 | tf_op jit(solution)/shard_map/ppermute | solution.py:997
  949.9 9.3 reduce-scatter.2.cloned.1.call-done
  987.0 47.7 %collective-permute-done.22 = bf16[18,16,1536]{2,1,0:T(8,128)(2,1)S(1)} collective-permute-done((bf16[18,16,1536]{2,1,0:T(8,128)(2,1)S(1)}, bf16[18,16,1536]{2,1,0:T(8,128)(2,1)S(1)}, u32[]{:S(2)}, u32[]{:S(2)}) %collective-permute-start.22) | collective-permute-done | bytes 884768 | tf_op jit(solution)/shard_map/ppermute | solution.py:1115
  1049.4 9.1 fusion.65
  (430 shorter events, 350.5 us)
Async XLA Ops:
  7.2 206.5 %all-gather.3.cloned.1.call-start = ((), (), s32[]{:S(2)}) async-start(), calls=%async_computation.8 | async-start | bytes 18653184 | tf_op jit(solution)/shard_map/all_gather | solution.py:976
  26.3 37.2 %all-to-all-start = ((bf16[16,16,1536]{2,1,0:T(8,128)(2,1)}), bf16[16,16,1536]{2,1,0:T(8,128)(2,1)}, u32[]{:S(2)}, u32[]{:S(2)}) async-start(bf16[16,16,1536]{2,1,0:T(8,128)(2,1)} %broadcast_in_dim.152), calls=%async_computation | async-start | bytes 1572864 | tf_op jit(solution)/shard_map/all_to_all | solution.py:958
  33.2 31.1 %collective-permute-start.3 = (bf16[8,64,1536]{2,1,0:T(8,128)(2,1)}, bf16[8,64,1536]{2,1,0:T(8,128)(2,1)}, u32[]{:S(2)}, u32[]{:S(2)}) collective-permute-start(bf16[8,64,1536]{2,1,0:T(8,128)(2,1)} %constant_dynamic-slice_fusion.9), channel_id=1, source_target_pairs={{0,16},{16,0},{1,17},{17,1},{2,18},{18,2},{3,19},{19,3},{4,20},{20... | collective-permute-start | bytes 4718600 | tf_op jit(solution)/shard_map/ppermute | solution.py:852
  68.3 139.4 %all-to-all-start.1 = ((bf16[16,64,1536]{2,1,0:T(8,128)(2,1)}), bf16[16,64,1536]{2,1,0:T(8,128)(2,1)S(1)}, u32[]{:S(2)}, u32[]{:S(2)}) async-start(bf16[16,64,1536]{2,1,0:T(8,128)(2,1)} %pad_maximum_fusion.6), calls=%async_computation.1 | async-start | bytes 6291456 | tf_op jit(solution)/shard_map/all_to_all | solution.py:960
  74.3 336.3 %all-gather.5.cloned.1.call-start = ((), (), s32[]{:S(2)}) async-start(), calls=%async_computation.9 | async-start | bytes 18653184 | tf_op jit(solution)/shard_map/all_gather | solution.py:978
  282.0 83.6 %all-to-all-start.3 = ((bf16[16,128,384]{2,1,0:T(8,128)(2,1)}), bf16[16,128,384]{2,1,0:T(8,128)(2,1)}, u32[]{:S(2)}, u32[]{:S(2)}) async-start(bf16[16,128,384]{2,1,0:T(8,128)(2,1)} %bitcast.10), calls=%async_computation.3 | async-start | bytes 3145728 | tf_op jit(solution)/shard_map/all_to_all | solution.py:865
  365.6 42.4 %all-to-all-start.2 = ((bf16[16,128,384]{2,1,0:T(8,128)(2,1)}), bf16[16,128,384]{2,1,0:T(8,128)(2,1)S(1)}, u32[]{:S(2)}, u32[]{:S(2)}) async-start(bf16[16,128,384]{2,1,0:T(8,128)(2,1)} %bitcast.9), calls=%async_computation.2 | async-start | bytes 3145728 | tf_op jit(solution)/shard_map/all_to_all | solution.py:865
  374.4 47.7 %collective-permute-start.6 = (bf16[8,1,128,384]{3,2,0,1:T(8,128)(2,1)}, bf16[8,1,128,384]{3,2,0,1:T(8,128)(2,1)S(1)}, u32[]{:S(2)}, u32[]{:S(2)}) collective-permute-start(bf16[8,1,128,384]{3,2,0,1:T(8,128)(2,1)} %get-tuple-element.160), channel_id=1, source_target_pairs={{0,16},{16,0},{1,17},{17,1},{2,18},{18,2},{3,19},{19,3},{4,20},{20... | collective-permute-start | bytes 2359304 | tf_op jit(solution)/shard_map/ppermute | solution.py:852
  589.7 43.5 %all-to-all-start.4 = ((bf16[16,128,384]{2,1,0:T(8,128)(2,1)}), bf16[16,128,384]{2,1,0:T(8,128)(2,1)}, u32[]{:S(2)}, u32[]{:S(2)}) async-start(bf16[16,128,384]{2,1,0:T(8,128)(2,1)} %maximum_bitcast_fusion), calls=%async_computation.4 | async-start | bytes 3145728 | tf_op jit(solution)/shard_map/all_to_all | solution.py:865
  594.1 365.1 %reduce-scatter.2.cloned.1.call-start = ((), (), s32[]{:S(2)}) async-start(), calls=%async_computation.10 | async-start | bytes 29196288 | tf_op jit(solution)/shard_map/reduce_scatter | solution.py:1276
  638.1 48.1 %all-to-all-start.5 = ((bf16[16,128,384]{2,1,0:T(8,128)(2,1)}), bf16[16,128,384]{2,1,0:T(8,128)(2,1)S(1)}, u32[]{:S(2)}, u32[]{:S(2)}) async-start(bf16[16,128,384]{2,1,0:T(8,128)(2,1)} %maximum_bitcast_fusion.1), calls=%async_computation.5 | async-start | bytes 3145728 | tf_op jit(solution)/shard_map/all_to_all | solution.py:865
  775.0 105.8 %all-to-all-start.6 = ((bf16[16,64,1536]{2,1,0:T(8,128)(2,1)}), bf16[16,64,1536]{2,1,0:T(8,128)(2,1)}, u32[]{:S(2)}, u32[]{:S(2)}) async-start(bf16[16,64,1536]{2,1,0:T(8,128)(2,1)} %fusion.19), calls=%async_computation.6 | async-start | bytes 6291456 | tf_op jit(solution)/shard_map/all_to_all | solution.py:865
  795.7 45.1 %collective-permute-start.16 = (bf16[2,2,2,80,512]{4,3,0,1,2:T(8,128)(2,1)}, bf16[2,2,2,80,512]{4,3,0,1,2:T(8,128)(2,1)}, u32[]{:S(2)}, u32[]{:S(2)}) collective-permute-start(bf16[2,2,2,80,512]{4,3,0,1,2:T(8,128)(2,1)} %bitcast.146), channel_id=1, source_target_pairs={{0,2},{1,3},{2,0},{3,1},{4,6},{5,7},{6,4},{7,5},{8,10},{9,11},{10,... | collective-permute-start | bytes 1966088 | tf_op jit(solution)/shard_map/ppermute | solution.py:997
  802.7 42.9 %collective-permute-start.14 = (bf16[2,2,2,80,512]{4,3,0,1,2:T(8,128)(2,1)}, bf16[2,2,2,80,512]{4,3,0,1,2:T(8,128)(2,1)}, u32[]{:S(2)}, u32[]{:S(2)}) collective-permute-start(bf16[2,2,2,80,512]{4,3,0,1,2:T(8,128)(2,1)} %bitcast.147), channel_id=1, source_target_pairs={{0,1},{1,0},{2,3},{3,2},{4,5},{5,4},{6,7},{7,6},{8,9},{9,8},{10,11... | collective-permute-start | bytes 1966088 | tf_op jit(solution)/shard_map/ppermute | solution.py:997
  817.1 31.9 %collective-permute-start.18 = (bf16[2,2,2,80,512]{4,3,2,1,0:T(8,128)(2,1)S(1)}, bf16[2,2,2,80,512]{4,3,2,1,0:T(8,128)(2,1)S(1)}, u32[]{:S(2)}, u32[]{:S(2)}) collective-permute-start(bf16[2,2,2,80,512]{4,3,2,1,0:T(8,128)(2,1)S(1)} %dynamic-slice_bitcast_fusion.4), channel_id=1, source_target_pairs={{0,4},{1,5},{2,6},{3,7},{4,0},{5,1},{6,2},{7,3},{8,12},{9,13},{10,... | collective-permute-start | bytes 1966088 | tf_op jit(solution)/shard_map/ppermute | solution.py:997
  849.3 30.8 %collective-permute-start.19 = (bf16[2,2,80,512]{3,2,1,0:T(8,128)(2,1)S(1)}, bf16[2,2,80,512]{3,2,1,0:T(8,128)(2,1)S(1)}, u32[]{:S(2)}, u32[]{:S(2)}) collective-permute-start(bf16[2,2,80,512]{3,2,1,0:T(8,128)(2,1)S(1)} %dynamic-slice_bitcast_fusion.5), channel_id=1, source_target_pairs={{0,8},{1,9},{2,10},{3,11},{4,12},{5,13},{6,14},{7,15},{8,0},{9,1},... | collective-permute-start | bytes 983048 | tf_op jit(solution)/shard_map/ppermute | solution.py:997
  887.9 29.8 %collective-permute-start.21 = (bf16[8,64,1536]{2,1,0:T(8,128)(2,1)S(1)}, bf16[8,64,1536]{2,1,0:T(8,128)(2,1)S(1)}, u32[]{:S(2)}, u32[]{:S(2)}) collective-permute-start(bf16[8,64,1536]{2,1,0:T(8,128)(2,1)S(1)} %constant_dynamic-slice_fusion), channel_id=1, source_target_pairs={{0,16},{16,0},{1,17},{17,1},{2,18},{18,2},{3,19},{19,3},{4,20},{20... | collective-permute-start | bytes 4718600 | tf_op jit(solution)/shard_map/ppermute | solution.py:852
  888.0 26.6 %collective-permute-start.30 = (bf16[2,80,512]{2,1,0:T(8,128)(2,1)S(1)}, bf16[2,80,512]{2,1,0:T(8,128)(2,1)S(1)}, u32[]{:S(2)}, u32[]{:S(2)}) collective-permute-start(bf16[2,80,512]{2,1,0:T(8,128)(2,1)S(1)} %dynamic-slice_bitcast_fusion.8), channel_id=1, source_target_pairs={{0,1},{1,0},{2,3},{3,2},{4,5},{5,4},{6,7},{7,6},{8,9},{9,8},{10,11... | collective-permute-start | bytes 491528 | tf_op jit(solution)/shard_map/ppermute | solution.py:997
  927.7 113.0 %collective-permute-start.32 = (bf16[5,16,1536]{2,1,0:T(8,128)(2,1)S(1)}, bf16[5,16,1536]{2,1,0:T(8,128)(2,1)}, u32[]{:S(2)}, u32[]{:S(2)}) collective-permute-start(bf16[5,16,1536]{2,1,0:T(8,128)(2,1)S(1)} %bitcast.170), channel_id=1, source_target_pairs={{0,0},{4,1},{9,2},{13,3},{18,4},{23,5},{27,6}} | collective-permute-start | bytes 737288 | tf_op jit(solution)/shard_map/ppermute | solution.py:1115
  929.1 113.5 %collective-permute-start.33 = (bf16[5,16,1536]{2,1,0:T(8,128)(2,1)S(1)}, bf16[5,16,1536]{2,1,0:T(8,128)(2,1)}, u32[]{:S(2)}, u32[]{:S(2)}) collective-permute-start(bf16[5,16,1536]{2,1,0:T(8,128)(2,1)S(1)} %bitcast.171), channel_id=1, source_target_pairs={{1,0},{5,1},{10,2},{14,3},{19,4},{24,5},{28,6}} | collective-permute-start | bytes 737288 | tf_op jit(solution)/shard_map/ppermute | solution.py:1115
  949.8 35.5 %collective-permute-start.42 = (f32[23040]{0:T(1024)S(1)}, f32[23040]{0:T(1024)}, u32[]{:S(2)}, u32[]{:S(2)}) collective-permute-start(f32[23040]{0:T(1024)S(1)} %add.421), channel_id=1, source_target_pairs={{0,1},{1,0},{2,3},{3,2},{4,5},{5,4},{6,7},{7,6},{8,9},{9,8},{10,11... | collective-permute-start | bytes 276488 | tf_op jit(solution)/shard_map/ppermute | solution.py:997
  967.1 69.0 %collective-permute-start.23 = (bf16[18,16,1536]{2,1,0:T(8,128)(2,1)S(1)}, bf16[18,16,1536]{2,1,0:T(8,128)(2,1)S(1)}, u32[]{:S(2)}, u32[]{:S(2)}) collective-permute-start(bf16[18,16,1536]{2,1,0:T(8,128)(2,1)S(1)} %broadcast_select_fusion.4), channel_id=1, source_target_pairs={{1,11},{2,12},{3,13},{4,14},{5,15},{7,16},{8,17},{9,18},{11,19},{1... | collective-permute-start | bytes 2654216 | tf_op jit(solution)/shard_map/ppermute | solution.py:1115
  976.1 58.5 %collective-permute-start.22 = (bf16[18,16,1536]{2,1,0:T(8,128)(2,1)S(1)}, bf16[18,16,1536]{2,1,0:T(8,128)(2,1)S(1)}, u32[]{:S(2)}, u32[]{:S(2)}) collective-permute-start(bf16[18,16,1536]{2,1,0:T(8,128)(2,1)S(1)} %get-tuple-element.170), channel_id=1, source_target_pairs={{0,11},{1,12},{2,13},{3,14},{4,15},{6,16},{7,17},{8,18},{10,19},{1... | collective-permute-start | bytes 2654216 | tf_op jit(solution)/shard_map/ppermute | solution.py:1115
  985.3 58.3 %collective-permute-start.34 = (bf16[5,16,1536]{2,1,0:T(8,128)(2,1)S(1)}, bf16[5,16,1536]{2,1,0:T(8,128)(2,1)S(1)}, u32[]{:S(2)}, u32[]{:S(2)}) collective-permute-start(bf16[5,16,1536]{2,1,0:T(8,128)(2,1)S(1)} %bitcast.172), channel_id=1, source_target_pairs={{2,0},{6,1},{11,2},{15,3},{20,4},{25,5},{29,6}} | collective-permute-start | bytes 737288 | tf_op jit(solution)/shard_map/ppermute | solution.py:1115
  (105 other events, 1256.2 us)
Sparse Core Ops, SparseCore 0:
  24.1 189.5 all-gather.2
  216.6 150.2 all-gather.4
  633.3 325.8 reduce-scatter.1

commit v3 on v2

--- a/solution.py
+++ b/solution.py
@@ -379,6 +379,46 @@
     )
 
 
+def own_weights_kernel(start_ref, q_ref, k_ref, v_a, v_b, v_c, out_ref, apart, *, own):
+    start = start_ref[0]
+    rows, narrow = (q_ref.shape[0], own * KD)
+    for number, (ref, scale) in enumerate(((q_ref, 1.0 / math.sqrt(KD)), (k_ref, 1.0))):
+        for third in range(3):
+            at = pl.multiple_of(third * (H * KD) + start * KD, LANES)
+            part = ref[:, pl.ds(at, narrow)].astype(jnp.float32) * scale
+            for lanes in range(narrow // LANES):
+                apart[lanes, pl.ds(third, rows, stride=3), :] = part[
+                    :, lanes * LANES : (lanes + 1) * LANES
+                ]
+        for lanes in range(narrow // LANES):
+            place = number * narrow + lanes * LANES
+            out_ref[:, place : place + LANES] = apart[lanes].astype(jnp.bfloat16)
+    at = pl.multiple_of(start * VD, LANES)
+    for number, ref in enumerate((v_a, v_b, v_c)):
+        out_ref[number * rows : (number + 1) * rows, 2 * narrow :] = ref[:, pl.ds(at, own * VD)]
+
+
+def own_weights(rows, start, own):
+    steps, narrow = (4, H * KD // 4)
+    out = jax.ShapeDtypeStruct((D, own * (2 * KD + VD)), jnp.bfloat16)
+    return pl.pallas_call(
+        functools.partial(own_weights_kernel, own=own),
+        grid=(steps,),
+        in_specs=[
+            pl.BlockSpec(memory_space=pltpu.SMEM),
+            pl.BlockSpec((narrow, D), lambda i: (i, 0)),
+            pl.BlockSpec((narrow, D), lambda i: (steps + i, 0)),
+            pl.BlockSpec((narrow, D), lambda i: (2 * steps + 3 * i, 0)),
+            pl.BlockSpec((narrow, D), lambda i: (2 * steps + 3 * i + 1, 0)),
+            pl.BlockSpec((narrow, D), lambda i: (2 * steps + 3 * i + 2, 0)),
+        ],
+        out_specs=pl.BlockSpec((D // steps, out.shape[1]), lambda i: (i, 0)),
+        out_shape=out,
+        scratch_shapes=[pltpu.VMEM((own * KD // LANES, D // steps, LANES), jnp.float32)],
+        compiler_params=pltpu.CompilerParams(vmem_limit_bytes=32 * 2**20),
+    )(start, *[rows] * 5)
+
+
 def up_units_kernel(lower_ref, upper_ref, out_ref, *, steps):
     units = out_ref.shape[0]
 
@@ -927,6 +967,12 @@
         return back.reshape(self.length, count)
 
 
+def normed_rows(moved, special, at):
+    vectors = special[F * H + FF :].reshape(12, D)
+    low_part, _, _ = layer_stats(moved.astype(jnp.float32), vectors[0], vectors[1])
+    return at.gather_rows(low_part.astype(jnp.bfloat16))
+
+
 def bias_tables(special, at):
     length, own = (at.length, at.heads)
     pos_low = special[: F * H].reshape(F, H)
@@ -960,6 +1006,7 @@
     ready = lax.all_to_all(sent, "seq", split_axis=0, concat_axis=0, tiled=True)
     special = special.astype(jnp.float32).reshape(-1)[TAIL - rest :]
     pos_basis, tables = bias_tables(special, at)
+    ready = normed_rows(ready, special, at)
     if own_rows % UNIT == 0:
         here = piece.reshape(own_rows // UNIT, UNIT, D)
         other = jnp.swapaxes(piece.reshape(own_rows // UNIT, 8, 2, D), 1, 2).reshape(here.shape)
@@ -1149,25 +1196,14 @@
     scale = 1.0 / math.sqrt(KD)
     f32, bf16 = jnp.float32, jnp.bfloat16
 
-    early, weights, special, moved, pos_basis, tables = gather_weights(
+    early, weights, special, low_all, pos_basis, tables = gather_weights(
         params, at.inputs_to_windows(block_input), at
     )
     up_bias = special[F * H : F * H + FF]
     vectors = special[F * H + FF :].reshape(12, D)
 
-    def columns(matrix, width):
-        return lax.dynamic_slice_in_dim(matrix, at.head_start * width, own * width, 1)
-
-    w_own = jnp.concatenate(
-        [
-            columns(early[:512].reshape(D, H * KD), KD) * jnp.asarray(scale, bf16),
-            columns(early[512:1024].reshape(D, H * KD), KD),
-            columns(early[1024:2560].reshape(D, H * VD), VD),
-        ],
-        axis=1,
-    )
-    low_part, _, _ = layer_stats(moved.astype(f32), vectors[0], vectors[1])
-    low_all = at.gather_rows(low_part.astype(bf16))
+    w_own = own_weights(early, jnp.asarray(at.head_start, jnp.int32).reshape(1), own)
+
     projected = jnp.einsum("rd,dk->kr", low_all, w_own, preferred_element_type=f32).astype(bf16)
     queries, keys, values = (
         projected[: own * KD],
@@ -1327,12 +1363,12 @@
     special_grads = jnp.concatenate(
         [late[: F * H], middle[:FF], late[F * H :], middle[FF:]]
     )
-    share = dense
+    buffer = jnp.zeros((ROWS // devices + TAIL // D + 2 * MARGIN, D), bf16)
+    buffer = to_owners(buffer, first_sums.finish(), QKV_PARTS)
+    share, buffer, special_grads = lax.optimization_barrier((dense, buffer, special_grads))
     if even:
         share = halves_apart(share, lax.axis_index(("dp", "seq")) * share.shape[0], 2, UNIT)
-    buffer = jnp.zeros((ROWS // devices + TAIL // D + 2 * MARGIN, D), bf16)
     buffer = to_owners(buffer, share, PARTS)
-    buffer = to_owners(buffer, first_sums.finish(), QKV_PARTS)
     reduced = own_entries(buffer, special_grads)
     shard_len = params.shape[0]
     position = lax.axis_index(("dp", "seq")) * shard_len + jnp.arange(shard_len)

time: 1080 us -> 1100 us (1.019)
  other arithmetic: 78.5 us -> 95.7 us
  waiting for transfers between devices: 400 us -> 417 us
    dynamic_update_slice x10, other arithmetic: 4.69 us -> 20.8 us  [to_owners(): buffer = lax.dynamic_update_slice_in_dim(buffer, there + moved, place, 0)]
    unnamed x169 -> x165, local copies, waits for them, and re-layouts: 25.2 us -> 32.5 us
  transfers between devices with their start and end apart: 53 -> 53, of which waited for: 25 -> 25; matrix products, arithmetic and copies ran while one was open for 16% -> 15% of each run, Pallas kernels for 16% -> 16%
where the time goes in v3:
time: 1100 us; the launch traced here: 1090 us
  waiting for transfers between devices  417 us (38%)
  Pallas kernels  308 us (28%)
  starting transfers between devices  126 us (11%)
  other arithmetic  95.7 us (9%)
  local copies, waits for them, and re-layouts  88.4 us (8%)
  matrix products  41.3 us (4%)
  between operations  15.8 us (1%)
    all_to_all x1, waiting for transfers between devices, gather_weights(): ready = lax.all_to_all(sent, 'seq', split_axis=0, concat_axis=0, tiled=True)  133 us
    ppermute x20, waiting for transfers between devices, partner(): return lax.ppermute(array, axis, pairs)  95.6 us
    all_to_all x5, waiting for transfers between devices, exchange(): return lax.all_to_all(array, 'seq', split_axis=0, concat_axis=0, tiled=True)  92.4 us
    pallas_call x2, Pallas kernels, attention_backward(): pl.pallas_call(functools.partial(backward_kernel, blocks=blocks), grid=(b...  81.6 us
    ppermute x10, waiting for transfers between devices, to_owners(): lax.ppermute(lax.dynamic_slice_in_dim(share, start, blocks, 0), ('dp', 's...  50.4 us
    pallas_call x1, Pallas kernels, dense_backward(): pl.pallas_call(functools.partial(dense_back_kernel, count=count, rows=row...  48 us
    pallas_call x2, Pallas kernels, attention_forward(): pl.pallas_call(functools.partial(forward_kernel, blocks=blocks), grid=(bl...  45 us
    ppermute x20, starting transfers between devices, partner(): return lax.ppermute(array, axis, pairs)  44.2 us
  transfers between devices with their start and end apart: 53, of which 25 were waited for; matrix products, arithmetic and copies ran while one was open for 15% of the time, Pallas kernels for 16%

profile of v3, /device:TPU:16, one launch (start us, length us, event | category | flops | bytes accessed | tf_op | source)
XLA Modules:
  0.0 1092.7 jit_solution(14962499801474962449)
XLA Ops:
  33.3 30.3 %all-to-all-done = bf16[16,16,1536]{2,1,0:T(8,128)(2,1)} async-done(((bf16[16,16,1536]{2,1,0:T(8,128)(2,1)}), bf16[16,16,1536]{2,1,0:T(8,128)(2,1)}, u32[]{:S(2)}, u32[]{:S(2)}) %all-to-all-start) | async-done | bytes 786464 | tf_op jit(solution)/shard_map/all_to_all | solution.py:1004
  75.1 132.7 %all-to-all-done.1 = bf16[16,64,1536]{2,1,0:T(8,128)(2,1)S(1)} async-done(((bf16[16,64,1536]{2,1,0:T(8,128)(2,1)}), bf16[16,64,1536]{2,1,0:T(8,128)(2,1)S(1)}, u32[]{:S(2)}, u32[]{:S(2)}) %all-to-all-start.1) | async-done | bytes 3145760 | tf_op jit(solution)/shard_map/all_to_all | solution.py:1006
  238.5 8.6 convolution_convert_fusion.1
  250.4 22.6 %shard_map.128 = (bf16[2048,384]{1,0:T(8,128)(2,1)}, f32[2,2048]{1,0:T(2,128)S(1)}) custom-call(f32[2,8,4096]{2,1,0:T(8,128)S(1)} %get-tuple-element.175.table_ref, bf16[128,2048]{1,0:T(8,128)(2,1)S(1)} %get-tuple-element.148.q_ref, bf16[128,2048]{1,0:T(8,128)(2,1)S(1)} %get-tuple-element.147.k_ref, bf16[384,2048]{1,0:T(8,128)(2,1)S(1)} %get-tuple-element.145.v_ref), custom_call_target="tpu_custom_call" | custom-call | flops 536870912 | bytes 524288 | tf_op jit(solution)/shard_map/pallas_call | solution.py:190
  282.8 22.4 %shard_map.127 = (bf16[2048,384]{1,0:T(8,128)(2,1)}, f32[2,2048]{1,0:T(2,128)S(1)}) custom-call(f32[2,8,4096]{2,1,0:T(8,128)S(1)} %copy-done.14, bf16[128,2048]{1,0:T(8,128)(2,1)S(1)} %copy-done.7, bf16[128,2048]{1,0:T(8,128)(2,1)S(1)} %get-tuple-element.149.k_ref, bf16[384,2048]{1,0:T(8,128)(2,1)S(1)} %copy-done.3), custom_call_target="tpu_custom_call" | custom-call | flops 536870912 | bytes 524288 | tf_op jit(solution)/shard_map/pallas_call | solution.py:190
  305.2 46.9 %all-to-all-done.3 = bf16[16,128,384]{2,1,0:T(8,128)(2,1)} async-done(((bf16[16,128,384]{2,1,0:T(8,128)(2,1)}), bf16[16,128,384]{2,1,0:T(8,128)(2,1)}, u32[]{:S(2)}, u32[]{:S(2)}) %all-to-all-start.3) | async-done | bytes 1572896 | tf_op jit(solution)/shard_map/all_to_all | solution.py:905
  360.5 45.5 %all-to-all-done.2 = bf16[16,128,384]{2,1,0:T(8,128)(2,1)S(1)} async-done(((bf16[16,128,384]{2,1,0:T(8,128)(2,1)}), bf16[16,128,384]{2,1,0:T(8,128)(2,1)S(1)}, u32[]{:S(2)}, u32[]{:S(2)}) %all-to-all-start.2) | async-done | bytes 1572896 | tf_op jit(solution)/shard_map/all_to_all | solution.py:905
  421.2 42.8 %shard_map.130 = (bf16[8,128,1536]{2,1,0:T(8,128)(2,1)}, f32[8,128,1536]{2,1,0:T(8,128)}, bf16[8,128,1536]{2,1,0:T(8,128)(2,1)}, bf16[8,128,3072]{2,1,0:T(8,128)...) custom-call(s32[1]{0:T(128)} %bitcast.core_ref, bf16[8,128,1536]{2,1,0:T(8,128)(2,1)} %inputs_ref.1, ...), custom_call_target="tpu_custom_call" | custom-call | flops 1509949440 | bytes 4030464 | tf_op jit(solution)/shard_map/pallas_call | solution.py:548
  475.5 43.5 %shard_map.131 = (bf16[8,256,1536]{2,1,0:T(8,128)(2,1)}, bf16[8,256,1536]{2,1,0:T(8,128)(2,1)}, bf16[288,2,16,1536]{3,2,1,0:T(8,128)(2,1)}, f32[8,1,1536]{2,1,0:T(1,128)}, f32[8,1536]{1,0:T(8,128)}) custom-call(f32[8,128,1536]{2,1,0:T(8,128)} %get-tuple-element.71.after_ref, bf16[8,256,1536]{2,1,0:T(8,128)(2,1)} %skip_ref.1, ...), custom_call_target="tpu_custom_call" | custom-call | flops 1811939328 | bytes 2555904 | tf_op jit(solution)/shard_map/pallas_call | solution.py:657
  534.6 48.0 %shard_map.132 = (f32[8,256,1536]{2,1,0:T(8,128)}, f32[8,128,1536]{2,1,0:T(8,128)}, bf16[8,128,1536]{2,1,0:T(8,128)(2,1)}, bf16[8,128,3072]{2,1,0:T(8,128)(2,1)}...) custom-call(s32[1]{0:T(128)} %bitcast.core_ref, ...), custom_call_target="tpu_custom_call" | custom-call | flops 1509949440 | bytes 5406720 | tf_op jit(solution)/shard_map/pallas_call | solution.py:810
  592.4 14.2 %shard_map.133.refs_0_ = bf16[288,2,16,1536]{3,2,1,0:T(8,128)(2,1)} custom-call(bf16[8,128,3072]{2,1,0:T(8,128)(2,1)} %get-tuple-element.81.left_ref, bf16[8,128,1536]{2,1,0:T(8,128)(2,1)S(1)} %copy-done.11, bf16[288,2,16,1536]{3,2,1,0:T(8,128)(2,1)} %get-tuple-element.83.refs_0_), custom_call_target="tpu_custom_call", output_to_operand_aliasing={{}: (2, {})} | custom-call | flops 603979776 | bytes 1179648 | tf_op jit(solution)/shard_map/pallas_call | solution.py:848
  606.5 15.8 %shard_map.134.refs_0_ = bf16[288,2,16,1536]{3,2,1,0:T(8,128)(2,1)} custom-call(bf16[8,128,1536]{2,1,0:T(8,128)(2,1)S(1)} %copy-done.10, bf16[8,128,3072]{2,1,0:T(8,128)(2,1)} %get-tuple-element.80.right_ref, bf16[288,2,16,1536]{3,2,1,0:T(8,128)(2,1)} %shard_map.133.refs_0_), custom_call_target="tpu_custom_call", output_to_operand_aliasing={{}: (2, {})} | custom-call | flops 603979776 | bytes 1179648 | tf_op jit(solution)/shard_map/pallas_call | solution.py:848
  622.4 8.9 shard_map.135
  643.3 40.7 %shard_map.136 = (bf16[2048,128]{1,0:T(8,128)(2,1)}, bf16[2048,128]{1,0:T(8,128)(2,1)}, bf16[2048,384]{1,0:T(8,128)(2,1)}, f32[2,4096]{1,0:T(2,128)}) custom-call(f32[2,8,4096]{2,1,0:T(8,128)} %get-tuple-element.176.table_ref, bf16[128,2048]{1,0:T(8,128)(2,1)} %get-tuple-element.150.q_ref, bf16[128,2048]{1,0:T(8,128)(2,1)} %copy-done.6, ...), custom_call_target="tpu_custom_call" | custom-call | flops 1342177280 | bytes 1048576 | tf_op jit(solution)/shard_map/pallas_call | solution.py:312
  685.2 40.9 %shard_map.137 = (bf16[2048,128]{1,0:T(8,128)(2,1)}, bf16[2048,128]{1,0:T(8,128)(2,1)}, bf16[2048,384]{1,0:T(8,128)(2,1)}, f32[2,4096]{1,0:T(2,128)}) custom-call(f32[2,8,4096]{2,1,0:T(8,128)} %copy-done.13, bf16[128,2048]{1,0:T(8,128)(2,1)} %copy-done.5, bf16[128,2048]{1,0:T(8,128)(2,1)} %copy-done.4, bf16[384,2048]{1,0:T(8,128)(2,1)} %copy-done.2, ...), custom_call_target="tpu_custom_call" | custom-call | flops 1342177280 | bytes 1048576 | tf_op jit(solution)/shard_map/pallas_call | solution.py:312
  730.1 9.2 convolution_convert_fusion
  743.0 10.7 fusion.70
  805.6 34.1 %collective-permute-done.16 = bf16[2,2,2,80,512]{4,3,0,1,2:T(8,128)(2,1)} collective-permute-done((bf16[2,2,2,80,512]{4,3,0,1,2:T(8,128)(2,1)}, bf16[2,2,2,80,512]{4,3,0,1,2:T(8,128)(2,1)}, u32[]{:S(2)}, u32[]{:S(2)}) %collective-permute-start.16) | collective-permute-done | bytes 655392 | tf_op jit(solution)/shard_map/ppermute | solution.py:1044
  851.0 14.0 %collective-permute-done.15 = bf16[2,2,80,512]{3,2,0,1:T(8,128)(2,1)S(1)} collective-permute-done((bf16[2,2,80,512]{3,2,0,1:T(8,128)(2,1)S(1)}, bf16[2,2,80,512]{3,2,0,1:T(8,128)(2,1)S(1)}, u32[]{:S(2)}, u32[]{:S(2)}) %collective-permute-start.15) | collective-permute-done | bytes 327712 | tf_op jit(solution)/shard_map/ppermute | solution.py:1044
  865.8 14.7 %collective-permute-done.19 = bf16[2,2,80,512]{3,2,1,0:T(8,128)(2,1)S(1)} collective-permute-done((bf16[2,2,80,512]{3,2,1,0:T(8,128)(2,1)S(1)}, bf16[2,2,80,512]{3,2,1,0:T(8,128)(2,1)S(1)}, u32[]{:S(2)}, u32[]{:S(2)}) %collective-permute-start.19) | collective-permute-done | bytes 327712 | tf_op jit(solution)/shard_map/ppermute | solution.py:1044
  891.9 11.2 %collective-permute-done.22 = bf16[2,80,512]{2,1,0:T(8,128)(2,1)S(1)} collective-permute-done((bf16[2,80,512]{2,1,0:T(8,128)(2,1)S(1)}, bf16[2,80,512]{2,1,0:T(8,128)(2,1)S(1)}, u32[]{:S(2)}, u32[]{:S(2)}) %collective-permute-start.22) | collective-permute-done | bytes 163872 | tf_op jit(solution)/shard_map/ppermute | solution.py:1044
  955.6 11.0 %collective-permute-start.34 = (f32[23040]{0:T(1024)S(1)}, f32[23040]{0:T(1024)S(1)}, u32[]{:S(2)}, u32[]{:S(2)}) collective-permute-start(f32[23040]{0:T(1024)S(1)} %constant_dynamic-update-slice_fusion.7), channel_id=1, source_target_pairs={{0,16},{16,0},{1,17},{17,1},{2,18},{18,2},{3,19},{19,3},{4,20},{20... | collective-permute-start | bytes 276488 | tf_op jit(solution)/shard_map/ppermute | solution.py:1044
  1009.8 50.4 %collective-permute-done.39 = bf16[18,16,1536]{2,1,0:T(8,128)(2,1)S(1)} collective-permute-done((bf16[18,16,1536]{2,1,0:T(8,128)(2,1)S(1)}, bf16[18,16,1536]{2,1,0:T(8,128)(2,1)S(1)}, u32[]{:S(2)}, u32[]{:S(2)}) %collective-permute-start.39) | collective-permute-done | bytes 884768 | tf_op jit(solution)/shard_map/ppermute | solution.py:1162
  1076.6 9.0 fusion.62
  (420 shorter events, 348.8 us)
Async XLA Ops:
  7.2 221.5 %all-gather.3.cloned.1.call-start = ((), (), s32[]{:S(2)}) async-start(), calls=%async_computation.8 | async-start | bytes 18653184 | tf_op jit(solution)/shard_map/all_gather | solution.py:1023
  26.4 37.2 %all-to-all-start = ((bf16[16,16,1536]{2,1,0:T(8,128)(2,1)}), bf16[16,16,1536]{2,1,0:T(8,128)(2,1)}, u32[]{:S(2)}, u32[]{:S(2)}) async-start(bf16[16,16,1536]{2,1,0:T(8,128)(2,1)} %broadcast_in_dim.152), calls=%async_computation | async-start | bytes 1572864 | tf_op jit(solution)/shard_map/all_to_all | solution.py:1004
  33.2 31.1 %collective-permute-start.3 = (bf16[8,64,1536]{2,1,0:T(8,128)(2,1)}, bf16[8,64,1536]{2,1,0:T(8,128)(2,1)}, u32[]{:S(2)}, u32[]{:S(2)}) collective-permute-start(bf16[8,64,1536]{2,1,0:T(8,128)(2,1)} %constant_dynamic-slice_fusion.7), channel_id=1, source_target_pairs={{0,16},{16,0},{1,17},{17,1},{2,18},{18,2},{3,19},{19,3},{4,20},{20... | collective-permute-start | bytes 4718600 | tf_op jit(solution)/shard_map/ppermute | solution.py:892
  68.3 139.4 %all-to-all-start.1 = ((bf16[16,64,1536]{2,1,0:T(8,128)(2,1)}), bf16[16,64,1536]{2,1,0:T(8,128)(2,1)S(1)}, u32[]{:S(2)}, u32[]{:S(2)}) async-start(bf16[16,64,1536]{2,1,0:T(8,128)(2,1)} %pad_maximum_fusion.5), calls=%async_computation.1 | async-start | bytes 6291456 | tf_op jit(solution)/shard_map/all_to_all | solution.py:1006
  74.3 334.3 %all-gather.5.cloned.1.call-start = ((), (), s32[]{:S(2)}) async-start(), calls=%async_computation.9 | async-start | bytes 18653184 | tf_op jit(solution)/shard_map/all_gather | solution.py:1025
  273.6 78.5 %all-to-all-start.3 = ((bf16[16,128,384]{2,1,0:T(8,128)(2,1)}), bf16[16,128,384]{2,1,0:T(8,128)(2,1)}, u32[]{:S(2)}, u32[]{:S(2)}) async-start(bf16[16,128,384]{2,1,0:T(8,128)(2,1)} %bitcast.11), calls=%async_computation.3 | async-start | bytes 3145728 | tf_op jit(solution)/shard_map/all_to_all | solution.py:905
  352.1 53.9 %all-to-all-start.2 = ((bf16[16,128,384]{2,1,0:T(8,128)(2,1)}), bf16[16,128,384]{2,1,0:T(8,128)(2,1)S(1)}, u32[]{:S(2)}, u32[]{:S(2)}) async-start(bf16[16,128,384]{2,1,0:T(8,128)(2,1)} %bitcast.10), calls=%async_computation.2 | async-start | bytes 3145728 | tf_op jit(solution)/shard_map/all_to_all | solution.py:905
  360.5 59.6 %collective-permute-start.6 = (bf16[8,1,128,384]{3,2,0,1:T(8,128)(2,1)}, bf16[8,1,128,384]{3,2,0,1:T(8,128)(2,1)S(1)}, u32[]{:S(2)}, u32[]{:S(2)}) collective-permute-start(bf16[8,1,128,384]{3,2,0,1:T(8,128)(2,1)} %get-tuple-element.164), channel_id=1, source_target_pairs={{0,16},{16,0},{1,17},{17,1},{2,18},{18,2},{3,19},{19,3},{4,20},{20... | collective-permute-start | bytes 2359304 | tf_op jit(solution)/shard_map/ppermute | solution.py:892
  587.9 43.4 %all-to-all-start.4 = ((bf16[16,128,384]{2,1,0:T(8,128)(2,1)}), bf16[16,128,384]{2,1,0:T(8,128)(2,1)}, u32[]{:S(2)}, u32[]{:S(2)}) async-start(bf16[16,128,384]{2,1,0:T(8,128)(2,1)} %maximum_bitcast_fusion), calls=%async_computation.4 | async-start | bytes 3145728 | tf_op jit(solution)/shard_map/all_to_all | solution.py:905
  592.3 396.9 %reduce-scatter.2.cloned.1.call-start = ((), (), s32[]{:S(2)}) async-start(), calls=%async_computation.10 | async-start | bytes 29196288 | tf_op jit(solution)/shard_map/reduce_scatter | solution.py:1312
  636.2 47.8 %all-to-all-start.5 = ((bf16[16,128,384]{2,1,0:T(8,128)(2,1)}), bf16[16,128,384]{2,1,0:T(8,128)(2,1)S(1)}, u32[]{:S(2)}, u32[]{:S(2)}) async-start(bf16[16,128,384]{2,1,0:T(8,128)(2,1)} %maximum_bitcast_fusion.1), calls=%async_computation.5 | async-start | bytes 3145728 | tf_op jit(solution)/shard_map/all_to_all | solution.py:905
  773.8 107.5 %all-to-all-start.6 = ((bf16[16,64,1536]{2,1,0:T(8,128)(2,1)}), bf16[16,64,1536]{2,1,0:T(8,128)(2,1)}, u32[]{:S(2)}, u32[]{:S(2)}) async-start(bf16[16,64,1536]{2,1,0:T(8,128)(2,1)} %fusion.19), calls=%async_computation.6 | async-start | bytes 6291456 | tf_op jit(solution)/shard_map/all_to_all | solution.py:905
  793.3 46.4 %collective-permute-start.16 = (bf16[2,2,2,80,512]{4,3,0,1,2:T(8,128)(2,1)}, bf16[2,2,2,80,512]{4,3,0,1,2:T(8,128)(2,1)}, u32[]{:S(2)}, u32[]{:S(2)}) collective-permute-start(bf16[2,2,2,80,512]{4,3,0,1,2:T(8,128)(2,1)} %bitcast.151), channel_id=1, source_target_pairs={{0,2},{1,3},{2,0},{3,1},{4,6},{5,7},{6,4},{7,5},{8,10},{9,11},{10,... | collective-permute-start | bytes 1966088 | tf_op jit(solution)/shard_map/ppermute | solution.py:1044
  799.6 43.5 %collective-permute-start.14 = (bf16[2,2,2,80,512]{4,3,0,1,2:T(8,128)(2,1)}, bf16[2,2,2,80,512]{4,3,0,1,2:T(8,128)(2,1)}, u32[]{:S(2)}, u32[]{:S(2)}) collective-permute-start(bf16[2,2,2,80,512]{4,3,0,1,2:T(8,128)(2,1)} %bitcast.152), channel_id=1, source_target_pairs={{0,1},{1,0},{2,3},{3,2},{4,5},{5,4},{6,7},{7,6},{8,9},{9,8},{10,11... | collective-permute-start | bytes 1966088 | tf_op jit(solution)/shard_map/ppermute | solution.py:1044
  804.1 44.4 %collective-permute-start.18 = (bf16[2,2,2,80,512]{4,3,2,1,0:T(8,128)(2,1)S(1)}, bf16[2,2,2,80,512]{4,3,2,1,0:T(8,128)(2,1)S(1)}, u32[]{:S(2)}, u32[]{:S(2)}) collective-permute-start(bf16[2,2,2,80,512]{4,3,2,1,0:T(8,128)(2,1)S(1)} %dynamic-slice_bitcast_fusion.4), channel_id=1, source_target_pairs={{0,4},{1,5},{2,6},{3,7},{4,0},{5,1},{6,2},{7,3},{8,12},{9,13},{10,... | collective-permute-start | bytes 1966088 | tf_op jit(solution)/shard_map/ppermute | solution.py:1044
  848.7 31.8 %collective-permute-start.19 = (bf16[2,2,80,512]{3,2,1,0:T(8,128)(2,1)S(1)}, bf16[2,2,80,512]{3,2,1,0:T(8,128)(2,1)S(1)}, u32[]{:S(2)}, u32[]{:S(2)}) collective-permute-start(bf16[2,2,80,512]{3,2,1,0:T(8,128)(2,1)S(1)} %dynamic-slice_bitcast_fusion.5), channel_id=1, source_target_pairs={{0,8},{1,9},{2,10},{3,11},{4,12},{5,13},{6,14},{7,15},{8,0},{9,1},... | collective-permute-start | bytes 983048 | tf_op jit(solution)/shard_map/ppermute | solution.py:1044
  922.9 27.3 %collective-permute-start.21 = (bf16[8,64,1536]{2,1,0:T(8,128)(2,1)}, bf16[8,64,1536]{2,1,0:T(8,128)(2,1)}, u32[]{:S(2)}, u32[]{:S(2)}) collective-permute-start(bf16[8,64,1536]{2,1,0:T(8,128)(2,1)} %constant_dynamic-slice_fusion), channel_id=1, source_target_pairs={{0,16},{16,0},{1,17},{17,1},{2,18},{18,2},{3,19},{19,3},{4,20},{20... | collective-permute-start | bytes 4718600 | tf_op jit(solution)/shard_map/ppermute | solution.py:892
  932.9 33.8 %collective-permute-start.31 = (bf16[5,16,1536]{2,1,0:T(8,128)(2,1)}, bf16[5,16,1536]{2,1,0:T(8,128)(2,1)S(1)}, u32[]{:S(2)}, u32[]{:S(2)}) collective-permute-start(bf16[5,16,1536]{2,1,0:T(8,128)(2,1)} %bitcast.59), channel_id=1, source_target_pairs={{3,0},{7,1},{12,2},{16,3},{21,4},{26,5},{30,6}} | collective-permute-start | bytes 737288 | tf_op jit(solution)/shard_map/ppermute | solution.py:1162
  933.6 34.9 %collective-permute-start.32 = (bf16[5,16,1536]{2,1,0:T(8,128)(2,1)}, bf16[5,16,1536]{2,1,0:T(8,128)(2,1)S(1)}, u32[]{:S(2)}, u32[]{:S(2)}) collective-permute-start(bf16[5,16,1536]{2,1,0:T(8,128)(2,1)} %bitcast.59), channel_id=1, source_target_pairs={{4,0},{8,1},{13,2},{17,3},{22,4},{27,5},{31,6}} | collective-permute-start | bytes 737288 | tf_op jit(solution)/shard_map/ppermute | solution.py:1162
  945.7 28.5 %collective-permute-start.33 = (bf16[5,16,1536]{2,1,0:T(8,128)(2,1)}, bf16[5,16,1536]{2,1,0:T(8,128)(2,1)S(1)}, u32[]{:S(2)}, u32[]{:S(2)}) collective-permute-start(bf16[5,16,1536]{2,1,0:T(8,128)(2,1)} %bitcast.59), channel_id=1, source_target_pairs={{9,1},{18,3},{23,4}} | collective-permute-start | bytes 737288 | tf_op jit(solution)/shard_map/ppermute | solution.py:1162
  997.1 65.6 %collective-permute-start.40 = (bf16[18,16,1536]{2,1,0:T(8,128)(2,1)S(1)}, bf16[18,16,1536]{2,1,0:T(8,128)(2,1)S(1)}, u32[]{:S(2)}, u32[]{:S(2)}) collective-permute-start(bf16[18,16,1536]{2,1,0:T(8,128)(2,1)S(1)} %broadcast_select_fusion.4), channel_id=1, source_target_pairs={{1,11},{2,12},{3,13},{4,14},{5,15},{7,16},{8,17},{9,18},{11,19},{1... | collective-permute-start | bytes 2654216 | tf_op jit(solution)/shard_map/ppermute | solution.py:1162
  1000.1 60.1 %collective-permute-start.39 = (bf16[18,16,1536]{2,1,0:T(8,128)(2,1)S(1)}, bf16[18,16,1536]{2,1,0:T(8,128)(2,1)S(1)}, u32[]{:S(2)}, u32[]{:S(2)}) collective-permute-start(bf16[18,16,1536]{2,1,0:T(8,128)(2,1)S(1)} %get-tuple-element.174), channel_id=1, source_target_pairs={{0,11},{1,12},{2,13},{3,14},{4,15},{6,16},{7,17},{8,18},{10,19},{1... | collective-permute-start | bytes 2654216 | tf_op jit(solution)/shard_map/ppermute | solution.py:1162
  1007.9 57.4 %collective-permute-start.41 = (bf16[18,16,1536]{2,1,0:T(8,128)(2,1)S(1)}, bf16[18,16,1536]{2,1,0:T(8,128)(2,1)S(1)}, u32[]{:S(2)}, u32[]{:S(2)}) collective-permute-start(bf16[18,16,1536]{2,1,0:T(8,128)(2,1)S(1)} %get-tuple-element.173), channel_id=1, source_target_pairs={{6,15},{10,18},{15,22},{19,25},{21,7},{25,9},{26,11},{28,28}} | collective-permute-start | bytes 2654216 | tf_op jit(solution)/shard_map/ppermute | solution.py:1162
  1008.8 59.0 %collective-permute-start.42 = (bf16[18,16,1536]{2,1,0:T(8,128)(2,1)S(1)}, bf16[18,16,1536]{2,1,0:T(8,128)(2,1)S(1)}, u32[]{:S(2)}, u32[]{:S(2)}) collective-permute-start(bf16[18,16,1536]{2,1,0:T(8,128)(2,1)S(1)} %get-tuple-element.172), channel_id=1, source_target_pairs={{26,27}} | collective-permute-start | bytes 2654216 | tf_op jit(solution)/shard_map/ppermute | solution.py:1162
  (102 other events, 1597.7 us)
Sparse Core Ops, SparseCore 0:
  24.1 189.5 all-gather.2
  229.7 166.5 all-gather.4
  631.5 326.4 reduce-scatter.1

commit v4 on v2

--- a/solution.py
+++ b/solution.py
@@ -1322,17 +1322,23 @@
     late = jnp.concatenate([grad_pos.reshape(-1), grad_gain_one, grad_bias_one])
     summed = jnp.concatenate([late, middle])
     for axis, bit in axis_bits("dp") + axis_bits("seq"):
-        summed = summed + partner(summed, axis, bit)
+        other = partner(summed, axis, bit)
+        if first_sums.steps > 0:
+            first_sums.send()
+            first_sums.move()
+            first_sums.add()
+            first_sums.states, other = lax.optimization_barrier((first_sums.states, other))
+        summed = summed + other
     late, middle = (summed[: late.shape[0]], summed[late.shape[0] :])
     special_grads = jnp.concatenate(
         [late[: F * H], middle[:FF], late[F * H :], middle[FF:]]
     )
-    share = dense
+    buffer = jnp.zeros((ROWS // devices + TAIL // D + 2 * MARGIN, D), bf16)
+    buffer = to_owners(buffer, first_sums.finish(), QKV_PARTS)
+    share, buffer = lax.optimization_barrier((dense, buffer))
     if even:
         share = halves_apart(share, lax.axis_index(("dp", "seq")) * share.shape[0], 2, UNIT)
-    buffer = jnp.zeros((ROWS // devices + TAIL // D + 2 * MARGIN, D), bf16)
     buffer = to_owners(buffer, share, PARTS)
-    buffer = to_owners(buffer, first_sums.finish(), QKV_PARTS)
     reduced = own_entries(buffer, special_grads)
     shard_len = params.shape[0]
     position = lax.axis_index(("dp", "seq")) * shard_len + jnp.arange(shard_len)

time: 1080 us -> 1090 us (level)
  other arithmetic: 78.5 us -> 96.9 us
  waiting for transfers between devices: 400 us -> 382 us
    dynamic_update_slice x10, other arithmetic: 4.69 us -> 19.8 us  [to_owners(): buffer = lax.dynamic_update_slice_in_dim(buffer, there + moved, place, 0)]
    unnamed x169 -> x159, local copies, waits for them, and re-layouts: 25.2 us -> 25.1 us
  transfers between devices with their start and end apart: 53 -> 53, of which waited for: 25 -> 23; matrix products, arithmetic and copies ran while one was open for 16% -> 18% of each run, Pallas kernels for 16% -> 16%
where the time goes in v4:
time: 1090 us; the launch traced here: 1080 us
  waiting for transfers between devices  382 us (35%)
  Pallas kernels  307 us (28%)
  starting transfers between devices  133 us (12%)
  local copies, waits for them, and re-layouts  103 us (9%)
  other arithmetic  96.9 us (9%)
  matrix products  44.3 us (4%)
  between operations  15.6 us (1%)
    all_to_all x1, waiting for transfers between devices, gather_weights(): ready = lax.all_to_all(sent, 'seq', split_axis=0, concat_axis=0, tiled=True)  124 us
    all_to_all x5, waiting for transfers between devices, exchange(): return lax.all_to_all(array, 'seq', split_axis=0, concat_axis=0, tiled=True)  82 us
    pallas_call x2, Pallas kernels, attention_backward(): pl.pallas_call(functools.partial(backward_kernel, blocks=blocks), grid=(b...  81.6 us
    ppermute x20, waiting for transfers between devices, partner(): return lax.ppermute(array, axis, pairs)  74.6 us
    ppermute x10, waiting for transfers between devices, to_owners(): lax.ppermute(lax.dynamic_slice_in_dim(share, start, blocks, 0), ('dp', 's...  48.9 us
    pallas_call x1, Pallas kernels, dense_backward(): pl.pallas_call(functools.partial(dense_back_kernel, count=count, rows=row...  47.8 us
    ppermute x20, starting transfers between devices, partner(): return lax.ppermute(array, axis, pairs)  46.8 us
    pallas_call x2, Pallas kernels, attention_forward(): pl.pallas_call(functools.partial(forward_kernel, blocks=blocks), grid=(bl...  44.8 us
  transfers between devices with their start and end apart: 53, of which 23 were waited for; matrix products, arithmetic and copies ran while one was open for 18% of the time, Pallas kernels for 16%

profile of v4, /device:TPU:16, one launch (start us, length us, event | category | flops | bytes accessed | tf_op | source)
XLA Modules:
  0.0 1081.4 jit_solution(9333418955447407092)
XLA Ops:
  33.2 30.3 %all-to-all-done = bf16[16,16,1536]{2,1,0:T(8,128)(2,1)} async-done(((bf16[16,16,1536]{2,1,0:T(8,128)(2,1)}), bf16[16,16,1536]{2,1,0:T(8,128)(2,1)}, u32[]{:S(2)}, u32[]{:S(2)}) %all-to-all-start) | async-done | bytes 786464 | tf_op jit(solution)/shard_map/all_to_all | solution.py:958
  83.5 124.2 %all-to-all-done.1 = bf16[16,64,1536]{2,1,0:T(8,128)(2,1)S(1)} async-done(((bf16[16,64,1536]{2,1,0:T(8,128)(2,1)}), bf16[16,64,1536]{2,1,0:T(8,128)(2,1)S(1)}, u32[]{:S(2)}, u32[]{:S(2)}) %all-to-all-start.1) | async-done | bytes 3145760 | tf_op jit(solution)/shard_map/all_to_all | solution.py:960
  247.4 8.9 convolution_convert_fusion.1
  259.0 22.4 %shard_map.127 = (bf16[2048,384]{1,0:T(8,128)(2,1)}, f32[2,2048]{1,0:T(2,128)S(1)}) custom-call(f32[2,8,4096]{2,1,0:T(8,128)S(1)} %get-tuple-element.191.table_ref, bf16[128,2048]{1,0:T(8,128)(2,1)S(1)} %get-tuple-element.164.q_ref, bf16[128,2048]{1,0:T(8,128)(2,1)S(1)} %get-tuple-element.163.k_ref, bf16[384,2048]{1,0:T(8,128)(2,1)S(1)} %get-tuple-element.161.v_ref), custom_call_target="tpu_custom_call" | custom-call | flops 536870912 | bytes 524288 | tf_op jit(solution)/shard_map/pallas_call | solution.py:190
  282.0 11.2 %all-to-all-start.3 = ((bf16[16,128,384]{2,1,0:T(8,128)(2,1)}), bf16[16,128,384]{2,1,0:T(8,128)(2,1)}, u32[]{:S(2)}, u32[]{:S(2)}) async-start(bf16[16,128,384]{2,1,0:T(8,128)(2,1)} %bitcast.10), calls=%async_computation.3 | async-start | bytes 3145728 | tf_op jit(solution)/shard_map/all_to_all | solution.py:865
  294.7 22.4 %shard_map.126 = (bf16[2048,384]{1,0:T(8,128)(2,1)}, f32[2,2048]{1,0:T(2,128)S(1)}) custom-call(f32[2,8,4096]{2,1,0:T(8,128)S(1)} %copy-done.11, bf16[128,2048]{1,0:T(8,128)(2,1)S(1)} %copy-done.6, bf16[128,2048]{1,0:T(8,128)(2,1)S(1)} %get-tuple-element.165.k_ref, bf16[384,2048]{1,0:T(8,128)(2,1)S(1)} %copy-done.2), custom_call_target="tpu_custom_call" | custom-call | flops 536870912 | bytes 524288 | tf_op jit(solution)/shard_map/pallas_call | solution.py:190
  317.1 48.5 %all-to-all-done.3 = bf16[16,128,384]{2,1,0:T(8,128)(2,1)} async-done(((bf16[16,128,384]{2,1,0:T(8,128)(2,1)}), bf16[16,128,384]{2,1,0:T(8,128)(2,1)}, u32[]{:S(2)}, u32[]{:S(2)}) %all-to-all-start.3) | async-done | bytes 1572896 | tf_op jit(solution)/shard_map/all_to_all | solution.py:865
  374.4 33.5 %all-to-all-done.2 = bf16[16,128,384]{2,1,0:T(8,128)(2,1)S(1)} async-done(((bf16[16,128,384]{2,1,0:T(8,128)(2,1)}), bf16[16,128,384]{2,1,0:T(8,128)(2,1)S(1)}, u32[]{:S(2)}, u32[]{:S(2)}) %all-to-all-start.2) | async-done | bytes 1572896 | tf_op jit(solution)/shard_map/all_to_all | solution.py:865
  423.2 42.8 %shard_map.129 = (bf16[8,128,1536]{2,1,0:T(8,128)(2,1)}, f32[8,128,1536]{2,1,0:T(8,128)}, bf16[8,128,1536]{2,1,0:T(8,128)(2,1)}, bf16[8,128,3072]{2,1,0:T(8,128)...) custom-call(s32[1]{0:T(128)} %bitcast.core_ref, bf16[8,128,1536]{2,1,0:T(8,128)(2,1)} %inputs_ref.1, ...), custom_call_target="tpu_custom_call" | custom-call | flops 1509949440 | bytes 4030464 | tf_op jit(solution)/shard_map/pallas_call | solution.py:508
  477.4 43.7 %shard_map.130 = (bf16[8,256,1536]{2,1,0:T(8,128)(2,1)}, bf16[8,256,1536]{2,1,0:T(8,128)(2,1)}, bf16[288,2,16,1536]{3,2,1,0:T(8,128)(2,1)}, f32[8,1,1536]{2,1,0:T(1,128)}, f32[8,1536]{1,0:T(8,128)}) custom-call(f32[8,128,1536]{2,1,0:T(8,128)} %get-tuple-element.78.after_ref, bf16[8,256,1536]{2,1,0:T(8,128)(2,1)} %skip_ref.1, ...), custom_call_target="tpu_custom_call" | custom-call | flops 1811939328 | bytes 2555904 | tf_op jit(solution)/shard_map/pallas_call | solution.py:617
  536.7 47.8 %shard_map.131 = (f32[8,256,1536]{2,1,0:T(8,128)}, f32[8,128,1536]{2,1,0:T(8,128)}, bf16[8,128,1536]{2,1,0:T(8,128)(2,1)}, bf16[8,128,3072]{2,1,0:T(8,128)(2,1)}...) custom-call(s32[1]{0:T(128)} %bitcast.core_ref, ...), custom_call_target="tpu_custom_call" | custom-call | flops 1509949440 | bytes 5406720 | tf_op jit(solution)/shard_map/pallas_call | solution.py:770
  594.2 14.2 %shard_map.132.refs_0_ = bf16[288,2,16,1536]{3,2,1,0:T(8,128)(2,1)} custom-call(bf16[8,128,3072]{2,1,0:T(8,128)(2,1)} %get-tuple-element.88.left_ref, bf16[8,128,1536]{2,1,0:T(8,128)(2,1)S(1)} %copy-done.8, bf16[288,2,16,1536]{3,2,1,0:T(8,128)(2,1)} %get-tuple-element.90.refs_0_), custom_call_target="tpu_custom_call", output_to_operand_aliasing={{}: (2, {})} | custom-call | flops 603979776 | bytes 1179648 | tf_op jit(solution)/shard_map/pallas_call | solution.py:808
  608.4 15.8 %shard_map.133.refs_0_ = bf16[288,2,16,1536]{3,2,1,0:T(8,128)(2,1)} custom-call(bf16[8,128,1536]{2,1,0:T(8,128)(2,1)S(1)} %copy-done.7, bf16[8,128,3072]{2,1,0:T(8,128)(2,1)} %get-tuple-element.87.right_ref, bf16[288,2,16,1536]{3,2,1,0:T(8,128)(2,1)} %shard_map.132.refs_0_), custom_call_target="tpu_custom_call", output_to_operand_aliasing={{}: (2, {})} | custom-call | flops 603979776 | bytes 1179648 | tf_op jit(solution)/shard_map/pallas_call | solution.py:808
  624.2 8.9 shard_map.134
  645.4 40.8 %shard_map.135 = (bf16[2048,128]{1,0:T(8,128)(2,1)}, bf16[2048,128]{1,0:T(8,128)(2,1)}, bf16[2048,384]{1,0:T(8,128)(2,1)}, f32[2,4096]{1,0:T(2,128)}) custom-call(f32[2,8,4096]{2,1,0:T(8,128)} %get-tuple-element.192.table_ref, bf16[128,2048]{1,0:T(8,128)(2,1)} %get-tuple-element.166.q_ref, bf16[128,2048]{1,0:T(8,128)(2,1)} %copy-done.5, ...), custom_call_target="tpu_custom_call" | custom-call | flops 1342177280 | bytes 1048576 | tf_op jit(solution)/shard_map/pallas_call | solution.py:312
  687.3 40.8 %shard_map.136 = (bf16[2048,128]{1,0:T(8,128)(2,1)}, bf16[2048,128]{1,0:T(8,128)(2,1)}, bf16[2048,384]{1,0:T(8,128)(2,1)}, f32[2,4096]{1,0:T(2,128)}) custom-call(f32[2,8,4096]{2,1,0:T(8,128)} %copy-done.10, bf16[128,2048]{1,0:T(8,128)(2,1)} %copy-done.4, bf16[128,2048]{1,0:T(8,128)(2,1)} %copy-done.3, bf16[384,2048]{1,0:T(8,128)(2,1)} %copy-done.1, ...), custom_call_target="tpu_custom_call" | custom-call | flops 1342177280 | bytes 1048576 | tf_op jit(solution)/shard_map/pallas_call | solution.py:312
  732.4 9.2 convolution_convert_fusion
  745.3 10.3 fusion.74
  804.2 36.4 %collective-permute-done.16 = bf16[2,2,2,80,512]{4,3,0,1,2:T(8,128)(2,1)} collective-permute-done((bf16[2,2,2,80,512]{4,3,0,1,2:T(8,128)(2,1)}, bf16[2,2,2,80,512]{4,3,0,1,2:T(8,128)(2,1)}, u32[]{:S(2)}, u32[]{:S(2)}) %collective-permute-start.16) | collective-permute-done | bytes 655392 | tf_op jit(solution)/shard_map/ppermute | solution.py:997
  873.4 11.0 %fusion.20 = f32[192,4]{1,0:T(8,128)} fusion(f32[4095,96]{1,0:T(8,128)} %get-tuple-element.196, f32[4095,96]{1,0:T(8,128)} %get-tuple-element.195, f32[2,4096]{1,0:T(2,128)} %get-tuple-element.118, f32[2,4096]{1,0:T(2,128)} %get-tuple-element.117), kind=kOutput, calls=%fused_computation.36 | convolution fusion | flops 38574900 | bytes 3213568 | tf_op jit(solution)/shard_map/dot_general | solution.py:1318
  922.3 9.2 collective-permute-done.27
  936.5 9.1 collective-permute-start.40
  1000.2 48.8 %collective-permute-done.36 = bf16[18,16,1536]{2,1,0:T(8,128)(2,1)S(1)} collective-permute-done((bf16[18,16,1536]{2,1,0:T(8,128)(2,1)S(1)}, bf16[18,16,1536]{2,1,0:T(8,128)(2,1)S(1)}, u32[]{:S(2)}, u32[]{:S(2)}) %collective-permute-start.36) | collective-permute-done | bytes 884768 | tf_op jit(solution)/shard_map/ppermute | solution.py:1115
  1065.6 9.0 fusion.65
  (420 shorter events, 366.7 us)
Async XLA Ops:
  7.2 206.5 %all-gather.3.cloned.1.call-start = ((), (), s32[]{:S(2)}) async-start(), calls=%async_computation.8 | async-start | bytes 18653184 | tf_op jit(solution)/shard_map/all_gather | solution.py:976
  26.3 37.2 %all-to-all-start = ((bf16[16,16,1536]{2,1,0:T(8,128)(2,1)}), bf16[16,16,1536]{2,1,0:T(8,128)(2,1)}, u32[]{:S(2)}, u32[]{:S(2)}) async-start(bf16[16,16,1536]{2,1,0:T(8,128)(2,1)} %broadcast_in_dim.152), calls=%async_computation | async-start | bytes 1572864 | tf_op jit(solution)/shard_map/all_to_all | solution.py:958
  33.2 31.1 %collective-permute-start.3 = (bf16[8,64,1536]{2,1,0:T(8,128)(2,1)}, bf16[8,64,1536]{2,1,0:T(8,128)(2,1)}, u32[]{:S(2)}, u32[]{:S(2)}) collective-permute-start(bf16[8,64,1536]{2,1,0:T(8,128)(2,1)} %constant_dynamic-slice_fusion.9), channel_id=1, source_target_pairs={{0,16},{16,0},{1,17},{17,1},{2,18},{18,2},{3,19},{19,3},{4,20},{20... | collective-permute-start | bytes 4718600 | tf_op jit(solution)/shard_map/ppermute | solution.py:852
  68.3 139.4 %all-to-all-start.1 = ((bf16[16,64,1536]{2,1,0:T(8,128)(2,1)}), bf16[16,64,1536]{2,1,0:T(8,128)(2,1)S(1)}, u32[]{:S(2)}, u32[]{:S(2)}) async-start(bf16[16,64,1536]{2,1,0:T(8,128)(2,1)} %pad_maximum_fusion.6), calls=%async_computation.1 | async-start | bytes 6291456 | tf_op jit(solution)/shard_map/all_to_all | solution.py:960
  74.3 336.3 %all-gather.5.cloned.1.call-start = ((), (), s32[]{:S(2)}) async-start(), calls=%async_computation.9 | async-start | bytes 18653184 | tf_op jit(solution)/shard_map/all_gather | solution.py:978
  218.6 23.1 %collective-permute-start.4 = (bf16[16,1,64,1536]{3,2,0,1:T(8,128)(2,1)}, bf16[16,1,64,1536]{3,2,0,1:T(8,128)(2,1)}, u32[]{:S(2)}, u32[]{:S(2)}) collective-permute-start(bf16[16,1,64,1536]{3,2,0,1:T(8,128)(2,1)} %fusion.50), channel_id=1, source_target_pairs={{0,16},{16,0},{1,17},{17,1},{2,18},{18,2},{3,19},{19,3},{4,20},{20... | collective-permute-start | bytes 9437192 | tf_op jit(solution)/shard_map/ppermute | solution.py:852
  282.0 83.6 %all-to-all-start.3 = ((bf16[16,128,384]{2,1,0:T(8,128)(2,1)}), bf16[16,128,384]{2,1,0:T(8,128)(2,1)}, u32[]{:S(2)}, u32[]{:S(2)}) async-start(bf16[16,128,384]{2,1,0:T(8,128)(2,1)} %bitcast.10), calls=%async_computation.3 | async-start | bytes 3145728 | tf_op jit(solution)/shard_map/all_to_all | solution.py:865
  365.6 42.3 %all-to-all-start.2 = ((bf16[16,128,384]{2,1,0:T(8,128)(2,1)}), bf16[16,128,384]{2,1,0:T(8,128)(2,1)S(1)}, u32[]{:S(2)}, u32[]{:S(2)}) async-start(bf16[16,128,384]{2,1,0:T(8,128)(2,1)} %bitcast.9), calls=%async_computation.2 | async-start | bytes 3145728 | tf_op jit(solution)/shard_map/all_to_all | solution.py:865
  374.4 47.6 %collective-permute-start.6 = (bf16[8,1,128,384]{3,2,0,1:T(8,128)(2,1)}, bf16[8,1,128,384]{3,2,0,1:T(8,128)(2,1)S(1)}, u32[]{:S(2)}, u32[]{:S(2)}) collective-permute-start(bf16[8,1,128,384]{3,2,0,1:T(8,128)(2,1)} %get-tuple-element.180), channel_id=1, source_target_pairs={{0,16},{16,0},{1,17},{17,1},{2,18},{18,2},{3,19},{19,3},{4,20},{20... | collective-permute-start | bytes 2359304 | tf_op jit(solution)/shard_map/ppermute | solution.py:852
  589.7 43.4 %all-to-all-start.4 = ((bf16[16,128,384]{2,1,0:T(8,128)(2,1)}), bf16[16,128,384]{2,1,0:T(8,128)(2,1)}, u32[]{:S(2)}, u32[]{:S(2)}) async-start(bf16[16,128,384]{2,1,0:T(8,128)(2,1)} %maximum_bitcast_fusion), calls=%async_computation.4 | async-start | bytes 3145728 | tf_op jit(solution)/shard_map/all_to_all | solution.py:865
  594.1 384.3 %reduce-scatter.2.cloned.1.call-start = ((), (), s32[]{:S(2)}) async-start(), calls=%async_computation.10 | async-start | bytes 29196288 | tf_op jit(solution)/shard_map/reduce_scatter | solution.py:1276
  638.0 48.1 %all-to-all-start.5 = ((bf16[16,128,384]{2,1,0:T(8,128)(2,1)}), bf16[16,128,384]{2,1,0:T(8,128)(2,1)S(1)}, u32[]{:S(2)}, u32[]{:S(2)}) async-start(bf16[16,128,384]{2,1,0:T(8,128)(2,1)} %maximum_bitcast_fusion.1), calls=%async_computation.5 | async-start | bytes 3145728 | tf_op jit(solution)/shard_map/all_to_all | solution.py:865
  745.3 23.7 %collective-permute-start.20 = (bf16[16,64,1536]{2,1,0:T(8,128)(2,1)}, bf16[16,64,1536]{2,1,0:T(8,128)(2,1)}, u32[]{:S(2)}, u32[]{:S(2)}) collective-permute-start(bf16[16,64,1536]{2,1,0:T(8,128)(2,1)} %dynamic-slice_bitcast_fusion.1), channel_id=1, source_target_pairs={{0,16},{16,0},{1,17},{17,1},{2,18},{18,2},{3,19},{19,3},{4,20},{20... | collective-permute-start | bytes 9437192 | tf_op jit(solution)/shard_map/ppermute | solution.py:852
  774.7 90.5 %all-to-all-start.6 = ((bf16[16,64,1536]{2,1,0:T(8,128)(2,1)}), bf16[16,64,1536]{2,1,0:T(8,128)(2,1)}, u32[]{:S(2)}, u32[]{:S(2)}) async-start(bf16[16,64,1536]{2,1,0:T(8,128)(2,1)} %fusion.19), calls=%async_computation.6 | async-start | bytes 6291456 | tf_op jit(solution)/shard_map/all_to_all | solution.py:865
  792.9 47.8 %collective-permute-start.16 = (bf16[2,2,2,80,512]{4,3,0,1,2:T(8,128)(2,1)}, bf16[2,2,2,80,512]{4,3,0,1,2:T(8,128)(2,1)}, u32[]{:S(2)}, u32[]{:S(2)}) collective-permute-start(bf16[2,2,2,80,512]{4,3,0,1,2:T(8,128)(2,1)} %bitcast.148), channel_id=1, source_target_pairs={{0,2},{1,3},{2,0},{3,1},{4,6},{5,7},{6,4},{7,5},{8,10},{9,11},{10,... | collective-permute-start | bytes 1966088 | tf_op jit(solution)/shard_map/ppermute | solution.py:997
  798.0 48.1 %collective-permute-start.14 = (bf16[2,2,2,80,512]{4,3,0,1,2:T(8,128)(2,1)}, bf16[2,2,2,80,512]{4,3,0,1,2:T(8,128)(2,1)}, u32[]{:S(2)}, u32[]{:S(2)}) collective-permute-start(bf16[2,2,2,80,512]{4,3,0,1,2:T(8,128)(2,1)} %bitcast.149), channel_id=1, source_target_pairs={{0,1},{1,0},{2,3},{3,2},{4,5},{5,4},{6,7},{7,6},{8,9},{9,8},{10,11... | collective-permute-start | bytes 1966088 | tf_op jit(solution)/shard_map/ppermute | solution.py:997
  802.5 46.6 %collective-permute-start.18 = (bf16[2,2,2,80,512]{4,3,2,1,0:T(8,128)(2,1)S(1)}, bf16[2,2,2,80,512]{4,3,2,1,0:T(8,128)(2,1)S(1)}, u32[]{:S(2)}, u32[]{:S(2)}) collective-permute-start(bf16[2,2,2,80,512]{4,3,2,1,0:T(8,128)(2,1)S(1)} %dynamic-slice_bitcast_fusion.4), channel_id=1, source_target_pairs={{0,4},{1,5},{2,6},{3,7},{4,0},{5,1},{6,2},{7,3},{8,12},{9,13},{10,... | collective-permute-start | bytes 1966088 | tf_op jit(solution)/shard_map/ppermute | solution.py:997
  867.9 42.1 %collective-permute-start.21 = (bf16[8,64,1536]{2,1,0:T(8,128)(2,1)}, bf16[8,64,1536]{2,1,0:T(8,128)(2,1)}, u32[]{:S(2)}, u32[]{:S(2)}) collective-permute-start(bf16[8,64,1536]{2,1,0:T(8,128)(2,1)} %constant_dynamic-slice_fusion), channel_id=1, source_target_pairs={{0,16},{16,0},{1,17},{17,1},{2,18},{18,2},{3,19},{19,3},{4,20},{20... | collective-permute-start | bytes 4718600 | tf_op jit(solution)/shard_map/ppermute | solution.py:852
  935.8 29.1 %collective-permute-start.30 = (bf16[5,16,1536]{2,1,0:T(8,128)(2,1)S(1)}, bf16[5,16,1536]{2,1,0:T(8,128)(2,1)S(1)}, u32[]{:S(2)}, u32[]{:S(2)}) collective-permute-start(bf16[5,16,1536]{2,1,0:T(8,128)(2,1)S(1)} %bitcast.172), channel_id=1, source_target_pairs={{0,0},{4,1},{9,2},{13,3},{18,4},{23,5},{27,6}} | collective-permute-start | bytes 737288 | tf_op jit(solution)/shard_map/ppermute | solution.py:1115
  968.3 30.2 %collective-permute-start.42 = (f32[23040]{0:T(1024)S(1)}, f32[23040]{0:T(1024)S(1)}, u32[]{:S(2)}, u32[]{:S(2)}) collective-permute-start(f32[23040]{0:T(1024)S(1)} %add.421), channel_id=1, source_target_pairs={{0,1},{1,0},{2,3},{3,2},{4,5},{5,4},{6,7},{7,6},{8,9},{9,8},{10,11... | collective-permute-start | bytes 276488 | tf_op jit(solution)/shard_map/ppermute | solution.py:997
  986.3 65.3 %collective-permute-start.37 = (bf16[18,16,1536]{2,1,0:T(8,128)(2,1)S(1)}, bf16[18,16,1536]{2,1,0:T(8,128)(2,1)S(1)}, u32[]{:S(2)}, u32[]{:S(2)}) collective-permute-start(bf16[18,16,1536]{2,1,0:T(8,128)(2,1)S(1)} %broadcast_select_fusion.4), channel_id=1, source_target_pairs={{1,11},{2,12},{3,13},{4,14},{5,15},{7,16},{8,17},{9,18},{11,19},{1... | collective-permute-start | bytes 2654216 | tf_op jit(solution)/shard_map/ppermute | solution.py:1115
  989.8 59.3 %collective-permute-start.36 = (bf16[18,16,1536]{2,1,0:T(8,128)(2,1)S(1)}, bf16[18,16,1536]{2,1,0:T(8,128)(2,1)S(1)}, u32[]{:S(2)}, u32[]{:S(2)}) collective-permute-start(bf16[18,16,1536]{2,1,0:T(8,128)(2,1)S(1)} %get-tuple-element.190), channel_id=1, source_target_pairs={{0,11},{1,12},{2,13},{3,14},{4,15},{6,16},{7,17},{8,18},{10,19},{1... | collective-permute-start | bytes 2654216 | tf_op jit(solution)/shard_map/ppermute | solution.py:1115
  998.5 55.6 %collective-permute-start.38 = (bf16[18,16,1536]{2,1,0:T(8,128)(2,1)S(1)}, bf16[18,16,1536]{2,1,0:T(8,128)(2,1)S(1)}, u32[]{:S(2)}, u32[]{:S(2)}) collective-permute-start(bf16[18,16,1536]{2,1,0:T(8,128)(2,1)S(1)} %get-tuple-element.189), channel_id=1, source_target_pairs={{6,15},{10,18},{15,22},{19,25},{21,7},{25,9},{26,11},{28,28}} | collective-permute-start | bytes 2654216 | tf_op jit(solution)/shard_map/ppermute | solution.py:1115
  999.3 57.4 %collective-permute-start.39 = (bf16[18,16,1536]{2,1,0:T(8,128)(2,1)S(1)}, bf16[18,16,1536]{2,1,0:T(8,128)(2,1)S(1)}, u32[]{:S(2)}, u32[]{:S(2)}) collective-permute-start(bf16[18,16,1536]{2,1,0:T(8,128)(2,1)S(1)} %get-tuple-element.188), channel_id=1, source_target_pairs={{26,27}} | collective-permute-start | bytes 2654216 | tf_op jit(solution)/shard_map/ppermute | solution.py:1115
  (100 other events, 1416.9 us)
Sparse Core Ops, SparseCore 0:
  24.1 189.5 all-gather.2
  216.6 150.3 all-gather.4
  633.3 320.8 reduce-scatter.1
